TPU v7x, 256 devices: a whole 4x4x8 slice. The times are simulated.
256 devices in a mesh: lat: 16 (over x, y_lo, core), lon: 16 (over y_hi, z).
Axes of the slice: x: 4, y: 4 (y_hi: 2, y_lo: 2; y = y_hi * 2 + y_lo), z: 8, core: 2. Of those that a mesh axis runs over, the one named last changes fastest.
Arguments:
- fields: float32 [78, 32, 2048], P(None, 'lat', 'lon'), may hold values from -6 to 6
- diffusivity: float32 [32, 2048], P('lat', 'lon'), may hold values from 0.1 to 1.5
- w_embed: float32 [78, 256], replicated, may hold values from -0.625 to 0.625
- query_weight: float32 [256, 256], replicated, may hold values from -12 to 12
- key_weight: float32 [256, 256], replicated, may hold values from -1 to 1
- value_weight: float32 [256, 256], replicated, may hold values from -0.375 to 0.375
- out_weight: float32 [256, 256], replicated, may hold values from -0.375 to 0.375
- up_weight: float32 [256, 1024], replicated, may hold values from -0.375 to 0.375
- down_weight: float32 [1024, 256], replicated, may hold values from -0.1875 to 0.1875
Outputs:
- block_out: float32 [32, 2048, 256], P('lat', 'lon')
All inputs are finite; a program needn't handle non-finite values.
Results may differ from a plain program's by a relative error of at most 0.0003.
Values sent between devices are 32-bit elements; how exact they have to be, the bound alone decides.
No kernel may reach another device: no remote copies, remote signals or barrier semaphores. Data moves between devices by JAX's collectives and lax.ppermute only.
A program may use at most 128 MiB of HBM per device.

v0:
```python
import math

import jax
import jax.numpy as jnp
from jax import lax
from jax.sharding import PartitionSpec as P

HEADS = 8


HIGH = lax.Precision.HIGHEST
STEP_SIZE = 0.15
CENTER_LAT = 45.0
SPACING = 0.25
EPSILON = 1e-05


def extended(block, sides, width, periodic):
    for axis, dim in sides:
        count = lax.axis_size(axis)
        forward = [(i, i + 1) for i in range(count - 1)]
        if periodic:
            forward.append((count - 1, 0))
        backward = [(target, source) for source, target in forward]
        low = lax.ppermute(
            lax.slice_in_dim(block, block.shape[dim] - width, None, axis=dim), axis, forward
        )
        high = lax.ppermute(lax.slice_in_dim(block, 0, width, axis=dim), axis, backward)
        block = jnp.concatenate([low, block, high], axis=dim)
    return block


def cosines(first_row, count, total):
    faces = first_row.astype(jnp.float32) + jnp.arange(count + 1, dtype=jnp.float32)
    face_deg = CENTER_LAT + (faces - 0.5 * total) * SPACING
    cell_deg = CENTER_LAT + (faces[:-1] + 0.5 - 0.5 * total) * SPACING
    return (jnp.cos(face_deg * (math.pi / 180.0)), jnp.cos(cell_deg * (math.pi / 180.0)))


def tendency(padded_lat, padded_lon, face_cos, cell_cos):
    fields_lat = padded_lat[:-1]
    kappa_lat = padded_lat[-1]
    north_coef = 0.5 * (kappa_lat[1:] + kappa_lat[:-1]) * face_cos[:, None]
    north_flux = north_coef * (fields_lat[:, 1:] - fields_lat[:, :-1])
    lat_term = north_flux[:, 1:] - north_flux[:, :-1]
    fields_lon = padded_lon[:-1]
    kappa_lon = padded_lon[-1]
    east_coef = 0.5 * (kappa_lon[:, 1:] + kappa_lon[:, :-1])
    east_flux = east_coef * (fields_lon[:, :, 1:] - fields_lon[:, :, :-1])
    lon_term = (east_flux[:, :, 1:] - east_flux[:, :, :-1]) / cell_cos[:, None]
    return (lat_term + lon_term) / cell_cos[:, None]


def layer_norm(values):
    mean = jnp.mean(values, axis=-1, keepdims=True)
    centered = values - mean
    variance = jnp.mean(centered * centered, axis=-1, keepdims=True)
    return centered * lax.rsqrt(variance + EPSILON)


def project(values, weight):
    return jnp.einsum("yxd,de->yxe", values, weight, precision=HIGH)


def on_device(
    fields,
    diffusivity,
    w_embed,
    query_weight,
    key_weight,
    value_weight,
    out_weight,
    up_weight,
    down_weight,
):
    channels, lat_rows, lon_cells = fields.shape
    width = w_embed.shape[1]
    head_dim = width // HEADS
    scale = 1.0 / math.sqrt(head_dim)
    stacked = jnp.concatenate([fields, diffusivity[None]], axis=0)
    padded_lat = extended(stacked, (("lat", 1),), 1, False)
    padded_lon = extended(stacked, (("lon", 2),), 1, True)
    first_row = lax.axis_index("lat") * lat_rows
    total_rows = lat_rows * lax.axis_size("lat")
    face_cos, cell_cos = cosines(first_row, lat_rows, total_rows)
    updated = fields + STEP_SIZE * tendency(padded_lat, padded_lon, face_cos, cell_cos)
    hidden = jnp.einsum("cyx,cd->yxd", updated, w_embed, precision=HIGH)
    normed = layer_norm(hidden)
    queries = project(normed, query_weight)
    key_rows = project(normed, key_weight)
    value_rows = project(normed, value_weight)
    query_heads = queries.reshape(lat_rows, lon_cells, HEADS, head_dim)
    start_max = jnp.full((lat_rows, HEADS, lon_cells), -1e30, jnp.float32)
    key_piece = lax.all_gather(key_rows, "lon", axis=1, tiled=True)
    value_piece = lax.all_gather(value_rows, "lon", axis=1, tiled=True)
    span = key_piece.shape[1]
    key_heads = key_piece.reshape(lat_rows, span, HEADS, head_dim)
    value_heads = value_piece.reshape(lat_rows, span, HEADS, head_dim)
    scores = jnp.einsum("yqhe,ykhe->yhqk", query_heads, key_heads, precision=HIGH) * scale
    new_max = jnp.maximum(start_max, jnp.max(scores, axis=-1))
    weights = jnp.exp(scores - new_max[..., None])
    new_sum = jnp.sum(weights, axis=-1)
    added = jnp.einsum("yhqk,ykhe->yqhe", weights, value_heads, precision=HIGH)
    attended = (added / jnp.transpose(new_sum, (0, 2, 1))[..., None]).reshape(
        lat_rows, lon_cells, width
    )
    mixed = hidden + project(attended, out_weight)
    normed_two = layer_norm(mixed)
    activated = jax.nn.gelu(project(normed_two, up_weight))
    return mixed + project(activated, down_weight)


def solution(mesh):
    placed = (P(None, "lat", "lon"), P("lat", "lon"), P(), P(), P(), P(), P(), P(), P())
    return jax.shard_map(
        on_device, mesh=mesh, in_specs=placed, out_specs=P("lat", "lon", None), check_vma=False
    )
```

profile of v0, /device:TPU:6, one launch (start us, length us, event | category | flops | bytes accessed | tf_op | source)
XLA Modules:
  0.0 269.2 jit_solution(18096452094832794589)
XLA Ops:
  6.5 1.1 fusion.40
  7.6 3.2 %collective-permute-start = (f32[79,1,128]{2,1,0:T(1,128)S(1)}, f32[79,1,128]{2,1,0:T(1,128)S(1)}, u32[]{:S(2)}, u32[]{:S(2)}) collective-permute-start(f32[79,1,128]{2,1,0:T(1,128)S(1)} %get-tuple-element.5), channel_id=1, source_target_pairs={{16,0},{32,16},{48,32},{64,48},{80,64},{96,80},{112,96},{128,112},... | collective-permute-start | bytes 121352 | tf_op jit(solution)/shard_map/ppermute | solution.py:28
  10.8 1.9 collective-permute-start.1
  12.8 1.1 pad_maximum_fusion.8
  13.9 2.0 collective-permute-start.2
  15.9 6.4 %collective-permute-start.3 = (f32[79,2,1]{2,1,0:T(2,128)S(1)}, f32[79,2,1]{2,1,0:T(2,128)S(1)}, u32[]{:S(2)}, u32[]{:S(2)}) collective-permute-start(f32[79,2,1]{2,1,0:T(2,128)S(1)} %get-tuple-element.7), channel_id=1, source_target_pairs={{1,0},{2,1},{3,2},{4,3},{5,4},{6,5},{7,6},{8,7},{9,8},{10,9},{11,1... | collective-permute-start | bytes 1904 | tf_op jit(solution)/shard_map/ppermute | solution.py:28
  22.4 3.0 %collective-permute-done.2 = f32[79,2,1]{2,1,0:T(2,128)S(1)} collective-permute-done((f32[79,2,1]{2,1,0:T(2,128)S(1)}, f32[79,2,1]{2,1,0:T(2,128)S(1)}, u32[]{:S(2)}, u32[]{:S(2)}) %collective-permute-start.2) | collective-permute-done | bytes 664 | tf_op jit(solution)/shard_map/ppermute | solution.py:25
  26.2 1.2 fusion.25
  28.2 1.1 fusion.27
  29.3 1.0 multiply_add_fusion
  30.4 1.4 fusion.47
  32.0 2.1 fusion.16
  34.1 2.1 fusion.20
  36.2 1.6 fusion.18
  37.8 95.0 %all-gather.5.cloned.1.call-done = f32[2,2048,256]{2,1,0:T(8,128)} async-done(((f32[2,128,256]{2,1,0:T(8,128)}), f32[2,2048,256]{2,1,0:T(8,128)}) %all-gather.5.cloned.1.call-update) | async-done | bytes 4194320 | tf_op jit(solution)/shard_map/all_gather | solution.py:94
  132.8 5.4 %copy.18 = f32[2,2048,256]{1,2,0:T(8,128)} copy(f32[2,2048,256]{2,1,0:T(8,128)} %all-gather.5.cloned.1.call-done) | data formatting | bytes 8388608 | tf_op jit(solution)/shard_map/all_gather | solution.py:94
  138.3 16.3 %multiply_reduce_fusion = (f32[2,8,128]{2,1,0:T(8,128)S(1)}, f32[2,8,128,2048]{3,2,1,0:T(8,128)S(1)}) fusion(f32[2,128,8,32]{1,3,2,0:T(8,128)S(1)} %bitcast.47, f32[2,2048,8,32]{1,3,2,0:T(8,128)} %bitcast.45), kind=kOutput, calls=%fused_computation.1 | convolution fusion | flops 1618999296 | bytes 21241856 | tf_op jit(solution)/shard_map/yqhe,ykhe->yhqk/dot_general | solution.py:99
  154.6 5.7 %copy-done.1 = f32[2,8,128,2048]{3,2,1,0:T(8,128)} copy-done((f32[2,8,128,2048]{3,2,1,0:T(8,128)}, f32[2,8,128,2048]{3,2,1,0:T(8,128)S(1)}, u32[]{:S(2)}) %copy-start.1) | copy-done | bytes 16777240
  160.3 3.3 %fusion = f32[2,8,128]{2,1,0:T(8,128)S(1)} fusion(f32[2,8,128,2048]{3,2,1,0:T(8,128)S(1)} %get-tuple-element.12, f32[2,8,128]{2,1,0:T(8,128)S(1)} %broadcast_maximum_fusion), kind=kLoop, calls=%fused_computation.2 | loop fusion | flops 12580864 | bytes 16793600 | tf_op jit(solution)/shard_map/reduce_sum | solution.py:102
  163.6 68.5 %all-gather.3.cloned.1.call-done = f32[2,2048,256]{2,1,0:T(8,128)} async-done(((f32[2,128,256]{2,1,0:T(8,128)}), f32[2,2048,256]{2,1,0:T(8,128)}) %all-gather.3.cloned.1.call-update) | async-done | bytes 4194320 | tf_op jit(solution)/shard_map/all_gather | solution.py:95
  232.0 5.4 %copy.16 = f32[2,2048,256]{1,2,0:T(8,128)} copy(f32[2,2048,256]{2,1,0:T(8,128)} %all-gather.3.cloned.1.call-done) | data formatting | bytes 8388608 | tf_op jit(solution)/shard_map/all_gather | solution.py:95
  237.5 21.0 %fusion.5 = f32[2,128,8,32]{1,3,2,0:T(8,128)S(1)} fusion(f32[2,2048,8,32]{1,3,2,0:T(8,128)} %bitcast.44, f32[2,8,128,2048]{3,2,1,0:T(8,128)} %copy-done.1, f32[2,8,128]{2,1,0:T(8,128)S(1)} %broadcast_maximum_fusion, f32[2,128,8]{1,2,0:T(8,128)S(1)} %bitcast.48), kind=kOutput, calls=%fused_computation.10 | convolution fusion | flops 1619066880 | bytes 21250048 | tf_op jit(solution)/shard_map/yhqk,ykhe->yqhe/dot_general | solution.py:103
  259.3 1.3 fusion.12
  260.7 1.7 convolution_add_fusion.1
  (28 shorter events, 2.9 us)
Async XLA Ops:
  6.5 252.8 %copy-start = (f32[256,1024]{1,0:T(8,128)S(1)}, f32[256,1024]{1,0:T(8,128)}, u32[]{:S(2)}) copy-start(f32[256,1024]{1,0:T(8,128)} %param.16) | copy-start | bytes 3145732
  6.5 126.3 %all-gather.5.cloned.1.call-start = ((), (), s32[]{:S(2)}) async-start(), calls=%async_computation.1 | async-start | bytes 4456448 | tf_op jit(solution)/shard_map/all_gather | solution.py:94
  7.6 19.7 %collective-permute-start = (f32[79,1,128]{2,1,0:T(1,128)S(1)}, f32[79,1,128]{2,1,0:T(1,128)S(1)}, u32[]{:S(2)}, u32[]{:S(2)}) collective-permute-start(f32[79,1,128]{2,1,0:T(1,128)S(1)} %get-tuple-element.5), channel_id=1, source_target_pairs={{16,0},{32,16},{48,32},{64,48},{80,64},{96,80},{112,96},{128,112},... | collective-permute-start | bytes 121352 | tf_op jit(solution)/shard_map/ppermute | solution.py:28
  10.8 16.5 %collective-permute-start.1 = (f32[79,1,128]{2,1,0:T(1,128)S(1)}, f32[79,1,128]{2,1,0:T(1,128)S(1)}, u32[]{:S(2)}, u32[]{:S(2)}) collective-permute-start(f32[79,1,128]{2,1,0:T(1,128)S(1)} %get-tuple-element.6), channel_id=1, source_target_pairs={{0,16},{16,32},{32,48},{48,64},{64,80},{80,96},{96,112},{112,128},... | collective-permute-start | bytes 121352 | tf_op jit(solution)/shard_map/ppermute | solution.py:25
  13.9 11.4 %collective-permute-start.2 = (f32[79,2,1]{2,1,0:T(2,128)S(1)}, f32[79,2,1]{2,1,0:T(2,128)S(1)}, u32[]{:S(2)}, u32[]{:S(2)}) collective-permute-start(f32[79,2,1]{2,1,0:T(2,128)S(1)} %get-tuple-element.8), channel_id=1, source_target_pairs={{0,1},{1,2},{2,3},{3,4},{4,5},{5,6},{6,7},{7,8},{8,9},{9,10},{10,1... | collective-permute-start | bytes 1904 | tf_op jit(solution)/shard_map/ppermute | solution.py:25
  15.9 9.4 %collective-permute-start.3 = (f32[79,2,1]{2,1,0:T(2,128)S(1)}, f32[79,2,1]{2,1,0:T(2,128)S(1)}, u32[]{:S(2)}, u32[]{:S(2)}) collective-permute-start(f32[79,2,1]{2,1,0:T(2,128)S(1)} %get-tuple-element.7), channel_id=1, source_target_pairs={{1,0},{2,1},{3,2},{4,3},{5,4},{6,5},{7,6},{8,7},{9,8},{10,9},{11,1... | collective-permute-start | bytes 1904 | tf_op jit(solution)/shard_map/ppermute | solution.py:28
  34.1 198.0 %all-gather.3.cloned.1.call-start = ((), (), s32[]{:S(2)}) async-start(), calls=%async_computation | async-start | bytes 4456448 | tf_op jit(solution)/shard_map/all_gather | solution.py:95
  154.6 5.7 %copy-start.1 = (f32[2,8,128,2048]{3,2,1,0:T(8,128)}, f32[2,8,128,2048]{3,2,1,0:T(8,128)S(1)}, u32[]{:S(2)}) copy-start(f32[2,8,128,2048]{3,2,1,0:T(8,128)S(1)} %get-tuple-element.12) | copy-start | bytes 50331652
  237.5 21.0 %copy-start.3 = (f32[256,256]{1,0:T(8,128)S(1)}, f32[256,256]{1,0:T(8,128)}, u32[]{:S(2)}) copy-start(f32[256,256]{1,0:T(8,128)} %param.15) | copy-start | bytes 786436
  237.5 23.2 %copy-start.2 = (f32[1024,256]{1,0:T(8,128)S(1)}, f32[1024,256]{1,0:T(8,128)}, u32[]{:S(2)}) copy-start(f32[1024,256]{1,0:T(8,128)} %param.17) | copy-start | bytes 3145732
Sparse Core Ops, SparseCore 0:
  34.2 98.6 all-gather.4
  135.4 96.5 all-gather.2
where the time goes:
time: 270 us; the launch traced here: 269 us
  waiting for transfers between devices  166 us (61%)
  matrix products  48.1 us (18%)
  local copies, waits for them, and re-layouts  16.6 us (6%)
  between operations  13.6 us (5%)
  starting transfers between devices  13.5 us (5%)
  other arithmetic  11 us (4%)
    all_gather x1, waiting for transfers between devices, on_device(): key_piece = lax.all_gather(key_rows, 'lon', axis=1, tiled=True)  95 us
    all_gather x1, waiting for transfers between devices, on_device(): value_piece = lax.all_gather(value_rows, 'lon', axis=1, tiled=True)  68.5 us
    dot_general x1, matrix products, on_device(): added = jnp.einsum('yhqk,ykhe->yqhe', weights, value_heads, precision=HIGH)  21 us
    dot_general x1, matrix products, on_device(): jnp.einsum('yqhe,ykhe->yhqk', query_heads, key_heads, precision=HIGH)  16.3 us
    ppermute x2, starting transfers between devices, extended(): lax.ppermute(lax.slice_in_dim(block, 0, width, axis=dim), axis, backward)  9.55 us
    dot_general x6, matrix products, project(): return jnp.einsum('yxd,de->yxe', values, weight, precision=HIGH)  9.48 us
    unnamed x8, local copies, waits for them, and re-layouts  5.71 us
    all_gather x1, local copies, waits for them, and re-layouts, on_device(): value_piece = lax.all_gather(value_rows, 'lon', axis=1, tiled=True)  5.42 us
  transfers between devices with their start and end apart: 6, of which 3 were waited for; matrix products, arithmetic and copies ran while one was open for 12% of the time, Pallas kernels for 0%

commit v1 on v0

v1 whole, which is shorter than its diff:
```python
import functools
import math

import jax
import jax.numpy as jnp
from jax import lax
from jax.experimental import pallas as pl
from jax.experimental.pallas import tpu as pltpu
from jax.sharding import PartitionSpec as P

HEADS = 8
STEP_SIZE = 0.15
CENTER_LAT = 45.0
SPACING = 0.25
EPSILON = 1e-05
ROWS = 80
F32 = jnp.float32
BF16 = jnp.bfloat16
VMEM = pl.BlockSpec(memory_space=pltpu.VMEM)
SMEM = pl.BlockSpec(memory_space=pltpu.SMEM)


def split(values):
    high = values.astype(BF16)
    return high, (values - high.astype(F32)).astype(BF16)


def dot(left, right):
    return jnp.dot(left, right, preferred_element_type=F32)


def dot3(left, right):
    return dot(left[0], right[0]) + dot(left[1], right[0]) + dot(left[0], right[1])


def pack_kernel(fields_ref, kappa_ref, both_ref, mine_ref, other_ref):
    y = lax.axis_index("lon") // 8
    channels = fields_ref.shape[0]
    zero = jnp.zeros((1, 128), F32)
    rows = []
    for row in range(2):
        rows.append(
            jnp.concatenate([fields_ref[:, row, :], kappa_ref[row : row + 1, :], zero], axis=0)
        )
    flag = (jnp.zeros((ROWS, 128), jnp.int32) + y) == 0
    mine = jnp.where(flag, rows[0], rows[1])
    other = jnp.where(flag, rows[1], rows[0])
    both_ref[0] = mine
    both_ref[1] = other
    mine_ref[...] = mine
    other_ref[...] = other


def stencil_kernel(cos_ref, both_ref, outer_ref, partner_ref, partner_outer_ref, chunk_ref):
    inverse = 1.0 / cos_ref[0]
    face_inner = cos_ref[1]
    face_outer = cos_ref[2]
    lane = lax.broadcasted_iota(jnp.int32, (ROWS, 128), 1)
    sectors = (
        (both_ref[0], both_ref[1], outer_ref[...]),
        (partner_ref[1], partner_ref[0], partner_outer_ref[...]),
    )
    for index, (q, inner, outer) in enumerate(sectors):
        kappa = q[78:79]
        lat_term = (0.5 * (kappa + inner[78:79]) * face_inner) * (inner - q)
        lat_term = lat_term + (0.5 * (kappa + outer[78:79]) * face_outer) * (outer - q)
        east = pltpu.roll(q, 127, 1)
        flux = (0.5 * (kappa + east[78:79])) * (east - q)
        flux = jnp.where(lane == 127, 0.0, flux)
        lon_term = flux - pltpu.roll(flux, 1, 1)
        updated = q + STEP_SIZE * ((lat_term + lon_term * inverse) * inverse)
        padded = jnp.concatenate([q, jnp.zeros((128 - ROWS, 128), F32)], axis=0)
        turned = jnp.transpose(padded)
        chunk_ref[index] = updated
        chunk_ref[index, 78:79, :] = turned[0:1]
        chunk_ref[index, 79:80, :] = turned[127:128]


def weights_kernel(
    embed_ref, query_ref, key_ref, value_ref, out_ref, up_ref, down_ref,
    embed3_ref, qkv_high_ref, qkv_low_ref, out2_ref, up2_ref, down2_ref,
):
    embed = jnp.concatenate([embed_ref[...], jnp.zeros((128 - 78, 256), F32)], axis=0)
    high, low = split(jnp.transpose(embed)[:, :ROWS])
    embed3_ref[...] = jnp.concatenate([high, high, low], axis=1)
    for index, ref in enumerate((query_ref, key_ref, value_ref)):
        high, low = split(jnp.transpose(ref[...]))
        qkv_high_ref[index * 256 : (index + 1) * 256, :] = high
        qkv_low_ref[index * 256 : (index + 1) * 256, :] = low
    for source, target in ((out_ref, out2_ref), (up_ref, up2_ref), (down_ref, down2_ref)):
        high, low = split(source[...])
        target[0] = high
        target[1] = low


def layer_norm(values, axis):
    mean = jnp.mean(values, axis=axis, keepdims=True)
    centered = values - mean
    variance = jnp.mean(centered * centered, axis=axis, keepdims=True)
    return centered * lax.rsqrt(variance + EPSILON)


def block_kernel(
    cos_ref, *refs,
):
    pieces = refs[:8]
    embed3_ref, qkv_high_ref, qkv_low_ref, out2_ref, up2_ref, down2_ref = refs[8:14]
    mine_ref, send_ref = refs[14:16]
    edges, fixes, key3, value3, query3 = refs[16:]
    position = lax.axis_index("lon")
    y = position // 8
    z = position % 8
    inverse = 1.0 / cos_ref[0]
    step = 0.5 * STEP_SIZE * inverse * inverse
    for k in range(8):
        for index in range(2):
            half = y if index == 0 else 1 - y
            edges[half * 8 + jnp.bitwise_xor(z, k)] = pieces[k][index, 78:80, :]
    fixes[...] = jnp.zeros_like(fixes)
    for k in range(8):
        for index in range(2):
            half = y if index == 0 else 1 - y
            sector = half * 8 + jnp.bitwise_xor(z, k)
            here = edges[sector]
            west = edges[(sector + 15) % 16]
            east = edges[(sector + 1) % 16]
            first, last = here[0:1], here[1:2]
            west_last, east_first = west[1:2], east[0:1]
            slot = 2 * (2 * k + index)
            fixes[slot : slot + 1, :] = (
                step * (first[:, 78:79] + west_last[:, 78:79]) * (west_last - first)
            )
            fixes[slot + 1 : slot + 2, :] = (
                step * (last[:, 78:79] + east_first[:, 78:79]) * (east_first - last)
            )
    columns = jnp.transpose(fixes[...])[:ROWS]
    lane = lax.broadcasted_iota(jnp.int32, (ROWS, 128), 1)
    hidden = None
    for k in range(8):
        parts = []
        for index in range(2):
            slot = 2 * (2 * k + index)
            part = pieces[k][index]
            part = part + jnp.where(lane == 0, columns[:, slot : slot + 1], 0.0)
            part = part + jnp.where(lane == 127, columns[:, slot + 1 : slot + 2], 0.0)
            parts.append(part)
        high, low = split(jnp.concatenate(parts, axis=1))
        tokens = slice(256 * k, 256 * (k + 1))
        piece_hidden = dot(embed3_ref[...], jnp.concatenate([high, low, high], axis=0))
        normed = split(layer_norm(piece_hidden, 0))
        if k == 0:
            hidden = jnp.transpose(piece_hidden)
            weight = (qkv_high_ref[0:256], qkv_low_ref[0:256])
            scaled = dot3(weight, normed) * (math.log2(math.e) / math.sqrt(256 // HEADS))
            high, low = split(scaled)
            for h in range(HEADS):
                rows = slice(32 * h, 32 * h + 32)
                query3[h, 0:32] = high[rows]
                query3[h, 32:64] = high[rows]
                query3[h, 64:96] = low[rows]
        weight = (qkv_high_ref[256:768], qkv_low_ref[256:768])
        high, low = split(dot3(weight, normed))
        ones = jnp.ones((16, 256), BF16)
        for h in range(HEADS):
            rows = slice(32 * h, 32 * h + 32)
            key3[h, 0:32, tokens] = high[rows]
            key3[h, 32:64, tokens] = low[rows]
            key3[h, 64:96, tokens] = high[rows]
            rows = slice(256 + 32 * h, 256 + 32 * h + 32)
            value3[h, 0:32, tokens] = high[rows]
            value3[h, 32:64, tokens] = low[rows]
            value3[h, 64:80, tokens] = ones
    attended = []
    for h in range(HEADS):
        scores = lax.dot_general(
            query3[h], key3[h], (((0,), (0,)), ((), ())), preferred_element_type=F32
        )
        weights = jnp.exp2(scores - jnp.max(scores, axis=1, keepdims=True))
        high, low = split(weights)
        nt = (((1,), (1,)), ((), ()))
        sums = lax.dot_general(high, value3[h], nt, preferred_element_type=F32)
        sums = sums + lax.dot_general(low, value3[h], nt, preferred_element_type=F32)
        attended.append((sums[:, 0:32] + sums[:, 32:64]) / sums[:, 64:65])
    attended = split(jnp.concatenate(attended, axis=1))
    mixed = hidden + dot3(attended, (out2_ref[0], out2_ref[1]))
    normed = split(layer_norm(mixed, 1))
    activated = split(jax.nn.gelu(dot3(normed, (up2_ref[0], up2_ref[1]))))
    block = mixed + dot3(activated, (down2_ref[0], down2_ref[1]))
    mine_ref[...] = block[:128]
    send_ref[...] = block[128:]


def shape(*dims, dtype=F32):
    return jax.ShapeDtypeStruct(dims, dtype)


def call(kernel, outs, operands, scalars, scratch=(), limit=None, flops=0, moved=0):
    return pl.pallas_call(
        kernel,
        out_shape=outs,
        in_specs=[SMEM] * scalars + [VMEM] * (len(operands) - scalars),
        out_specs=jax.tree.map(lambda _: VMEM, outs),
        scratch_shapes=scratch,
        compiler_params=pltpu.CompilerParams(vmem_limit_bytes=limit),
        cost_estimate=pl.CostEstimate(flops=flops, bytes_accessed=moved, transcendentals=0),
    )(*operands)


def pairs_over(axis_sizes, move):
    lats, lons = axis_sizes
    found = []
    for lat in range(lats):
        for lon in range(lons):
            target = move(lat, lon)
            if 0 <= target[0] < lats:
                found.append((lat * lons + lon, target[0] * lons + target[1]))
    return found


def swap_lon(values, mask):
    count = lax.axis_size("lon")
    return lax.ppermute(values, "lon", [(r, r ^ mask) for r in range(count)])


def on_device(
    fields, diffusivity, w_embed, query_weight, key_weight, value_weight, out_weight, up_weight, down_weight,
):
    sizes = (lax.axis_size("lat"), lax.axis_size("lon"))
    lat = lax.axis_index("lat")
    y = lax.axis_index("lon") // 8
    row = (2 * lat + y).astype(F32)
    faces = jnp.stack([row + 0.5, (2 * lat + 1).astype(F32), (2 * (lat + y)).astype(F32)])
    half = 0.5 * 2 * sizes[0]
    cosines = jnp.cos((CENTER_LAT + (faces - half) * SPACING) * (math.pi / 180.0))

    plane = shape(ROWS, 128)
    pair = shape(2, ROWS, 128)
    both, mine, other = call(pack_kernel, (pair, plane, plane), (fields, diffusivity), 0, moved=400000)
    outward = pairs_over(sizes, lambda a, b: (a + 1 if b < 8 else a - 1, b))
    crossing = pairs_over(sizes, lambda a, b: (a - 1 if b < 8 else a + 1, b ^ 8))
    outer = lax.ppermute(other, ("lat", "lon"), outward)
    partner_outer = lax.ppermute(mine, ("lat", "lon"), crossing)
    partner = swap_lon(both, 8)
    prepared = call(
        weights_kernel,
        (
            shape(256, 3 * ROWS, dtype=BF16),
            shape(768, 256, dtype=BF16),
            shape(768, 256, dtype=BF16),
            shape(2, 256, 256, dtype=BF16),
            shape(2, 256, 1024, dtype=BF16),
            shape(2, 1024, 256, dtype=BF16),
        ),
        (w_embed, query_weight, key_weight, value_weight, out_weight, up_weight, down_weight),
        0,
        limit=24 * 2**20,
        moved=8000000,
    )
    chunk = call(stencil_kernel, pair, (cosines, both, outer, partner, partner_outer), 1, moved=400000)
    far = swap_lon(chunk, 4)
    near = [swap_lon(chunk, k) for k in (1, 2, 3)]
    far_near = [swap_lon(far, k) for k in (1, 2, 3)]
    pieces = [chunk, *near, far, *far_near]
    tile = shape(128, 256)
    own, send = call(
        block_kernel,
        (tile, tile),
        (cosines, *pieces, *prepared),
        1,
        scratch=[
            pltpu.VMEM((16, 2, 128), F32),
            pltpu.VMEM((128, 128), F32),
            pltpu.VMEM((HEADS, 96, 2048), BF16),
            pltpu.VMEM((HEADS, 80, 2048), BF16),
            pltpu.VMEM((HEADS, 96, 256), BF16),
        ],
        limit=48 * 2**20,
        flops=10**10,
        moved=6000000,
    )
    received = swap_lon(send, 8)
    first = jnp.where(y == 0, own, received)
    second = jnp.where(y == 0, received, own)
    return jnp.stack([first, second])


def solution(mesh):
    placed = (P(None, "lat", "lon"), P("lat", "lon"), P(), P(), P(), P(), P(), P(), P())
    return jax.shard_map(
        on_device, mesh=mesh, in_specs=placed, out_specs=P("lat", "lon", None), check_vma=False
    )
```

time: 270 us -> 68.6 us (0.25)
  waiting for transfers between devices: 166 us -> 11.3 us
  matrix products: 48.1 us -> 0 us
  Pallas kernels: 0 us -> 19.6 us
  starting transfers between devices: 13.5 us -> 29.3 us
  between operations: 13.6 us -> 0.09 us
  local copies, waits for them, and re-layouts: 16.6 us -> 6.55 us
  other arithmetic: 11 us -> 1.38 us
    all_gather x2 -> x0, waiting for transfers between devices: 163 us -> none  [the longest x1 95 us: on_device(): key_piece = lax.all_gather(key_rows, 'lon', axis=1, tiled=True)]
    dot_general x9 -> x0, matrix products: 48.1 us -> none  [the longest x1 21 us: on_device(): added = jnp.einsum('yhqk,ykhe->yqhe', weights, value_heads, precision=HIGH)]
    pallas_call x0 -> x4, Pallas kernels: none -> 19.6 us  [call(): pl.pallas_call(kernel, out_shape=outs, in_specs=[SMEM] * scalars + [VMEM]...]
    ppermute x4 -> x11, starting transfers between devices: 13.5 us -> 29.3 us  [the longest x9 22.1 us: swap_lon(): return lax.ppermute(values, 'lon', [(r, r ^ mask) for r in range(count)])]
    all_gather x2 -> x0, local copies, waits for them, and re-layouts: 10.8 us -> none  [the longest x1 5.42 us: on_device(): value_piece = lax.all_gather(value_rows, 'lon', axis=1, tiled=True)]
    ppermute x4 -> x11, waiting for transfers between devices: 2.98 us -> 11.3 us  [the longest x9 11.1 us: swap_lon(): return lax.ppermute(values, 'lon', [(r, r ^ mask) for r in range(count)])]
    reduce_sum x3 -> x0, other arithmetic: 3.64 us -> none  [the longest x1 3.27 us: on_device(): new_sum = jnp.sum(weights, axis=-1)]
    mul x5 -> x0, other arithmetic: 3.26 us -> none  [the longest x2 1.93 us: tendency(): north_flux = north_coef * (fields_lat[:, 1:] - fields_lat[:, :-1])]
  transfers between devices with their start and end apart: 6 -> 11, of which waited for: 3 -> 4; matrix products, arithmetic and copies ran while one was open for 12% -> 1% of each run, Pallas kernels for 0% -> 1%
where the time goes in v1:
time: 68.6 us; the launch traced here: 68.2 us
  starting transfers between devices  29.3 us (43%)
  Pallas kernels  19.6 us (29%)
  waiting for transfers between devices  11.3 us (16%)
  local copies, waits for them, and re-layouts  6.55 us (10%)
  other arithmetic  1.38 us (2%)
    ppermute x9, starting transfers between devices, swap_lon(): return lax.ppermute(values, 'lon', [(r, r ^ mask) for r in range(count)])  22.1 us
    pallas_call x4, Pallas kernels, call(): pl.pallas_call(kernel, out_shape=outs, in_specs=[SMEM] * scalars + [VMEM]...  19.6 us
    ppermute x9, waiting for transfers between devices, swap_lon(): return lax.ppermute(values, 'lon', [(r, r ^ mask) for r in range(count)])  11.1 us
    unnamed x24, local copies, waits for them, and re-layouts  6.55 us
    ppermute x1, starting transfers between devices, on_device(): partner_outer = lax.ppermute(mine, ('lat', 'lon'), crossing)  5.29 us
    ppermute x1, starting transfers between devices, on_device(): outer = lax.ppermute(other, ('lat', 'lon'), outward)  1.91 us
  transfers between devices with their start and end apart: 11, of which 4 were waited for; matrix products, arithmetic and copies ran while one was open for 1% of the time, Pallas kernels for 1%

profile of v1, /device:TPU:6, one launch (start us, length us, event | category | flops | bytes accessed | tf_op | source)
XLA Modules:
  0.0 68.2 jit_solution(17553014837074838569)
XLA Ops:
  0.0 1.6 %shard_map.91 = (f32[2,80,128]{2,1,0:T(8,128)}, f32[80,128]{1,0:T(8,128)}, f32[80,128]{1,0:T(8,128)}) custom-call(f32[78,2,128]{2,1,0:T(2,128)} %fields_ref.1, f32[2,128]{1,0:T(2,128)} %kappa_ref.1), custom_call_target="tpu_custom_call" | custom-call | bytes 400000 | tf_op jit(solution)/shard_map/pallas_call | solution.py:198
  1.6 1.9 %collective-permute-start = (f32[80,128]{1,0:T(8,128)}, f32[80,128]{1,0:T(8,128)S(1)}, u32[]{:S(2)}, u32[]{:S(2)}) collective-permute-start(f32[80,128]{1,0:T(8,128)} %get-tuple-element.17), channel_id=1, source_target_pairs={{0,16},{1,17},{2,18},{3,19},{4,20},{5,21},{6,22},{7,23},{16,32},{1... | collective-permute-start | bytes 122888 | tf_op jit(solution)/shard_map/ppermute | solution.py:241
  3.6 5.3 %collective-permute-start.2 = (f32[80,128]{1,0:T(8,128)}, f32[80,128]{1,0:T(8,128)S(1)}, u32[]{:S(2)}, u32[]{:S(2)}) collective-permute-start(f32[80,128]{1,0:T(8,128)} %get-tuple-element.18), channel_id=1, source_target_pairs={{8,16},{9,17},{10,18},{11,19},{12,20},{13,21},{14,22},{15,23},{16,... | collective-permute-start | bytes 122888 | tf_op jit(solution)/shard_map/ppermute | solution.py:242
  8.8 1.5 %collective-permute-start.1 = (f32[2,80,128]{2,1,0:T(8,128)}, f32[2,80,128]{2,1,0:T(8,128)S(1)}, u32[]{:S(2)}, u32[]{:S(2)}) collective-permute-start(f32[2,80,128]{2,1,0:T(8,128)} %get-tuple-element.16.both_ref), channel_id=1, source_target_pairs={{0,8},{1,9},{2,10},{3,11},{4,12},{5,13},{6,14},{7,15},{8,0},{9,1},... | collective-permute-start | bytes 245768 | tf_op jit(solution)/shard_map/ppermute | solution.py:222
  10.4 0.6 multiply_cosine_fusion.cos_ref
  11.2 4.7 %collective-permute-done.1.partner_ref = f32[2,80,128]{2,1,0:T(8,128)S(1)} collective-permute-done((f32[2,80,128]{2,1,0:T(8,128)}, f32[2,80,128]{2,1,0:T(8,128)S(1)}, u32[]{:S(2)}, u32[]{:S(2)}) %collective-permute-start.1) | collective-permute-done | bytes 81952 | tf_op jit(solution)/shard_map/ppermute | solution.py:222
  16.5 1.8 %shard_map.92.refs_0_ = f32[2,80,128]{2,1,0:T(8,128)} custom-call(f32[3]{0:T(128)} %multiply_cosine_fusion.cos_ref, f32[2,80,128]{2,1,0:T(8,128)} %get-tuple-element.16.both_ref, f32[80,128]{1,0:T(8,128)} %copy-done.10, f32[2,80,128]{2,1,0:T(8,128)} %copy-done.9, f32[80,128]{1,0:T(8,128)} %copy-done.11), custom_call_target="tpu_custom_call" | custom-call | bytes 400000 | tf_op jit(solution)/shard_map/pallas_call | solution.py:198
  18.4 7.2 %collective-permute-start.6 = (f32[2,80,128]{2,1,0:T(8,128)}, f32[2,80,128]{2,1,0:T(8,128)S(1)}, u32[]{:S(2)}, u32[]{:S(2)}) collective-permute-start(f32[2,80,128]{2,1,0:T(8,128)} %shard_map.92.refs_0_), channel_id=1, source_target_pairs={{0,4},{1,5},{2,6},{3,7},{4,0},{5,1},{6,2},{7,3},{8,12},{9,13},{10,... | collective-permute-start | bytes 245768 | tf_op jit(solution)/shard_map/ppermute | solution.py:222
  25.6 1.9 %collective-permute-start.5 = (f32[2,80,128]{2,1,0:T(8,128)}, f32[2,80,128]{2,1,0:T(8,128)S(1)}, u32[]{:S(2)}, u32[]{:S(2)}) collective-permute-start(f32[2,80,128]{2,1,0:T(8,128)} %shard_map.92.refs_0_), channel_id=1, source_target_pairs={{0,3},{1,2},{2,1},{3,0},{4,7},{5,6},{6,5},{7,4},{8,11},{9,10},{10,... | collective-permute-start | bytes 245768 | tf_op jit(solution)/shard_map/ppermute | solution.py:222
  28.0 1.9 %collective-permute-start.3 = (f32[2,80,128]{2,1,0:T(8,128)}, f32[2,80,128]{2,1,0:T(8,128)S(1)}, u32[]{:S(2)}, u32[]{:S(2)}) collective-permute-start(f32[2,80,128]{2,1,0:T(8,128)} %shard_map.92.refs_0_), channel_id=1, source_target_pairs={{0,1},{1,0},{2,3},{3,2},{4,5},{5,4},{6,7},{7,6},{8,9},{9,8},{10,11... | collective-permute-start | bytes 245768 | tf_op jit(solution)/shard_map/ppermute | solution.py:222
  30.0 2.6 %collective-permute-start.9 = (f32[2,80,128]{2,1,0:T(8,128)S(1)}, f32[2,80,128]{2,1,0:T(8,128)S(1)}, u32[]{:S(2)}, u32[]{:S(2)}) collective-permute-start(f32[2,80,128]{2,1,0:T(8,128)S(1)} %collective-permute-done.6.refs_4_), channel_id=1, source_target_pairs={{0,3},{1,2},{2,1},{3,0},{4,7},{5,6},{6,5},{7,4},{8,11},{9,10},{10,... | collective-permute-start | bytes 245768 | tf_op jit(solution)/shard_map/ppermute | solution.py:222
  32.6 0.8 %collective-permute-start.8 = (f32[2,80,128]{2,1,0:T(8,128)S(1)}, f32[2,80,128]{2,1,0:T(8,128)S(1)}, u32[]{:S(2)}, u32[]{:S(2)}) collective-permute-start(f32[2,80,128]{2,1,0:T(8,128)S(1)} %collective-permute-done.6.refs_4_), channel_id=1, source_target_pairs={{0,2},{1,3},{2,0},{3,1},{4,6},{5,7},{6,4},{7,5},{8,10},{9,11},{10,... | collective-permute-start | bytes 245768 | tf_op jit(solution)/shard_map/ppermute | solution.py:222
  33.4 3.7 %collective-permute-start.7 = (f32[2,80,128]{2,1,0:T(8,128)S(1)}, f32[2,80,128]{2,1,0:T(8,128)S(1)}, u32[]{:S(2)}, u32[]{:S(2)}) collective-permute-start(f32[2,80,128]{2,1,0:T(8,128)S(1)} %collective-permute-done.6.refs_4_), channel_id=1, source_target_pairs={{0,1},{1,0},{2,3},{3,2},{4,5},{5,4},{6,7},{7,6},{8,9},{9,8},{10,11... | collective-permute-start | bytes 245768 | tf_op jit(solution)/shard_map/ppermute | solution.py:222
  37.1 1.2 %copy-done = f32[256,1024]{1,0:T(8,128)S(1)} copy-done((f32[256,1024]{1,0:T(8,128)S(1)}, f32[256,1024]{1,0:T(8,128)}, u32[]{:S(2)}) %copy-start) | copy-done | bytes 1048600
  38.3 1.2 %copy-done.1 = f32[1024,256]{1,0:T(8,128)S(1)} copy-done((f32[1024,256]{1,0:T(8,128)S(1)}, f32[1024,256]{1,0:T(8,128)}, u32[]{:S(2)}) %copy-start.1) | copy-done | bytes 1048600
  39.5 0.9 %copy-done.3 = f32[256,256]{1,0:T(8,128)S(1)} copy-done((f32[256,256]{1,0:T(8,128)S(1)}, f32[256,256]{1,0:T(8,128)}, u32[]{:S(2)}) %copy-start.3) | copy-done | bytes 262168
  40.5 0.9 %copy-done.4 = f32[256,256]{1,0:T(8,128)S(1)} copy-done((f32[256,256]{1,0:T(8,128)S(1)}, f32[256,256]{1,0:T(8,128)}, u32[]{:S(2)}) %copy-start.4) | copy-done | bytes 262168
  41.4 0.9 %copy-done.5 = f32[256,256]{1,0:T(8,128)S(1)} copy-done((f32[256,256]{1,0:T(8,128)S(1)}, f32[256,256]{1,0:T(8,128)}, u32[]{:S(2)}) %copy-start.5) | copy-done | bytes 262168
  42.4 1.0 %shard_map.93 = (bf16[256,240]{1,0:T(8,128)(2,1)S(1)}, bf16[768,256]{1,0:T(8,128)(2,1)S(1)}, bf16[768,256]{1,0:T(8,128)(2,1)S(1)}, bf16[2,256,256]{2,1,0:T(8,128...) custom-call(f32[78,256]{1,0:T(8,128)S(1)} %copy-done.6, f32[256,256]{1,0:T(8,128)S(1)} %copy-done.2, ...), custom_call_target="tpu_custom_call" | custom-call | bytes 8000000 | tf_op jit(solution)/shard_map/pallas_call | solution.py:198
  43.4 1.3 %collective-permute-done.8.refs_6_ = f32[2,80,128]{2,1,0:T(8,128)S(1)} collective-permute-done((f32[2,80,128]{2,1,0:T(8,128)S(1)}, f32[2,80,128]{2,1,0:T(8,128)S(1)}, u32[]{:S(2)}, u32[]{:S(2)}) %collective-permute-start.8) | collective-permute-done | bytes 81952 | tf_op jit(solution)/shard_map/ppermute | solution.py:222
  45.3 15.2 %shard_map.94 = (f32[128,256]{1,0:T(8,128)S(1)}, f32[128,256]{1,0:T(8,128)S(1)}) custom-call(f32[3]{0:T(128)S(1)} %copy-done.8, f32[2,80,128]{2,1,0:T(8,128)S(1)} %copy-done.7, f32[2,80,128]{2,1,0:T(8,128)S(1)} %collective-permute-done.3.refs_1_, f32[2,80,128]{2,1,0:T(8,128)S(1)} %collective-permute-done.4.refs_2_, ...), custom_call_target="tpu_custom_call" | custom-call | flops 10000000000 | bytes 6000000 | tf_op jit(solution)/shard_map/pallas_call | solution.py:198
  60.5 1.9 %collective-permute-start.10 = (f32[128,256]{1,0:T(8,128)S(1)}, f32[128,256]{1,0:T(8,128)S(1)}, u32[]{:S(2)}, u32[]{:S(2)}) collective-permute-start(f32[128,256]{1,0:T(8,128)S(1)} %get-tuple-element.26), channel_id=1, source_target_pairs={{0,8},{1,9},{2,10},{3,11},{4,12},{5,13},{6,14},{7,15},{8,0},{9,1},... | collective-permute-start | bytes 393224 | tf_op jit(solution)/shard_map/ppermute | solution.py:222
  62.4 5.1 %collective-permute-done.10 = f32[128,256]{1,0:T(8,128)S(1)} collective-permute-done((f32[128,256]{1,0:T(8,128)S(1)}, f32[128,256]{1,0:T(8,128)S(1)}, u32[]{:S(2)}, u32[]{:S(2)}) %collective-permute-start.10) | collective-permute-done | bytes 131104 | tf_op jit(solution)/shard_map/ppermute | solution.py:222
  67.5 0.7 %pad_maximum_fusion = f32[2,128,256]{2,1,0:T(8,128)} fusion(f32[1,128,256]{2,1,0:T(8,128)S(1)} %get-tuple-element.28, f32[1,128,256]{2,1,0:T(8,128)S(1)} %get-tuple-element.27), kind=kLoop, calls=%fused_computation | loop fusion | flops 65536 | bytes 524288 | tf_op jit(solution)/shard_map/stack | solution.py:284
  (29 shorter events, 2.0 us)
Async XLA Ops:
  0.0 37.1 %copy-start.2 = (f32[256,256]{1,0:T(8,128)S(1)}, f32[256,256]{1,0:T(8,128)}, u32[]{:S(2)}) copy-start(f32[256,256]{1,0:T(8,128)} %query_ref.1) | copy-start | bytes 786436
  1.6 9.4 %collective-permute-start = (f32[80,128]{1,0:T(8,128)}, f32[80,128]{1,0:T(8,128)S(1)}, u32[]{:S(2)}, u32[]{:S(2)}) collective-permute-start(f32[80,128]{1,0:T(8,128)} %get-tuple-element.17), channel_id=1, source_target_pairs={{0,16},{1,17},{2,18},{3,19},{4,20},{5,21},{6,22},{7,23},{16,32},{1... | collective-permute-start | bytes 122888 | tf_op jit(solution)/shard_map/ppermute | solution.py:241
  3.6 7.6 %collective-permute-start.2 = (f32[80,128]{1,0:T(8,128)}, f32[80,128]{1,0:T(8,128)S(1)}, u32[]{:S(2)}, u32[]{:S(2)}) collective-permute-start(f32[80,128]{1,0:T(8,128)} %get-tuple-element.18), channel_id=1, source_target_pairs={{8,16},{9,17},{10,18},{11,19},{12,20},{13,21},{14,22},{15,23},{16,... | collective-permute-start | bytes 122888 | tf_op jit(solution)/shard_map/ppermute | solution.py:242
  8.8 7.1 %collective-permute-start.1 = (f32[2,80,128]{2,1,0:T(8,128)}, f32[2,80,128]{2,1,0:T(8,128)S(1)}, u32[]{:S(2)}, u32[]{:S(2)}) collective-permute-start(f32[2,80,128]{2,1,0:T(8,128)} %get-tuple-element.16.both_ref), channel_id=1, source_target_pairs={{0,8},{1,9},{2,10},{3,11},{4,12},{5,13},{6,14},{7,15},{8,0},{9,1},... | collective-permute-start | bytes 245768 | tf_op jit(solution)/shard_map/ppermute | solution.py:222
  11.0 26.1 %copy-start.6 = (f32[78,256]{1,0:T(8,128)S(1)}, f32[78,256]{1,0:T(8,128)}, u32[]{:S(2)}) copy-start(f32[78,256]{1,0:T(8,128)} %embed_ref.1) | copy-start | bytes 239620
  11.0 4.9 %copy-start.10 = (f32[80,128]{1,0:T(8,128)}, f32[80,128]{1,0:T(8,128)S(1)}, u32[]{:S(2)}) copy-start(f32[80,128]{1,0:T(8,128)S(1)} %collective-permute-done.outer_ref) | copy-start | bytes 122884
  11.2 4.7 %copy-start.11 = (f32[80,128]{1,0:T(8,128)}, f32[80,128]{1,0:T(8,128)S(1)}, u32[]{:S(2)}) copy-start(f32[80,128]{1,0:T(8,128)S(1)} %collective-permute-done.2.partner_outer_ref) | copy-start | bytes 122884
  15.9 0.6 copy-start.9
  18.4 11.6 %collective-permute-start.6 = (f32[2,80,128]{2,1,0:T(8,128)}, f32[2,80,128]{2,1,0:T(8,128)S(1)}, u32[]{:S(2)}, u32[]{:S(2)}) collective-permute-start(f32[2,80,128]{2,1,0:T(8,128)} %shard_map.92.refs_0_), channel_id=1, source_target_pairs={{0,4},{1,5},{2,6},{3,7},{4,0},{5,1},{6,2},{7,3},{8,12},{9,13},{10,... | collective-permute-start | bytes 245768 | tf_op jit(solution)/shard_map/ppermute | solution.py:222
  25.6 7.8 %collective-permute-start.5 = (f32[2,80,128]{2,1,0:T(8,128)}, f32[2,80,128]{2,1,0:T(8,128)S(1)}, u32[]{:S(2)}, u32[]{:S(2)}) collective-permute-start(f32[2,80,128]{2,1,0:T(8,128)} %shard_map.92.refs_0_), channel_id=1, source_target_pairs={{0,3},{1,2},{2,1},{3,0},{4,7},{5,6},{6,5},{7,4},{8,11},{9,10},{10,... | collective-permute-start | bytes 245768 | tf_op jit(solution)/shard_map/ppermute | solution.py:222
  27.5 15.9 %collective-permute-start.4 = (f32[2,80,128]{2,1,0:T(8,128)}, f32[2,80,128]{2,1,0:T(8,128)S(1)}, u32[]{:S(2)}, u32[]{:S(2)}) collective-permute-start(f32[2,80,128]{2,1,0:T(8,128)} %shard_map.92.refs_0_), channel_id=1, source_target_pairs={{0,2},{1,3},{2,0},{3,1},{4,6},{5,7},{6,4},{7,5},{8,10},{9,11},{10,... | collective-permute-start | bytes 245768 | tf_op jit(solution)/shard_map/ppermute | solution.py:222
  28.0 15.4 %collective-permute-start.3 = (f32[2,80,128]{2,1,0:T(8,128)}, f32[2,80,128]{2,1,0:T(8,128)S(1)}, u32[]{:S(2)}, u32[]{:S(2)}) collective-permute-start(f32[2,80,128]{2,1,0:T(8,128)} %shard_map.92.refs_0_), channel_id=1, source_target_pairs={{0,1},{1,0},{2,3},{3,2},{4,5},{5,4},{6,7},{7,6},{8,9},{9,8},{10,11... | collective-permute-start | bytes 245768 | tf_op jit(solution)/shard_map/ppermute | solution.py:222
  30.0 13.5 %collective-permute-start.9 = (f32[2,80,128]{2,1,0:T(8,128)S(1)}, f32[2,80,128]{2,1,0:T(8,128)S(1)}, u32[]{:S(2)}, u32[]{:S(2)}) collective-permute-start(f32[2,80,128]{2,1,0:T(8,128)S(1)} %collective-permute-done.6.refs_4_), channel_id=1, source_target_pairs={{0,3},{1,2},{2,1},{3,0},{4,7},{5,6},{6,5},{7,4},{8,11},{9,10},{10,... | collective-permute-start | bytes 245768 | tf_op jit(solution)/shard_map/ppermute | solution.py:222
  32.6 12.1 %collective-permute-start.8 = (f32[2,80,128]{2,1,0:T(8,128)S(1)}, f32[2,80,128]{2,1,0:T(8,128)S(1)}, u32[]{:S(2)}, u32[]{:S(2)}) collective-permute-start(f32[2,80,128]{2,1,0:T(8,128)S(1)} %collective-permute-done.6.refs_4_), channel_id=1, source_target_pairs={{0,2},{1,3},{2,0},{3,1},{4,6},{5,7},{6,4},{7,5},{8,10},{9,11},{10,... | collective-permute-start | bytes 245768 | tf_op jit(solution)/shard_map/ppermute | solution.py:222
  33.4 11.3 %collective-permute-start.7 = (f32[2,80,128]{2,1,0:T(8,128)S(1)}, f32[2,80,128]{2,1,0:T(8,128)S(1)}, u32[]{:S(2)}, u32[]{:S(2)}) collective-permute-start(f32[2,80,128]{2,1,0:T(8,128)S(1)} %collective-permute-done.6.refs_4_), channel_id=1, source_target_pairs={{0,1},{1,0},{2,3},{3,2},{4,5},{5,4},{6,7},{7,6},{8,9},{9,8},{10,11... | collective-permute-start | bytes 245768 | tf_op jit(solution)/shard_map/ppermute | solution.py:222
  37.1 1.2 %copy-start = (f32[256,1024]{1,0:T(8,128)S(1)}, f32[256,1024]{1,0:T(8,128)}, u32[]{:S(2)}) copy-start(f32[256,1024]{1,0:T(8,128)} %up_ref.1) | copy-start | bytes 3145732
  38.3 1.2 %copy-start.1 = (f32[1024,256]{1,0:T(8,128)S(1)}, f32[1024,256]{1,0:T(8,128)}, u32[]{:S(2)}) copy-start(f32[1024,256]{1,0:T(8,128)} %down_ref.1) | copy-start | bytes 3145732
  39.5 0.9 %copy-start.3 = (f32[256,256]{1,0:T(8,128)S(1)}, f32[256,256]{1,0:T(8,128)}, u32[]{:S(2)}) copy-start(f32[256,256]{1,0:T(8,128)} %key_ref.1) | copy-start | bytes 786436
  40.5 0.9 %copy-start.4 = (f32[256,256]{1,0:T(8,128)S(1)}, f32[256,256]{1,0:T(8,128)}, u32[]{:S(2)}) copy-start(f32[256,256]{1,0:T(8,128)} %value_ref.1) | copy-start | bytes 786436
  41.4 0.9 %copy-start.5 = (f32[256,256]{1,0:T(8,128)S(1)}, f32[256,256]{1,0:T(8,128)}, u32[]{:S(2)}) copy-start(f32[256,256]{1,0:T(8,128)} %out_ref.1) | copy-start | bytes 786436
  42.4 2.3 %copy-start.7 = (f32[2,80,128]{2,1,0:T(8,128)S(1)}, f32[2,80,128]{2,1,0:T(8,128)}, u32[]{:S(2)}) copy-start(f32[2,80,128]{2,1,0:T(8,128)} %shard_map.92.refs_0_) | copy-start | bytes 245764
  44.7 0.6 copy-start.8
  60.5 7.0 %collective-permute-start.10 = (f32[128,256]{1,0:T(8,128)S(1)}, f32[128,256]{1,0:T(8,128)S(1)}, u32[]{:S(2)}, u32[]{:S(2)}) collective-permute-start(f32[128,256]{1,0:T(8,128)S(1)} %get-tuple-element.26), channel_id=1, source_target_pairs={{0,8},{1,9},{2,10},{3,11},{4,12},{5,13},{6,14},{7,15},{8,0},{9,1},... | collective-permute-start | bytes 393224 | tf_op jit(solution)/shard_map/ppermute | solution.py:222

commit v2 on v1

v2 whole, which is shorter than its diff:
```python
import functools
import math

import jax
import jax.numpy as jnp
from jax import lax
from jax.experimental import pallas as pl
from jax.experimental.pallas import tpu as pltpu
from jax.sharding import PartitionSpec as P

HEADS = 8
STEP_SIZE = 0.15
CENTER_LAT = 45.0
SPACING = 0.25
EPSILON = 1e-05
ROWS = 80
F32 = jnp.float32
BF16 = jnp.bfloat16
VMEM = pl.BlockSpec(memory_space=pltpu.VMEM)
SMEM = pl.BlockSpec(memory_space=pltpu.SMEM)


def split(values):
    high = values.astype(BF16)
    return high, (values - high.astype(F32)).astype(BF16)


def dot(left, right):
    return jnp.dot(left, right, preferred_element_type=F32)


def dot3(left, right):
    return dot(left[0], right[0]) + dot(left[1], right[0]) + dot(left[0], right[1])


def pack_kernel(fields_ref, kappa_ref, both_ref, mine_ref, other_ref):
    y = lax.axis_index("lon") // 8
    channels = fields_ref.shape[0]
    zero = jnp.zeros((1, 128), F32)
    rows = []
    for row in range(2):
        rows.append(
            jnp.concatenate([fields_ref[:, row, :], kappa_ref[row : row + 1, :], zero], axis=0)
        )
    flag = (jnp.zeros((ROWS, 128), jnp.int32) + y) == 0
    mine = jnp.where(flag, rows[0], rows[1])
    other = jnp.where(flag, rows[1], rows[0])
    both_ref[0] = mine
    both_ref[1] = other
    mine_ref[...] = mine
    other_ref[...] = other


def stencil_kernel(
    cos_ref, both_ref, outer_ref, partner_ref, partner_outer_ref, order_ref, chunk_ref, edges_ref
):
    inverse = 1.0 / cos_ref[0]
    face_inner = cos_ref[1]
    face_outer = cos_ref[2]
    lane = lax.broadcasted_iota(jnp.int32, (ROWS, 128), 1)
    sectors = (
        (both_ref[0], both_ref[1], outer_ref[...]),
        (partner_ref[1], partner_ref[0], partner_outer_ref[...]),
    )
    for index, (q, inner, outer) in enumerate(sectors):
        kappa = q[78:79]
        lat_term = (0.5 * (kappa + inner[78:79]) * face_inner) * (inner - q)
        lat_term = lat_term + (0.5 * (kappa + outer[78:79]) * face_outer) * (outer - q)
        east = pltpu.roll(q, 127, 1)
        flux = (0.5 * (kappa + east[78:79])) * (east - q)
        flux = jnp.where(lane == 127, 0.0, flux)
        lon_term = flux - pltpu.roll(flux, 1, 1)
        updated = q + STEP_SIZE * ((lat_term + lon_term * inverse) * inverse)
        padded = jnp.concatenate([q, jnp.zeros((128 - ROWS, 128), F32)], axis=0)
        turned = jnp.transpose(padded)
        chunk_ref[index] = updated
        chunk_ref[index, 78:79, :] = turned[0:1]
        chunk_ref[index, 79:80, :] = turned[127:128]
        edges_ref[index, 0:1, :] = turned[0:1]
        edges_ref[index, 1:2, :] = turned[127:128]


def first_weights_kernel(*refs):
    sources = refs[:4]
    embed3_ref, qkv_high_ref, qkv_low_ref = refs[5:8]
    embed = jnp.concatenate([sources[0][...], jnp.zeros((128 - 78, 256), F32)], axis=0)
    high, low = split(jnp.transpose(embed)[:, :ROWS])
    embed3_ref[...] = jnp.concatenate([high, high, low], axis=1)
    for index in range(3):
        high, low = split(jnp.transpose(sources[1 + index][...]))
        qkv_high_ref[index * 256 : (index + 1) * 256, :] = high
        qkv_low_ref[index * 256 : (index + 1) * 256, :] = low


def last_weights_kernel(*refs):
    for source, target in zip(refs[:3], refs[4:7]):
        high, low = split(source[...])
        target[0] = high
        target[1] = low
    refs[7][...] = jnp.zeros_like(refs[7])


def layer_norm(values, axis):
    mean = jnp.mean(values, axis=axis, keepdims=True)
    centered = values - mean
    variance = jnp.mean(centered * centered, axis=axis, keepdims=True)
    return centered * lax.rsqrt(variance + EPSILON)


def embed_tokens(columns, embed3_ref):
    high, low = split(columns)
    hidden = dot(embed3_ref[...], jnp.concatenate([high, low, high], axis=0))
    return hidden, split(layer_norm(hidden, 0))


def store_keys(normed, masked, start, qkv_high_ref, qkv_low_ref, key3, value3):
    count = masked.shape[1]
    tokens = slice(start, start + count)
    high, low = split(dot3((qkv_high_ref[256:768], qkv_low_ref[256:768]), normed))
    row = lax.broadcasted_iota(jnp.int32, (16, count), 0)
    mask = jnp.where(jnp.logical_and(masked, row == 0), -1e30, 0.0).astype(BF16)
    ones = jnp.ones((16, count), BF16)
    for h in range(HEADS):
        rows = slice(32 * h, 32 * h + 32)
        key3[h, 0:32, tokens] = high[rows]
        key3[h, 32:64, tokens] = low[rows]
        key3[h, 64:96, tokens] = high[rows]
        key3[h, 96:112, tokens] = mask
        rows = slice(256 + 32 * h, 256 + 32 * h + 32)
        value3[h, 0:32, tokens] = high[rows]
        value3[h, 32:64, tokens] = low[rows]
        value3[h, 64:80, tokens] = ones


def face_fix(step, here, beyond):
    return step * (here[:, 78:79] + beyond[:, 78:79]) * (beyond - here)


def attend(queries, key3, value3, starts):
    nt = (((1,), (1,)), ((), ()))
    found = []
    scores = dot(queries(0), key3[0])
    for h in range(HEADS):
        later = dot(queries(h + 1), key3[h + 1]) if h + 1 < HEADS else None
        largest = jnp.max(scores, axis=1, keepdims=True)
        if starts is not None:
            largest = jnp.maximum(largest, starts(h))
        high, low = split(jnp.exp2(scores - largest))
        sums = lax.dot_general(high, value3[h], nt, preferred_element_type=F32)
        sums = sums + lax.dot_general(low, value3[h], nt, preferred_element_type=F32)
        found.append((largest, sums))
        scores = later
    return found


def place_edges(total, part, slot):
    lane = lax.broadcasted_iota(jnp.int32, (ROWS, 128), 1)
    total = jnp.where(lane == 2 * slot, pltpu.roll(part, 2 * slot, 1), total)
    return jnp.where(lane == 2 * slot + 1, pltpu.roll(part, 2 * slot + 2, 1), total)


def early_kernel(cos_ref, *refs):
    pieces = refs[:5]
    across_ref, embed3_ref, qkv_high_ref, qkv_low_ref = refs[5:9]
    hidden_ref, query3_ref, state_ref, columns_ref, edges_ref = refs[10:15]
    key3, value3 = refs[15:]
    z = lax.axis_index("lon") % 8
    inverse = 1.0 / cos_ref[0]
    step = 0.5 * STEP_SIZE * inverse * inverse
    total = jnp.zeros((ROWS, 128), F32)
    for k in range(5):
        for index in range(2):
            edges_ref[2 * k + index] = pieces[k][index, 78:80, :]
            total = place_edges(total, pieces[k][index], 2 * k + index)
    columns_ref[...] = total
    even = z % 2 == 0
    wraps = jnp.logical_or(z == 0, z == 7).astype(jnp.int32)
    lane = lax.broadcasted_iota(jnp.int32, (ROWS, 128), 1)
    flag = (jnp.zeros((2, 128), jnp.int32) + z % 2) == 0
    fixes = []
    for index in range(2):
        here = pieces[0][index, 78:80, :]
        beside = pieces[1][index, 78:80, :]
        across = across_ref[jnp.where(wraps == 1, 1 - index, index)]
        west = jnp.where(flag, across, beside)
        east = jnp.where(flag, beside, across)
        fixes.append(face_fix(step, here[0:1], west[1:2]))
        fixes.append(face_fix(step, here[1:2], east[0:1]))
    fixes = jnp.transpose(jnp.concatenate(fixes + [jnp.zeros((124, 128), F32)], axis=0))[:ROWS]
    parts = []
    for index in range(2):
        part = pieces[0][index]
        part = part + jnp.where(lane == 0, fixes[:, 2 * index : 2 * index + 1], 0.0)
        part = part + jnp.where(lane == 127, fixes[:, 2 * index + 1 : 2 * index + 2], 0.0)
        parts.append(part)
    for k in range(1, 5):
        parts += [pieces[k][0], pieces[k][1]]
    hidden, normed = embed_tokens(jnp.concatenate(parts, axis=1), embed3_ref)
    hidden_ref[...] = jnp.transpose(hidden[:, :256])
    own = (normed[0][:, :256], normed[1][:, :256])
    scaled = dot3((qkv_high_ref[0:256], qkv_low_ref[0:256]), own)
    scaled = jnp.transpose(scaled * (math.log2(math.e) / math.sqrt(256 // HEADS)))
    high, low = split(scaled)
    row = lax.broadcasted_iota(jnp.int32, (256, 16), 1)
    mask = jnp.where(row == 0, 1.0, 0.0).astype(BF16)
    for h in range(HEADS):
        part = slice(32 * h, 32 * h + 32)
        query3_ref[h] = jnp.concatenate([high[:, part], high[:, part], low[:, part], mask], axis=1)
    lane = lax.broadcasted_iota(jnp.int32, (16, 1280), 1)
    edge = jnp.logical_or(lane % 128 == 0, lane % 128 == 127)
    store_keys(
        normed, jnp.logical_and(edge, lane >= 256), 0, qkv_high_ref, qkv_low_ref, key3, value3
    )
    found = attend(lambda h: query3_ref[h], key3, value3, None)
    for h, (largest, sums) in enumerate(found):
        state_ref[h] = jnp.concatenate([sums, jnp.broadcast_to(largest, (256, 48))], axis=1)


def finish(rows, key3, value3, out2_ref, up2_ref, down2_ref, hidden_ref, query3_ref, state_ref):
    found = attend(
        lambda h: query3_ref[h, rows, :], key3, value3, lambda h: state_ref[h, rows, 80:81]
    )
    attended = []
    for h, (largest, sums) in enumerate(found):
        before = state_ref[h, rows, :]
        sums = sums + before[:, 0:80] * jnp.exp2(before[:, 80:81] - largest)
        attended.append((sums[:, 0:32] + sums[:, 32:64]) / sums[:, 64:65])
    attended = split(jnp.concatenate(attended, axis=1))
    mixed = hidden_ref[rows, :] + dot3(attended, (out2_ref[0], out2_ref[1]))
    normed = split(layer_norm(mixed, 1))
    activated = split(jax.nn.gelu(dot3(normed, (up2_ref[0], up2_ref[1]))))
    return mixed + dot3(activated, (down2_ref[0], down2_ref[1]))


def own_kernel(*refs):
    refs[8][...] = finish(slice(0, 128), *refs[:8])


def late_kernel(cos_ref, *refs):
    pieces = refs[:3]
    embed3_ref, qkv_high_ref, qkv_low_ref, out2_ref, up2_ref, down2_ref = refs[3:9]
    hidden_ref, query3_ref, state_ref, columns_ref, edges_ref = refs[9:14]
    send_ref, key3, value3 = refs[14:17]
    edges, fixes = refs[17:]
    position = lax.axis_index("lon")
    y = position // 8
    z = position % 8
    inverse = 1.0 / cos_ref[0]
    step = 0.5 * STEP_SIZE * inverse * inverse
    total = columns_ref[...]
    for k in range(8):
        for index in range(2):
            half = y if index == 0 else 1 - y
            if k < 5:
                here = edges_ref[2 * k + index]
            else:
                here = pieces[k - 5][index, 78:80, :]
                total = place_edges(total, pieces[k - 5][index], 2 * k + index)
            edges[half * 8 + jnp.bitwise_xor(z, k)] = here
    fixes[...] = jnp.zeros_like(fixes)
    for k in range(8):
        for index in range(2):
            half = y if index == 0 else 1 - y
            sector = half * 8 + jnp.bitwise_xor(z, k)
            here = edges[sector]
            west = edges[(sector + 15) % 16]
            east = edges[(sector + 1) % 16]
            slot = 2 * (2 * k + index)
            fixes[slot : slot + 1, :] = face_fix(step, here[0:1], west[1:2])
            fixes[slot + 1 : slot + 2, :] = face_fix(step, here[1:2], east[0:1])
    total = total + jnp.transpose(fixes[...])[:ROWS]
    parts = [pieces[k][index] for k in range(3) for index in range(2)] + [total]
    hidden, normed = embed_tokens(jnp.concatenate(parts, axis=1), embed3_ref)
    lane = lax.broadcasted_iota(jnp.int32, (16, 896), 1)
    edge = jnp.logical_or(lane % 128 == 0, lane % 128 == 127)
    unused = jnp.logical_or(lane < 768 + 4, lane >= 768 + 32)
    masked = jnp.where(lane < 768, edge.astype(jnp.int32), unused.astype(jnp.int32)) == 1
    store_keys(normed, masked, 0, qkv_high_ref, qkv_low_ref, key3, value3)
    send_ref[...] = finish(
        slice(128, 256), key3, value3, out2_ref, up2_ref, down2_ref, hidden_ref, query3_ref, state_ref
    )


def shape(*dims, dtype=F32):
    return jax.ShapeDtypeStruct(dims, dtype)


def call(kernel, outs, operands, spaces, scratch=(), limit=None, flops=0, moved=0):
    kinds = {"s": SMEM, "v": VMEM, "h": pl.BlockSpec(memory_space=pltpu.HBM)}
    return pl.pallas_call(
        kernel,
        out_shape=outs,
        in_specs=[kinds[letter] for letter in spaces],
        out_specs=jax.tree.map(lambda _: VMEM, outs),
        scratch_shapes=scratch,
        compiler_params=pltpu.CompilerParams(vmem_limit_bytes=limit),
        cost_estimate=pl.CostEstimate(flops=flops, bytes_accessed=moved, transcendentals=0),
    )(*operands)


def pairs_over(axis_sizes, move):
    lats, lons = axis_sizes
    found = []
    for lat in range(lats):
        for lon in range(lons):
            target = move(lat, lon)
            if 0 <= target[0] < lats:
                found.append((lat * lons + lon, target[0] * lons + target[1]))
    return found


def swap_lon(values, mask):
    count = lax.axis_size("lon")
    return lax.ppermute(values, "lon", [(r, r ^ mask) for r in range(count)])


def on_device(
    fields, diffusivity, w_embed, query_weight, key_weight, value_weight, out_weight, up_weight, down_weight,
):
    sizes = (lax.axis_size("lat"), lax.axis_size("lon"))
    lat = lax.axis_index("lat")
    y = lax.axis_index("lon") // 8
    row = (2 * lat + y).astype(F32)
    faces = jnp.stack([row + 0.5, (2 * lat + 1).astype(F32), (2 * (lat + y)).astype(F32)])
    half = 0.5 * 2 * sizes[0]
    cosines = jnp.cos((CENTER_LAT + (faces - half) * SPACING) * (math.pi / 180.0))

    plane = shape(ROWS, 128)
    pair = shape(2, ROWS, 128)
    both, mine, other = call(
        pack_kernel, (pair, plane, plane), (fields, diffusivity), "vv", limit=4 * 2**20, moved=400000
    )
    outward = pairs_over(sizes, lambda a, b: (a + 1 if b < 8 else a - 1, b))
    crossing = pairs_over(sizes, lambda a, b: (a - 1 if b < 8 else a + 1, b ^ 8))
    outer = lax.ppermute(other, ("lat", "lon"), outward)
    partner_outer = lax.ppermute(mine, ("lat", "lon"), crossing)
    partner = swap_lon(both, 8)
    first = call(
        first_weights_kernel,
        (shape(256, 3 * ROWS, dtype=BF16), shape(768, 256, dtype=BF16), shape(768, 256, dtype=BF16)),
        (w_embed, query_weight, key_weight, value_weight, both),
        "vvvvh",
        limit=8 * 2**20,
        moved=2000000,
    )
    chunk, edges = call(
        stencil_kernel,
        (pair, shape(2, 2, 128)),
        (cosines, both, outer, partner, partner_outer, first[0]),
        "svvvvh",
        limit=4 * 2**20,
        moved=400000,
    )
    turn = [(r, (r & 8) | ((r % 8 + (1 if r % 2 else 7)) % 8)) for r in range(sizes[1])]
    across = lax.ppermute(edges, "lon", turn)
    far = swap_lon(chunk, 4)
    near = [swap_lon(chunk, k) for k in (1, 2, 3)]
    far_near = [swap_lon(far, k) for k in (1, 2, 3)]
    *last, order = call(
        last_weights_kernel,
        (
            shape(2, 256, 256, dtype=BF16),
            shape(2, 256, 1024, dtype=BF16),
            shape(2, 1024, 256, dtype=BF16),
            shape(8, 128),
        ),
        (out_weight, up_weight, down_weight, edges),
        "vvvh",
        limit=12 * 2**20,
        moved=5000000,
    )
    early = call(
        early_kernel,
        (
            shape(256, 256),
            shape(HEADS, 256, 112, dtype=BF16),
            shape(HEADS, 256, 128),
            plane,
            shape(16, 2, 128),
        ),
        (cosines, chunk, *near, far, across, *first, order),
        "s" + 9 * "v" + "h",
        scratch=[pltpu.VMEM((HEADS, 112, 1280), BF16), pltpu.VMEM((HEADS, 80, 1280), BF16)],
        limit=40 * 2**20,
        flops=5 * 10**9,
        moved=3000000,
    )
    tile = shape(128, 256)
    send, *keys = call(
        late_kernel,
        (tile, shape(HEADS, 112, 896, dtype=BF16), shape(HEADS, 80, 896, dtype=BF16)),
        (cosines, *far_near, *first, *last, *early),
        "s" + 14 * "v",
        scratch=[pltpu.VMEM((16, 2, 128), F32), pltpu.VMEM((128, 128), F32)],
        limit=36 * 2**20,
        flops=5 * 10**9,
        moved=6000000,
    )
    own = call(
        own_kernel,
        tile,
        (*keys, *last, *early[:3]),
        8 * "v",
        limit=36 * 2**20,
        flops=3 * 10**9,
        moved=6000000,
    )
    received = swap_lon(send, 8)
    first = jnp.where(y == 0, own, received)
    second = jnp.where(y == 0, received, own)
    return jnp.stack([first, second])


def solution(mesh):
    placed = (P(None, "lat", "lon"), P("lat", "lon"), P(), P(), P(), P(), P(), P(), P())
    return jax.shard_map(
        on_device, mesh=mesh, in_specs=placed, out_specs=P("lat", "lon", None), check_vma=False
    )
```

time: 68.6 us -> 60.2 us (0.88)
  waiting for transfers between devices: 11.3 us -> 2.16 us
  starting transfers between devices: 29.3 us -> 30.4 us
  local copies, waits for them, and re-layouts: 6.55 us -> 7.56 us
  Pallas kernels: 19.6 us -> 18.6 us
    ppermute x9, waiting for transfers between devices: 11.1 us -> 1.9 us  [swap_lon(): return lax.ppermute(values, 'lon', [(r, r ^ mask) for r in range(count)])]
    unnamed x24 -> x18, local copies, waits for them, and re-layouts: 6.55 us -> 7.56 us
    pallas_call x4 -> x7, Pallas kernels: 19.6 us -> 18.6 us  [call(): pl.pallas_call(kernel, out_shape=outs, in_specs=[kinds[letter] for letter...]
    ppermute x9, starting transfers between devices: 22.1 us -> 23.1 us  [swap_lon(): return lax.ppermute(values, 'lon', [(r, r ^ mask) for r in range(count)])]
  transfers between devices with their start and end apart: 11 -> 12, of which waited for: 4 -> 3; matrix products, arithmetic and copies ran while one was open for 1% -> 0% of each run, Pallas kernels for 1% -> 20%
where the time goes in v2:
time: 60.2 us; the launch traced here: 59.7 us
  starting transfers between devices  30.4 us (50%)
  Pallas kernels  18.6 us (31%)
  local copies, waits for them, and re-layouts  7.56 us (13%)
  waiting for transfers between devices  2.16 us (4%)
  other arithmetic  0.86 us (1%)
    ppermute x9, starting transfers between devices, swap_lon(): return lax.ppermute(values, 'lon', [(r, r ^ mask) for r in range(count)])  23.1 us
    pallas_call x7, Pallas kernels, call(): pl.pallas_call(kernel, out_shape=outs, in_specs=[kinds[letter] for letter...  18.6 us
    unnamed x18, local copies, waits for them, and re-layouts  7.56 us
    ppermute x1, starting transfers between devices, on_device(): partner_outer = lax.ppermute(mine, ('lat', 'lon'), crossing)  5.29 us
    ppermute x1, starting transfers between devices, on_device(): outer = lax.ppermute(other, ('lat', 'lon'), outward)  1.92 us
    ppermute x9, waiting for transfers between devices, swap_lon(): return lax.ppermute(values, 'lon', [(r, r ^ mask) for r in range(count)])  1.9 us
  transfers between devices with their start and end apart: 12, of which 3 were waited for; matrix products, arithmetic and copies ran while one was open for 0% of the time, Pallas kernels for 20%

profile of v2, /device:TPU:6, one launch (start us, length us, event | category | flops | bytes accessed | tf_op | source)
XLA Modules:
  0.0 59.7 jit_solution(18025128419393221062)
XLA Ops:
  0.0 1.0 %copy-done.7 = f32[78,2,128]{2,1,0:T(2,128)S(1)} copy-done((f32[78,2,128]{2,1,0:T(2,128)S(1)}, f32[78,2,128]{2,1,0:T(2,128)}, u32[]{:S(2)}) %copy-start.7) | copy-done | bytes 79896
  1.0 0.7 %copy-done.8 = f32[2,128]{1,0:T(2,128)S(1)} copy-done((f32[2,128]{1,0:T(2,128)S(1)}, f32[2,128]{1,0:T(2,128)}, u32[]{:S(2)}) %copy-start.8) | copy-done | bytes 1048
  1.7 1.9 %collective-permute-start = (f32[80,128]{1,0:T(8,128)S(1)}, f32[80,128]{1,0:T(8,128)S(1)}, u32[]{:S(2)}, u32[]{:S(2)}) collective-permute-start(f32[80,128]{1,0:T(8,128)S(1)} %get-tuple-element.26), channel_id=1, source_target_pairs={{0,16},{1,17},{2,18},{3,19},{4,20},{5,21},{6,22},{7,23},{16,32},{1... | collective-permute-start | bytes 122888 | tf_op jit(solution)/shard_map/ppermute | solution.py:335
  3.6 5.3 %collective-permute-start.2 = (f32[80,128]{1,0:T(8,128)S(1)}, f32[80,128]{1,0:T(8,128)S(1)}, u32[]{:S(2)}, u32[]{:S(2)}) collective-permute-start(f32[80,128]{1,0:T(8,128)S(1)} %get-tuple-element.27), channel_id=1, source_target_pairs={{8,16},{9,17},{10,18},{11,19},{12,20},{13,21},{14,22},{15,23},{16,... | collective-permute-start | bytes 122888 | tf_op jit(solution)/shard_map/ppermute | solution.py:336
  8.9 1.5 %collective-permute-start.1 = (f32[2,80,128]{2,1,0:T(8,128)S(1)}, f32[2,80,128]{2,1,0:T(8,128)S(1)}, u32[]{:S(2)}, u32[]{:S(2)}) collective-permute-start(f32[2,80,128]{2,1,0:T(8,128)S(1)} %get-tuple-element.25.refs_4_.both_ref), channel_id=1, source_target_pairs={{0,8},{1,9},{2,10},{3,11},{4,12},{5,13},{6,14},{7,15},{8,0},{9,1},... | collective-permute-start | bytes 245768 | tf_op jit(solution)/shard_map/ppermute | solution.py:314
  10.6 0.9 %copy-done.2 = f32[256,256]{1,0:T(8,128)S(1)} copy-done((f32[256,256]{1,0:T(8,128)S(1)}, f32[256,256]{1,0:T(8,128)}, u32[]{:S(2)}) %copy-start.2) | copy-done | bytes 262168
  11.5 0.9 %copy-done.3 = f32[256,256]{1,0:T(8,128)S(1)} copy-done((f32[256,256]{1,0:T(8,128)S(1)}, f32[256,256]{1,0:T(8,128)}, u32[]{:S(2)}) %copy-start.3) | copy-done | bytes 262168
  12.5 0.9 %copy-done.4 = f32[256,256]{1,0:T(8,128)S(1)} copy-done((f32[256,256]{1,0:T(8,128)S(1)}, f32[256,256]{1,0:T(8,128)}, u32[]{:S(2)}) %copy-start.4) | copy-done | bytes 262168
  13.4 0.9 %copy-done.6 = f32[78,256]{1,0:T(8,128)S(1)} copy-done((f32[78,256]{1,0:T(8,128)S(1)}, f32[78,256]{1,0:T(8,128)}, u32[]{:S(2)}) %copy-start.6) | copy-done | bytes 79896
  14.7 1.0 %collective-permute-done.1.partner_ref = f32[2,80,128]{2,1,0:T(8,128)S(1)} collective-permute-done((f32[2,80,128]{2,1,0:T(8,128)S(1)}, f32[2,80,128]{2,1,0:T(8,128)S(1)}, u32[]{:S(2)}, u32[]{:S(2)}) %collective-permute-start.1) | collective-permute-done | bytes 81952 | tf_op jit(solution)/shard_map/ppermute | solution.py:314
  15.8 0.7 %shard_map.93 = (f32[2,80,128]{2,1,0:T(8,128)S(1)}, f32[2,2,128]{2,1,0:T(2,128)S(1)}) custom-call(f32[3]{0:T(128)S(1)} %multiply_cosine_fusion.cos_ref, f32[2,80,128]{2,1,0:T(8,128)S(1)} %get-tuple-element.25.refs_4_.both_ref, f32[80,128]{1,0:T(8,128)S(1)} %collective-permute-done.outer_ref, f32[2,80,128]{2,1,0:T(8,128)S(1)} %collective-permute-done.1.partner_ref, ...), custom_call_target="tpu_custom_call" | custom-call | bytes 400000 | tf_op jit(solution)/shard_map/pallas_call | solution.py:290
  16.5 7.3 %collective-permute-start.3 = (f32[2,80,128]{2,1,0:T(8,128)S(1)}, f32[2,80,128]{2,1,0:T(8,128)S(1)}, u32[]{:S(2)}, u32[]{:S(2)}) collective-permute-start(f32[2,80,128]{2,1,0:T(8,128)S(1)} %get-tuple-element.29.refs_0_), channel_id=1, source_target_pairs={{0,4},{1,5},{2,6},{3,7},{4,0},{5,1},{6,2},{7,3},{8,12},{9,13},{10,... | collective-permute-start | bytes 245768 | tf_op jit(solution)/shard_map/ppermute | solution.py:314
  23.8 1.9 %collective-permute-start.9 = (f32[2,80,128]{2,1,0:T(8,128)S(1)}, f32[2,80,128]{2,1,0:T(8,128)S(1)}, u32[]{:S(2)}, u32[]{:S(2)}) collective-permute-start(f32[2,80,128]{2,1,0:T(8,128)S(1)} %get-tuple-element.29.refs_0_), channel_id=1, source_target_pairs={{0,3},{1,2},{2,1},{3,0},{4,7},{5,6},{6,5},{7,4},{8,11},{9,10},{10,... | collective-permute-start | bytes 245768 | tf_op jit(solution)/shard_map/ppermute | solution.py:314
  26.3 1.9 %collective-permute-start.7 = (f32[2,80,128]{2,1,0:T(8,128)S(1)}, f32[2,80,128]{2,1,0:T(8,128)S(1)}, u32[]{:S(2)}, u32[]{:S(2)}) collective-permute-start(f32[2,80,128]{2,1,0:T(8,128)S(1)} %get-tuple-element.29.refs_0_), channel_id=1, source_target_pairs={{0,1},{1,0},{2,3},{3,2},{4,5},{5,4},{6,7},{7,6},{8,9},{9,8},{10,11... | collective-permute-start | bytes 245768 | tf_op jit(solution)/shard_map/ppermute | solution.py:314
  28.3 1.2 %copy-done.1 = f32[1024,256]{1,0:T(8,128)S(1)} copy-done((f32[1024,256]{1,0:T(8,128)S(1)}, f32[1024,256]{1,0:T(8,128)}, u32[]{:S(2)}) %copy-start.1) | copy-done | bytes 1048600
  29.5 0.9 %copy-done.5 = f32[256,256]{1,0:T(8,128)S(1)} copy-done((f32[256,256]{1,0:T(8,128)S(1)}, f32[256,256]{1,0:T(8,128)}, u32[]{:S(2)}) %copy-start.5) | copy-done | bytes 262168
  30.8 1.9 %collective-permute-start.6 = (f32[2,80,128]{2,1,0:T(8,128)S(1)}, f32[2,80,128]{2,1,0:T(8,128)S(1)}, u32[]{:S(2)}, u32[]{:S(2)}) collective-permute-start(f32[2,80,128]{2,1,0:T(8,128)S(1)} %collective-permute-done.3.refs_4_), channel_id=1, source_target_pairs={{0,3},{1,2},{2,1},{3,0},{4,7},{5,6},{6,5},{7,4},{8,11},{9,10},{10,... | collective-permute-start | bytes 245768 | tf_op jit(solution)/shard_map/ppermute | solution.py:314
  33.0 6.0 %collective-permute-start.5 = (f32[2,80,128]{2,1,0:T(8,128)S(1)}, f32[2,80,128]{2,1,0:T(8,128)S(1)}, u32[]{:S(2)}, u32[]{:S(2)}) collective-permute-start(f32[2,80,128]{2,1,0:T(8,128)S(1)} %collective-permute-done.3.refs_4_), channel_id=1, source_target_pairs={{0,2},{1,3},{2,0},{3,1},{4,6},{5,7},{6,4},{7,5},{8,10},{9,11},{10,... | collective-permute-start | bytes 245768 | tf_op jit(solution)/shard_map/ppermute | solution.py:314
  39.1 7.2 %shard_map.95 = (f32[256,256]{1,0:T(8,128)S(1)}, bf16[8,256,112]{2,1,0:T(8,128)(2,1)S(1)}, f32[8,256,128]{2,1,0:T(8,128)S(1)}, f32[80,128]{1,0:T(8,128)S(1)}, f32[16,2,128]{2,1,0:T(2,128)S(1)}) custom-call(f32[3]{0:T(128)S(1)} %multiply_cosine_fusion.cos_ref, f32[2,80,128]{2,1,0:T(8,128)S(1)} %get-tuple-element.29.refs_0_, ...), custom_call_target="tpu_custom_call" | custom-call | flops 5000000000 | bytes 3000000 | tf_op jit(solution)/shard_map/pallas_call | solution.py:290
  46.3 5.9 %shard_map.96 = (f32[128,256]{1,0:T(8,128)S(1)}, bf16[8,112,896]{2,1,0:T(8,128)(2,1)S(1)}, bf16[8,80,896]{2,1,0:T(8,128)(2,1)S(1)}) custom-call(f32[3]{0:T(128)S(1)} %multiply_cosine_fusion.cos_ref, f32[2,80,128]{2,1,0:T(8,128)S(1)} %collective-permute-done.4.refs_0_, f32[2,80,128]{2,1,0:T(8,128)S(1)} %collective-permute-done.5.refs_1_, ...), custom_call_target="tpu_custom_call" | custom-call | flops 5000000000 | bytes 6000000 | tf_op jit(solution)/shard_map/pallas_call | solution.py:290
  52.2 1.9 %collective-permute-start.11 = (f32[128,256]{1,0:T(8,128)S(1)}, f32[128,256]{1,0:T(8,128)S(1)}, u32[]{:S(2)}, u32[]{:S(2)}) collective-permute-start(f32[128,256]{1,0:T(8,128)S(1)} %get-tuple-element.44), channel_id=1, source_target_pairs={{0,8},{1,9},{2,10},{3,11},{4,12},{5,13},{6,14},{7,15},{8,0},{9,1},... | collective-permute-start | bytes 393224 | tf_op jit(solution)/shard_map/ppermute | solution.py:314
  54.1 4.0 %shard_map.97 = f32[128,256]{1,0:T(8,128)S(1)} custom-call(bf16[8,112,896]{2,1,0:T(8,128)(2,1)S(1)} %get-tuple-element.42.refs_0_, bf16[8,80,896]{2,1,0:T(8,128)(2,1)S(1)} %get-tuple-element.43.refs_1_, bf16[2,256,256]{2,1,0:T(8,128)(2,1)S(1)} %get-tuple-element.33.refs_6_.refs_2_, bf16[2,256,1024]{2,1,0:T(8,128)(2,1)S(1)} %get-tuple-element.34.refs_7_.refs_3_, ...), custom_call_target="tpu_custom_call" | custom-call | flops 3000000000 | bytes 6000000 | tf_op jit(solution)/shard_map/pallas_call | solution.py:290
  58.1 0.8 %collective-permute-done.11 = f32[128,256]{1,0:T(8,128)S(1)} collective-permute-done((f32[128,256]{1,0:T(8,128)S(1)}, f32[128,256]{1,0:T(8,128)S(1)}, u32[]{:S(2)}, u32[]{:S(2)}) %collective-permute-start.11) | collective-permute-done | bytes 131104 | tf_op jit(solution)/shard_map/ppermute | solution.py:314
  59.0 0.7 %pad_maximum_fusion = f32[2,128,256]{2,1,0:T(8,128)} fusion(f32[1,128,256]{2,1,0:T(8,128)S(1)} %get-tuple-element.46, f32[1,128,256]{2,1,0:T(8,128)S(1)} %get-tuple-element.45), kind=kLoop, calls=%fused_computation | loop fusion | flops 65536 | bytes 524288 | tf_op jit(solution)/shard_map/stack | solution.py:411
  (28 shorter events, 1.9 us)
Async XLA Ops:
  0.0 28.3 %copy-start = (f32[256,1024]{1,0:T(8,128)S(1)}, f32[256,1024]{1,0:T(8,128)}, u32[]{:S(2)}) copy-start(f32[256,1024]{1,0:T(8,128)} %refs_1_.3) | copy-start | bytes 3145732
  0.0 1.0 %copy-start.7 = (f32[78,2,128]{2,1,0:T(2,128)S(1)}, f32[78,2,128]{2,1,0:T(2,128)}, u32[]{:S(2)}) copy-start(f32[78,2,128]{2,1,0:T(2,128)} %fields_ref.1) | copy-start | bytes 239620
  1.0 0.7 %copy-start.8 = (f32[2,128]{1,0:T(2,128)S(1)}, f32[2,128]{1,0:T(2,128)}, u32[]{:S(2)}) copy-start(f32[2,128]{1,0:T(2,128)} %kappa_ref.1) | copy-start | bytes 3076
  1.7 13.0 %collective-permute-start = (f32[80,128]{1,0:T(8,128)S(1)}, f32[80,128]{1,0:T(8,128)S(1)}, u32[]{:S(2)}, u32[]{:S(2)}) collective-permute-start(f32[80,128]{1,0:T(8,128)S(1)} %get-tuple-element.26), channel_id=1, source_target_pairs={{0,16},{1,17},{2,18},{3,19},{4,20},{5,21},{6,22},{7,23},{16,32},{1... | collective-permute-start | bytes 122888 | tf_op jit(solution)/shard_map/ppermute | solution.py:335
  3.6 11.1 %collective-permute-start.2 = (f32[80,128]{1,0:T(8,128)S(1)}, f32[80,128]{1,0:T(8,128)S(1)}, u32[]{:S(2)}, u32[]{:S(2)}) collective-permute-start(f32[80,128]{1,0:T(8,128)S(1)} %get-tuple-element.27), channel_id=1, source_target_pairs={{8,16},{9,17},{10,18},{11,19},{12,20},{13,21},{14,22},{15,23},{16,... | collective-permute-start | bytes 122888 | tf_op jit(solution)/shard_map/ppermute | solution.py:336
  8.9 6.8 %collective-permute-start.1 = (f32[2,80,128]{2,1,0:T(8,128)S(1)}, f32[2,80,128]{2,1,0:T(8,128)S(1)}, u32[]{:S(2)}, u32[]{:S(2)}) collective-permute-start(f32[2,80,128]{2,1,0:T(8,128)S(1)} %get-tuple-element.25.refs_4_.both_ref), channel_id=1, source_target_pairs={{0,8},{1,9},{2,10},{3,11},{4,12},{5,13},{6,14},{7,15},{8,0},{9,1},... | collective-permute-start | bytes 245768 | tf_op jit(solution)/shard_map/ppermute | solution.py:314
  10.6 1.0 %copy-start.2 = (f32[256,256]{1,0:T(8,128)S(1)}, f32[256,256]{1,0:T(8,128)}, u32[]{:S(2)}) copy-start(f32[256,256]{1,0:T(8,128)} %refs_1_.2) | copy-start | bytes 786436
  11.5 0.9 %copy-start.3 = (f32[256,256]{1,0:T(8,128)S(1)}, f32[256,256]{1,0:T(8,128)}, u32[]{:S(2)}) copy-start(f32[256,256]{1,0:T(8,128)} %refs_2_.2) | copy-start | bytes 786436
  12.5 0.9 %copy-start.4 = (f32[256,256]{1,0:T(8,128)S(1)}, f32[256,256]{1,0:T(8,128)}, u32[]{:S(2)}) copy-start(f32[256,256]{1,0:T(8,128)} %refs_3_.1) | copy-start | bytes 786436
  13.4 0.9 %copy-start.6 = (f32[78,256]{1,0:T(8,128)S(1)}, f32[78,256]{1,0:T(8,128)}, u32[]{:S(2)}) copy-start(f32[78,256]{1,0:T(8,128)} %refs_0_.2) | copy-start | bytes 239620
  16.5 14.3 %collective-permute-start.3 = (f32[2,80,128]{2,1,0:T(8,128)S(1)}, f32[2,80,128]{2,1,0:T(8,128)S(1)}, u32[]{:S(2)}, u32[]{:S(2)}) collective-permute-start(f32[2,80,128]{2,1,0:T(8,128)S(1)} %get-tuple-element.29.refs_0_), channel_id=1, source_target_pairs={{0,4},{1,5},{2,6},{3,7},{4,0},{5,1},{6,2},{7,3},{8,12},{9,13},{10,... | collective-permute-start | bytes 245768 | tf_op jit(solution)/shard_map/ppermute | solution.py:314
  23.8 15.2 %collective-permute-start.9 = (f32[2,80,128]{2,1,0:T(8,128)S(1)}, f32[2,80,128]{2,1,0:T(8,128)S(1)}, u32[]{:S(2)}, u32[]{:S(2)}) collective-permute-start(f32[2,80,128]{2,1,0:T(8,128)S(1)} %get-tuple-element.29.refs_0_), channel_id=1, source_target_pairs={{0,3},{1,2},{2,1},{3,0},{4,7},{5,6},{6,5},{7,4},{8,11},{9,10},{10,... | collective-permute-start | bytes 245768 | tf_op jit(solution)/shard_map/ppermute | solution.py:314
  25.7 13.3 %collective-permute-start.8 = (f32[2,80,128]{2,1,0:T(8,128)S(1)}, f32[2,80,128]{2,1,0:T(8,128)S(1)}, u32[]{:S(2)}, u32[]{:S(2)}) collective-permute-start(f32[2,80,128]{2,1,0:T(8,128)S(1)} %get-tuple-element.29.refs_0_), channel_id=1, source_target_pairs={{0,2},{1,3},{2,0},{3,1},{4,6},{5,7},{6,4},{7,5},{8,10},{9,11},{10,... | collective-permute-start | bytes 245768 | tf_op jit(solution)/shard_map/ppermute | solution.py:314
  26.3 12.8 %collective-permute-start.7 = (f32[2,80,128]{2,1,0:T(8,128)S(1)}, f32[2,80,128]{2,1,0:T(8,128)S(1)}, u32[]{:S(2)}, u32[]{:S(2)}) collective-permute-start(f32[2,80,128]{2,1,0:T(8,128)S(1)} %get-tuple-element.29.refs_0_), channel_id=1, source_target_pairs={{0,1},{1,0},{2,3},{3,2},{4,5},{5,4},{6,7},{7,6},{8,9},{9,8},{10,11... | collective-permute-start | bytes 245768 | tf_op jit(solution)/shard_map/ppermute | solution.py:314
  28.2 4.8 %collective-permute-start.10 = (f32[2,2,128]{2,1,0:T(2,128)S(1)}, f32[2,2,128]{2,1,0:T(2,128)S(1)}, u32[]{:S(2)}, u32[]{:S(2)}) collective-permute-start(f32[2,2,128]{2,1,0:T(2,128)S(1)} %get-tuple-element.32.refs_3_), channel_id=1, source_target_pairs={{0,7},{1,2},{2,1},{3,4},{4,3},{5,6},{6,5},{7,0},{8,15},{9,10},{10,... | collective-permute-start | bytes 6152 | tf_op jit(solution)/shard_map/ppermute | solution.py:355
  28.3 1.2 %copy-start.1 = (f32[1024,256]{1,0:T(8,128)S(1)}, f32[1024,256]{1,0:T(8,128)}, u32[]{:S(2)}) copy-start(f32[1024,256]{1,0:T(8,128)} %refs_2_.3) | copy-start | bytes 3145732
  29.5 0.9 %copy-start.5 = (f32[256,256]{1,0:T(8,128)S(1)}, f32[256,256]{1,0:T(8,128)}, u32[]{:S(2)}) copy-start(f32[256,256]{1,0:T(8,128)} %refs_0_.3) | copy-start | bytes 786436
  30.8 15.4 %collective-permute-start.6 = (f32[2,80,128]{2,1,0:T(8,128)S(1)}, f32[2,80,128]{2,1,0:T(8,128)S(1)}, u32[]{:S(2)}, u32[]{:S(2)}) collective-permute-start(f32[2,80,128]{2,1,0:T(8,128)S(1)} %collective-permute-done.3.refs_4_), channel_id=1, source_target_pairs={{0,3},{1,2},{2,1},{3,0},{4,7},{5,6},{6,5},{7,4},{8,11},{9,10},{10,... | collective-permute-start | bytes 245768 | tf_op jit(solution)/shard_map/ppermute | solution.py:314
  33.0 13.2 %collective-permute-start.5 = (f32[2,80,128]{2,1,0:T(8,128)S(1)}, f32[2,80,128]{2,1,0:T(8,128)S(1)}, u32[]{:S(2)}, u32[]{:S(2)}) collective-permute-start(f32[2,80,128]{2,1,0:T(8,128)S(1)} %collective-permute-done.3.refs_4_), channel_id=1, source_target_pairs={{0,2},{1,3},{2,0},{3,1},{4,6},{5,7},{6,4},{7,5},{8,10},{9,11},{10,... | collective-permute-start | bytes 245768 | tf_op jit(solution)/shard_map/ppermute | solution.py:314
  39.0 7.2 %collective-permute-start.4 = (f32[2,80,128]{2,1,0:T(8,128)S(1)}, f32[2,80,128]{2,1,0:T(8,128)S(1)}, u32[]{:S(2)}, u32[]{:S(2)}) collective-permute-start(f32[2,80,128]{2,1,0:T(8,128)S(1)} %collective-permute-done.3.refs_4_), channel_id=1, source_target_pairs={{0,1},{1,0},{2,3},{3,2},{4,5},{5,4},{6,7},{7,6},{8,9},{9,8},{10,11... | collective-permute-start | bytes 245768 | tf_op jit(solution)/shard_map/ppermute | solution.py:314
  52.2 6.8 %collective-permute-start.11 = (f32[128,256]{1,0:T(8,128)S(1)}, f32[128,256]{1,0:T(8,128)S(1)}, u32[]{:S(2)}, u32[]{:S(2)}) collective-permute-start(f32[128,256]{1,0:T(8,128)S(1)} %get-tuple-element.44), channel_id=1, source_target_pairs={{0,8},{1,9},{2,10},{3,11},{4,12},{5,13},{6,14},{7,15},{8,0},{9,1},... | collective-permute-start | bytes 393224 | tf_op jit(solution)/shard_map/ppermute | solution.py:314

commit v3 on v2

--- a/solution.py
+++ b/solution.py
@@ -13,6 +13,7 @@
 CENTER_LAT = 45.0
 SPACING = 0.25
 EPSILON = 1e-05
+PARTNERS = (0, 1, 2, 3, 7, 6, 5, 4)
 ROWS = 80
 F32 = jnp.float32
 BF16 = jnp.bfloat16
@@ -33,7 +34,7 @@
     return dot(left[0], right[0]) + dot(left[1], right[0]) + dot(left[0], right[1])
 
 
-def pack_kernel(fields_ref, kappa_ref, both_ref, mine_ref, other_ref):
+def pack_kernel(fields_ref, kappa_ref, both_ref):
     y = lax.axis_index("lon") // 8
     channels = fields_ref.shape[0]
     zero = jnp.zeros((1, 128), F32)
@@ -47,12 +48,10 @@
     other = jnp.where(flag, rows[1], rows[0])
     both_ref[0] = mine
     both_ref[1] = other
-    mine_ref[...] = mine
-    other_ref[...] = other
 
 
 def stencil_kernel(
-    cos_ref, both_ref, outer_ref, partner_ref, partner_outer_ref, order_ref, chunk_ref, edges_ref
+    cos_ref, both_ref, outer_ref, partner_ref, partner_outer_ref, order_ref, chunk_ref
 ):
     inverse = 1.0 / cos_ref[0]
     face_inner = cos_ref[1]
@@ -76,8 +75,6 @@
         chunk_ref[index] = updated
         chunk_ref[index, 78:79, :] = turned[0:1]
         chunk_ref[index, 79:80, :] = turned[127:128]
-        edges_ref[index, 0:1, :] = turned[0:1]
-        edges_ref[index, 1:2, :] = turned[127:128]
 
 
 def first_weights_kernel(*refs):
@@ -161,9 +158,9 @@
 
 def early_kernel(cos_ref, *refs):
     pieces = refs[:5]
-    across_ref, embed3_ref, qkv_high_ref, qkv_low_ref = refs[5:9]
-    hidden_ref, query3_ref, state_ref, columns_ref, edges_ref = refs[10:15]
-    key3, value3 = refs[15:]
+    embed3_ref, qkv_high_ref, qkv_low_ref = refs[5:8]
+    hidden_ref, query3_ref, state_ref, columns_ref, edges_ref = refs[9:14]
+    key3, value3 = refs[14:]
     z = lax.axis_index("lon") % 8
     inverse = 1.0 / cos_ref[0]
     step = 0.5 * STEP_SIZE * inverse * inverse
@@ -173,15 +170,16 @@
             edges_ref[2 * k + index] = pieces[k][index, 78:80, :]
             total = place_edges(total, pieces[k][index], 2 * k + index)
     columns_ref[...] = total
-    even = z % 2 == 0
     wraps = jnp.logical_or(z == 0, z == 7).astype(jnp.int32)
     lane = lax.broadcasted_iota(jnp.int32, (ROWS, 128), 1)
     flag = (jnp.zeros((2, 128), jnp.int32) + z % 2) == 0
+    outer = (jnp.zeros((2, 128), jnp.int32) + ((z + 1) // 2) % 2) == 0
     fixes = []
     for index in range(2):
         here = pieces[0][index, 78:80, :]
         beside = pieces[1][index, 78:80, :]
-        across = across_ref[jnp.where(wraps == 1, 1 - index, index)]
+        wrapped = jnp.where(wraps == 1, 1 - index, index)
+        across = jnp.where(outer, pieces[4][wrapped, 78:80, :], pieces[3][index, 78:80, :])
         west = jnp.where(flag, across, beside)
         east = jnp.where(flag, beside, across)
         fixes.append(face_fix(step, here[0:1], west[1:2]))
@@ -256,12 +254,12 @@
             else:
                 here = pieces[k - 5][index, 78:80, :]
                 total = place_edges(total, pieces[k - 5][index], 2 * k + index)
-            edges[half * 8 + jnp.bitwise_xor(z, k)] = here
+            edges[half * 8 + jnp.bitwise_xor(z, PARTNERS[k])] = here
     fixes[...] = jnp.zeros_like(fixes)
     for k in range(8):
         for index in range(2):
             half = y if index == 0 else 1 - y
-            sector = half * 8 + jnp.bitwise_xor(z, k)
+            sector = half * 8 + jnp.bitwise_xor(z, PARTNERS[k])
             here = edges[sector]
             west = edges[(sector + 15) % 16]
             east = edges[(sector + 1) % 16]
@@ -327,14 +325,14 @@
 
     plane = shape(ROWS, 128)
     pair = shape(2, ROWS, 128)
-    both, mine, other = call(
-        pack_kernel, (pair, plane, plane), (fields, diffusivity), "vv", limit=4 * 2**20, moved=400000
+    both = call(
+        pack_kernel, pair, (fields, diffusivity), "vv", limit=4 * 2**20, moved=400000
     )
     outward = pairs_over(sizes, lambda a, b: (a + 1 if b < 8 else a - 1, b))
     crossing = pairs_over(sizes, lambda a, b: (a - 1 if b < 8 else a + 1, b ^ 8))
-    outer = lax.ppermute(other, ("lat", "lon"), outward)
-    partner_outer = lax.ppermute(mine, ("lat", "lon"), crossing)
     partner = swap_lon(both, 8)
+    outer = lax.ppermute(both[1], ("lat", "lon"), outward)
+    partner_outer = lax.ppermute(both[0], ("lat", "lon"), crossing)
     first = call(
         first_weights_kernel,
         (shape(256, 3 * ROWS, dtype=BF16), shape(768, 256, dtype=BF16), shape(768, 256, dtype=BF16)),
@@ -343,17 +341,15 @@
         limit=8 * 2**20,
         moved=2000000,
     )
-    chunk, edges = call(
+    chunk = call(
         stencil_kernel,
-        (pair, shape(2, 2, 128)),
+        pair,
         (cosines, both, outer, partner, partner_outer, first[0]),
         "svvvvh",
         limit=4 * 2**20,
         moved=400000,
     )
-    turn = [(r, (r & 8) | ((r % 8 + (1 if r % 2 else 7)) % 8)) for r in range(sizes[1])]
-    across = lax.ppermute(edges, "lon", turn)
-    far = swap_lon(chunk, 4)
+    far = swap_lon(chunk, 7)
     near = [swap_lon(chunk, k) for k in (1, 2, 3)]
     far_near = [swap_lon(far, k) for k in (1, 2, 3)]
     *last, order = call(
@@ -364,7 +360,7 @@
             shape(2, 1024, 256, dtype=BF16),
             shape(8, 128),
         ),
-        (out_weight, up_weight, down_weight, edges),
+        (out_weight, up_weight, down_weight, chunk),
         "vvvh",
         limit=12 * 2**20,
         moved=5000000,
@@ -378,8 +374,8 @@
             plane,
             shape(16, 2, 128),
         ),
-        (cosines, chunk, *near, far, across, *first, order),
-        "s" + 9 * "v" + "h",
+        (cosines, chunk, *near, far, *first, order),
+        "s" + 8 * "v" + "h",
         scratch=[pltpu.VMEM((HEADS, 112, 1280), BF16), pltpu.VMEM((HEADS, 80, 1280), BF16)],
         limit=40 * 2**20,
         flops=5 * 10**9,

time: 60.2 us -> 57.1 us (0.949)
  starting transfers between devices: 30.4 us -> 26.1 us
  waiting for transfers between devices: 2.16 us -> 4.33 us
  local copies, waits for them, and re-layouts: 7.56 us -> 6.62 us
    ppermute x3 -> x2, starting transfers between devices: 7.32 us -> 4.3 us  [the longest x1 2.38 us: on_device(): partner_outer = lax.ppermute(both[0], ('lat', 'lon'), crossing)]
    ppermute x9, waiting for transfers between devices: 1.9 us -> 4.33 us  [swap_lon(): return lax.ppermute(values, 'lon', [(r, r ^ mask) for r in range(count)])]
    ppermute x9, starting transfers between devices: 23.1 us -> 21.8 us  [swap_lon(): return lax.ppermute(values, 'lon', [(r, r ^ mask) for r in range(count)])]
    unnamed x18, local copies, waits for them, and re-layouts: 7.56 us -> 6.62 us
  transfers between devices with their start and end apart: 12 -> 11, of which waited for: 3 -> 1; matrix products, arithmetic and copies ran while one was open for 0% -> 0% of each run, Pallas kernels for 20% -> 21%
where the time goes in v3:
time: 57.1 us; the launch traced here: 56.5 us
  starting transfers between devices  26.1 us (46%)
  Pallas kernels  18.5 us (32%)
  local copies, waits for them, and re-layouts  6.62 us (12%)
  waiting for transfers between devices  4.33 us (8%)
  other arithmetic  0.86 us (2%)
    ppermute x9, starting transfers between devices, swap_lon(): return lax.ppermute(values, 'lon', [(r, r ^ mask) for r in range(count)])  21.8 us
    pallas_call x7, Pallas kernels, call(): pl.pallas_call(kernel, out_shape=outs, in_specs=[kinds[letter] for letter...  18.5 us
    unnamed x18, local copies, waits for them, and re-layouts  6.62 us
    ppermute x9, waiting for transfers between devices, swap_lon(): return lax.ppermute(values, 'lon', [(r, r ^ mask) for r in range(count)])  4.33 us
    ppermute x1, starting transfers between devices, on_device(): partner_outer = lax.ppermute(both[0], ('lat', 'lon'), crossing)  2.38 us
    ppermute x1, starting transfers between devices, on_device(): outer = lax.ppermute(both[1], ('lat', 'lon'), outward)  1.92 us
  transfers between devices with their start and end apart: 11, of which 1 were waited for; matrix products, arithmetic and copies ran while one was open for 0% of the time, Pallas kernels for 21%

profile of v3, /device:TPU:6, one launch (start us, length us, event | category | flops | bytes accessed | tf_op | source)
XLA Modules:
  0.0 56.5 jit_solution(2470452019086405952)
XLA Ops:
  0.0 1.0 %copy-done.7 = f32[78,2,128]{2,1,0:T(2,128)S(1)} copy-done((f32[78,2,128]{2,1,0:T(2,128)S(1)}, f32[78,2,128]{2,1,0:T(2,128)}, u32[]{:S(2)}) %copy-start.7) | copy-done | bytes 79896
  1.0 0.7 %copy-done.8 = f32[2,128]{1,0:T(2,128)S(1)} copy-done((f32[2,128]{1,0:T(2,128)S(1)}, f32[2,128]{1,0:T(2,128)}, u32[]{:S(2)}) %copy-start.8) | copy-done | bytes 1048
  1.7 3.3 %collective-permute-start.1 = (f32[2,80,128]{2,1,0:T(8,128)S(1)}, f32[2,80,128]{2,1,0:T(8,128)S(1)}, u32[]{:S(2)}, u32[]{:S(2)}) collective-permute-start(f32[2,80,128]{2,1,0:T(8,128)S(1)} %shard_map.91.refs_4_.both_ref), channel_id=1, source_target_pairs={{0,8},{1,9},{2,10},{3,11},{4,12},{5,13},{6,14},{7,15},{8,0},{9,1},... | collective-permute-start | bytes 245768 | tf_op jit(solution)/shard_map/ppermute | solution.py:312
  5.0 2.4 %collective-permute-start.2 = (f32[80,128]{1,0:T(8,128)S(1)}, f32[80,128]{1,0:T(8,128)S(1)}, u32[]{:S(2)}, u32[]{:S(2)}) collective-permute-start(f32[80,128]{1,0:T(8,128)S(1)} %get-tuple-element.37), channel_id=1, source_target_pairs={{8,16},{9,17},{10,18},{11,19},{12,20},{13,21},{14,22},{15,23},{16,... | collective-permute-start | bytes 122888 | tf_op jit(solution)/shard_map/ppermute | solution.py:335
  7.4 1.9 %collective-permute-start = (f32[80,128]{1,0:T(8,128)S(1)}, f32[80,128]{1,0:T(8,128)S(1)}, u32[]{:S(2)}, u32[]{:S(2)}) collective-permute-start(f32[80,128]{1,0:T(8,128)S(1)} %get-tuple-element.38), channel_id=1, source_target_pairs={{0,16},{1,17},{2,18},{3,19},{4,20},{5,21},{6,22},{7,23},{16,32},{1... | collective-permute-start | bytes 122888 | tf_op jit(solution)/shard_map/ppermute | solution.py:334
  9.5 0.9 %copy-done.3 = f32[256,256]{1,0:T(8,128)S(1)} copy-done((f32[256,256]{1,0:T(8,128)S(1)}, f32[256,256]{1,0:T(8,128)}, u32[]{:S(2)}) %copy-start.3) | copy-done | bytes 262168
  10.4 0.9 %copy-done.4 = f32[256,256]{1,0:T(8,128)S(1)} copy-done((f32[256,256]{1,0:T(8,128)S(1)}, f32[256,256]{1,0:T(8,128)}, u32[]{:S(2)}) %copy-start.4) | copy-done | bytes 262168
  11.4 0.9 %copy-done.5 = f32[256,256]{1,0:T(8,128)S(1)} copy-done((f32[256,256]{1,0:T(8,128)S(1)}, f32[256,256]{1,0:T(8,128)}, u32[]{:S(2)}) %copy-start.5) | copy-done | bytes 262168
  12.3 0.9 %copy-done.6 = f32[78,256]{1,0:T(8,128)S(1)} copy-done((f32[78,256]{1,0:T(8,128)S(1)}, f32[78,256]{1,0:T(8,128)}, u32[]{:S(2)}) %copy-start.6) | copy-done | bytes 79896
  13.6 0.8 %shard_map.93.refs_3_.refs_0_ = f32[2,80,128]{2,1,0:T(8,128)S(1)} custom-call(f32[3]{0:T(128)S(1)} %multiply_cosine_fusion.cos_ref, f32[2,80,128]{2,1,0:T(8,128)S(1)} %shard_map.91.refs_4_.both_ref, f32[80,128]{1,0:T(8,128)S(1)} %collective-permute-done.outer_ref, f32[2,80,128]{2,1,0:T(8,128)S(1)} %collective-permute-done.1.partner_ref, ...), custom_call_target="tpu_custom_call" | custom-call | bytes 400000 | tf_op jit(solution)/shard_map/pallas_call | solution.py:288
  14.4 5.9 %collective-permute-start.3 = (f32[2,80,128]{2,1,0:T(8,128)S(1)}, f32[2,80,128]{2,1,0:T(8,128)S(1)}, u32[]{:S(2)}, u32[]{:S(2)}) collective-permute-start(f32[2,80,128]{2,1,0:T(8,128)S(1)} %shard_map.93.refs_3_.refs_0_), channel_id=1, source_target_pairs={{0,7},{1,6},{2,5},{3,4},{4,3},{5,2},{6,1},{7,0},{8,15},{9,14},{10,... | collective-permute-start | bytes 245768 | tf_op jit(solution)/shard_map/ppermute | solution.py:312
  20.3 1.9 %collective-permute-start.9 = (f32[2,80,128]{2,1,0:T(8,128)S(1)}, f32[2,80,128]{2,1,0:T(8,128)S(1)}, u32[]{:S(2)}, u32[]{:S(2)}) collective-permute-start(f32[2,80,128]{2,1,0:T(8,128)S(1)} %shard_map.93.refs_3_.refs_0_), channel_id=1, source_target_pairs={{0,3},{1,2},{2,1},{3,0},{4,7},{5,6},{6,5},{7,4},{8,11},{9,10},{10,... | collective-permute-start | bytes 245768 | tf_op jit(solution)/shard_map/ppermute | solution.py:312
  22.2 1.5 %collective-permute-start.8 = (f32[2,80,128]{2,1,0:T(8,128)S(1)}, f32[2,80,128]{2,1,0:T(8,128)S(1)}, u32[]{:S(2)}, u32[]{:S(2)}) collective-permute-start(f32[2,80,128]{2,1,0:T(8,128)S(1)} %shard_map.93.refs_3_.refs_0_), channel_id=1, source_target_pairs={{0,2},{1,3},{2,0},{3,1},{4,6},{5,7},{6,4},{7,5},{8,10},{9,11},{10,... | collective-permute-start | bytes 245768 | tf_op jit(solution)/shard_map/ppermute | solution.py:312
  23.7 1.0 %collective-permute-start.7 = (f32[2,80,128]{2,1,0:T(8,128)S(1)}, f32[2,80,128]{2,1,0:T(8,128)S(1)}, u32[]{:S(2)}, u32[]{:S(2)}) collective-permute-start(f32[2,80,128]{2,1,0:T(8,128)S(1)} %shard_map.93.refs_3_.refs_0_), channel_id=1, source_target_pairs={{0,1},{1,0},{2,3},{3,2},{4,5},{5,4},{6,7},{7,6},{8,9},{9,8},{10,11... | collective-permute-start | bytes 245768 | tf_op jit(solution)/shard_map/ppermute | solution.py:312
  24.7 1.2 %copy-done.1 = f32[1024,256]{1,0:T(8,128)S(1)} copy-done((f32[1024,256]{1,0:T(8,128)S(1)}, f32[1024,256]{1,0:T(8,128)}, u32[]{:S(2)}) %copy-start.1) | copy-done | bytes 1048600
  26.3 2.0 %collective-permute-start.6 = (f32[2,80,128]{2,1,0:T(8,128)S(1)}, f32[2,80,128]{2,1,0:T(8,128)S(1)}, u32[]{:S(2)}, u32[]{:S(2)}) collective-permute-start(f32[2,80,128]{2,1,0:T(8,128)S(1)} %collective-permute-done.3.refs_4_), channel_id=1, source_target_pairs={{0,3},{1,2},{2,1},{3,0},{4,7},{5,6},{6,5},{7,4},{8,11},{9,10},{10,... | collective-permute-start | bytes 245768 | tf_op jit(solution)/shard_map/ppermute | solution.py:312
  28.3 0.6 %collective-permute-start.5 = (f32[2,80,128]{2,1,0:T(8,128)S(1)}, f32[2,80,128]{2,1,0:T(8,128)S(1)}, u32[]{:S(2)}, u32[]{:S(2)}) collective-permute-start(f32[2,80,128]{2,1,0:T(8,128)S(1)} %collective-permute-done.3.refs_4_), channel_id=1, source_target_pairs={{0,2},{1,3},{2,0},{3,1},{4,6},{5,7},{6,4},{7,5},{8,10},{9,11},{10,... | collective-permute-start | bytes 245768 | tf_op jit(solution)/shard_map/ppermute | solution.py:312
  28.9 2.5 %collective-permute-start.4 = (f32[2,80,128]{2,1,0:T(8,128)S(1)}, f32[2,80,128]{2,1,0:T(8,128)S(1)}, u32[]{:S(2)}, u32[]{:S(2)}) collective-permute-start(f32[2,80,128]{2,1,0:T(8,128)S(1)} %collective-permute-done.3.refs_4_), channel_id=1, source_target_pairs={{0,1},{1,0},{2,3},{3,2},{4,5},{5,4},{6,7},{7,6},{8,9},{9,8},{10,11... | collective-permute-start | bytes 245768 | tf_op jit(solution)/shard_map/ppermute | solution.py:312
  31.4 4.3 %collective-permute-done.8.refs_2_ = f32[2,80,128]{2,1,0:T(8,128)S(1)} collective-permute-done((f32[2,80,128]{2,1,0:T(8,128)S(1)}, f32[2,80,128]{2,1,0:T(8,128)S(1)}, u32[]{:S(2)}, u32[]{:S(2)}) %collective-permute-start.8) | collective-permute-done | bytes 81952 | tf_op jit(solution)/shard_map/ppermute | solution.py:312
  35.7 7.1 %shard_map.95 = (f32[256,256]{1,0:T(8,128)S(1)}, bf16[8,256,112]{2,1,0:T(8,128)(2,1)S(1)}, f32[8,256,128]{2,1,0:T(8,128)S(1)}, f32[80,128]{1,0:T(8,128)S(1)}, f32[16,2,128]{2,1,0:T(2,128)S(1)}) custom-call(f32[3]{0:T(128)S(1)} %multiply_cosine_fusion.cos_ref, f32[2,80,128]{2,1,0:T(8,128)S(1)} %shard_map.93.refs_3_.refs_0_, ...), custom_call_target="tpu_custom_call" | custom-call | flops 5000000000 | bytes 3000000 | tf_op jit(solution)/shard_map/pallas_call | solution.py:288
  42.8 5.9 %shard_map.96 = (f32[128,256]{1,0:T(8,128)S(1)}, bf16[8,112,896]{2,1,0:T(8,128)(2,1)S(1)}, bf16[8,80,896]{2,1,0:T(8,128)(2,1)S(1)}) custom-call(f32[3]{0:T(128)S(1)} %multiply_cosine_fusion.cos_ref, f32[2,80,128]{2,1,0:T(8,128)S(1)} %collective-permute-done.4.refs_0_, f32[2,80,128]{2,1,0:T(8,128)S(1)} %collective-permute-done.5.refs_1_, ...), custom_call_target="tpu_custom_call" | custom-call | flops 5000000000 | bytes 6000000 | tf_op jit(solution)/shard_map/pallas_call | solution.py:288
  48.7 3.1 %collective-permute-start.10 = (f32[128,256]{1,0:T(8,128)S(1)}, f32[128,256]{1,0:T(8,128)S(1)}, u32[]{:S(2)}, u32[]{:S(2)}) collective-permute-start(f32[128,256]{1,0:T(8,128)S(1)} %get-tuple-element.34), channel_id=1, source_target_pairs={{0,8},{1,9},{2,10},{3,11},{4,12},{5,13},{6,14},{7,15},{8,0},{9,1},... | collective-permute-start | bytes 393224 | tf_op jit(solution)/shard_map/ppermute | solution.py:312
  51.8 4.0 %shard_map.97 = f32[128,256]{1,0:T(8,128)S(1)} custom-call(bf16[8,112,896]{2,1,0:T(8,128)(2,1)S(1)} %get-tuple-element.32.refs_0_, bf16[8,80,896]{2,1,0:T(8,128)(2,1)S(1)} %get-tuple-element.33.refs_1_, bf16[2,256,256]{2,1,0:T(8,128)(2,1)S(1)} %get-tuple-element.23.refs_6_.refs_2_, bf16[2,256,1024]{2,1,0:T(8,128)(2,1)S(1)} %get-tuple-element.24.refs_7_.refs_3_, ...), custom_call_target="tpu_custom_call" | custom-call | flops 3000000000 | bytes 6000000 | tf_op jit(solution)/shard_map/pallas_call | solution.py:288
  55.8 0.7 %pad_maximum_fusion = f32[2,128,256]{2,1,0:T(8,128)} fusion(f32[1,128,256]{2,1,0:T(8,128)S(1)} %get-tuple-element.36, f32[1,128,256]{2,1,0:T(8,128)S(1)} %get-tuple-element.35), kind=kLoop, calls=%fused_computation | loop fusion | flops 65536 | bytes 524288 | tf_op jit(solution)/shard_map/stack | solution.py:407
  (27 shorter events, 1.0 us)
Async XLA Ops:
  0.0 24.7 %copy-start = (f32[256,1024]{1,0:T(8,128)S(1)}, f32[256,1024]{1,0:T(8,128)}, u32[]{:S(2)}) copy-start(f32[256,1024]{1,0:T(8,128)} %refs_1_.3) | copy-start | bytes 3145732
  0.0 1.0 %copy-start.7 = (f32[78,2,128]{2,1,0:T(2,128)S(1)}, f32[78,2,128]{2,1,0:T(2,128)}, u32[]{:S(2)}) copy-start(f32[78,2,128]{2,1,0:T(2,128)} %fields_ref.1) | copy-start | bytes 239620
  1.0 0.7 %copy-start.8 = (f32[2,128]{1,0:T(2,128)S(1)}, f32[2,128]{1,0:T(2,128)}, u32[]{:S(2)}) copy-start(f32[2,128]{1,0:T(2,128)} %kappa_ref.1) | copy-start | bytes 3076
  1.7 23.1 %copy-start.2 = (f32[256,256]{1,0:T(8,128)S(1)}, f32[256,256]{1,0:T(8,128)}, u32[]{:S(2)}) copy-start(f32[256,256]{1,0:T(8,128)} %refs_0_.3) | copy-start | bytes 786436
  1.7 11.9 %collective-permute-start.1 = (f32[2,80,128]{2,1,0:T(8,128)S(1)}, f32[2,80,128]{2,1,0:T(8,128)S(1)}, u32[]{:S(2)}, u32[]{:S(2)}) collective-permute-start(f32[2,80,128]{2,1,0:T(8,128)S(1)} %shard_map.91.refs_4_.both_ref), channel_id=1, source_target_pairs={{0,8},{1,9},{2,10},{3,11},{4,12},{5,13},{6,14},{7,15},{8,0},{9,1},... | collective-permute-start | bytes 245768 | tf_op jit(solution)/shard_map/ppermute | solution.py:312
  5.0 8.6 %collective-permute-start.2 = (f32[80,128]{1,0:T(8,128)S(1)}, f32[80,128]{1,0:T(8,128)S(1)}, u32[]{:S(2)}, u32[]{:S(2)}) collective-permute-start(f32[80,128]{1,0:T(8,128)S(1)} %get-tuple-element.37), channel_id=1, source_target_pairs={{8,16},{9,17},{10,18},{11,19},{12,20},{13,21},{14,22},{15,23},{16,... | collective-permute-start | bytes 122888 | tf_op jit(solution)/shard_map/ppermute | solution.py:335
  7.4 6.2 %collective-permute-start = (f32[80,128]{1,0:T(8,128)S(1)}, f32[80,128]{1,0:T(8,128)S(1)}, u32[]{:S(2)}, u32[]{:S(2)}) collective-permute-start(f32[80,128]{1,0:T(8,128)S(1)} %get-tuple-element.38), channel_id=1, source_target_pairs={{0,16},{1,17},{2,18},{3,19},{4,20},{5,21},{6,22},{7,23},{16,32},{1... | collective-permute-start | bytes 122888 | tf_op jit(solution)/shard_map/ppermute | solution.py:334
  9.5 1.0 %copy-start.3 = (f32[256,256]{1,0:T(8,128)S(1)}, f32[256,256]{1,0:T(8,128)}, u32[]{:S(2)}) copy-start(f32[256,256]{1,0:T(8,128)} %refs_1_.2) | copy-start | bytes 786436
  10.4 0.9 %copy-start.4 = (f32[256,256]{1,0:T(8,128)S(1)}, f32[256,256]{1,0:T(8,128)}, u32[]{:S(2)}) copy-start(f32[256,256]{1,0:T(8,128)} %refs_2_.2) | copy-start | bytes 786436
  11.4 0.9 %copy-start.5 = (f32[256,256]{1,0:T(8,128)S(1)}, f32[256,256]{1,0:T(8,128)}, u32[]{:S(2)}) copy-start(f32[256,256]{1,0:T(8,128)} %refs_3_.1) | copy-start | bytes 786436
  12.3 0.9 %copy-start.6 = (f32[78,256]{1,0:T(8,128)S(1)}, f32[78,256]{1,0:T(8,128)}, u32[]{:S(2)}) copy-start(f32[78,256]{1,0:T(8,128)} %refs_0_.2) | copy-start | bytes 239620
  14.4 11.9 %collective-permute-start.3 = (f32[2,80,128]{2,1,0:T(8,128)S(1)}, f32[2,80,128]{2,1,0:T(8,128)S(1)}, u32[]{:S(2)}, u32[]{:S(2)}) collective-permute-start(f32[2,80,128]{2,1,0:T(8,128)S(1)} %shard_map.93.refs_3_.refs_0_), channel_id=1, source_target_pairs={{0,7},{1,6},{2,5},{3,4},{4,3},{5,2},{6,1},{7,0},{8,15},{9,14},{10,... | collective-permute-start | bytes 245768 | tf_op jit(solution)/shard_map/ppermute | solution.py:312
  20.3 8.5 %collective-permute-start.9 = (f32[2,80,128]{2,1,0:T(8,128)S(1)}, f32[2,80,128]{2,1,0:T(8,128)S(1)}, u32[]{:S(2)}, u32[]{:S(2)}) collective-permute-start(f32[2,80,128]{2,1,0:T(8,128)S(1)} %shard_map.93.refs_3_.refs_0_), channel_id=1, source_target_pairs={{0,3},{1,2},{2,1},{3,0},{4,7},{5,6},{6,5},{7,4},{8,11},{9,10},{10,... | collective-permute-start | bytes 245768 | tf_op jit(solution)/shard_map/ppermute | solution.py:312
  22.2 13.5 %collective-permute-start.8 = (f32[2,80,128]{2,1,0:T(8,128)S(1)}, f32[2,80,128]{2,1,0:T(8,128)S(1)}, u32[]{:S(2)}, u32[]{:S(2)}) collective-permute-start(f32[2,80,128]{2,1,0:T(8,128)S(1)} %shard_map.93.refs_3_.refs_0_), channel_id=1, source_target_pairs={{0,2},{1,3},{2,0},{3,1},{4,6},{5,7},{6,4},{7,5},{8,10},{9,11},{10,... | collective-permute-start | bytes 245768 | tf_op jit(solution)/shard_map/ppermute | solution.py:312
  23.7 12.0 %collective-permute-start.7 = (f32[2,80,128]{2,1,0:T(8,128)S(1)}, f32[2,80,128]{2,1,0:T(8,128)S(1)}, u32[]{:S(2)}, u32[]{:S(2)}) collective-permute-start(f32[2,80,128]{2,1,0:T(8,128)S(1)} %shard_map.93.refs_3_.refs_0_), channel_id=1, source_target_pairs={{0,1},{1,0},{2,3},{3,2},{4,5},{5,4},{6,7},{7,6},{8,9},{9,8},{10,11... | collective-permute-start | bytes 245768 | tf_op jit(solution)/shard_map/ppermute | solution.py:312
  24.7 1.2 %copy-start.1 = (f32[1024,256]{1,0:T(8,128)S(1)}, f32[1024,256]{1,0:T(8,128)}, u32[]{:S(2)}) copy-start(f32[1024,256]{1,0:T(8,128)} %refs_2_.3) | copy-start | bytes 3145732
  26.3 16.5 %collective-permute-start.6 = (f32[2,80,128]{2,1,0:T(8,128)S(1)}, f32[2,80,128]{2,1,0:T(8,128)S(1)}, u32[]{:S(2)}, u32[]{:S(2)}) collective-permute-start(f32[2,80,128]{2,1,0:T(8,128)S(1)} %collective-permute-done.3.refs_4_), channel_id=1, source_target_pairs={{0,3},{1,2},{2,1},{3,0},{4,7},{5,6},{6,5},{7,4},{8,11},{9,10},{10,... | collective-permute-start | bytes 245768 | tf_op jit(solution)/shard_map/ppermute | solution.py:312
  28.3 14.6 %collective-permute-start.5 = (f32[2,80,128]{2,1,0:T(8,128)S(1)}, f32[2,80,128]{2,1,0:T(8,128)S(1)}, u32[]{:S(2)}, u32[]{:S(2)}) collective-permute-start(f32[2,80,128]{2,1,0:T(8,128)S(1)} %collective-permute-done.3.refs_4_), channel_id=1, source_target_pairs={{0,2},{1,3},{2,0},{3,1},{4,6},{5,7},{6,4},{7,5},{8,10},{9,11},{10,... | collective-permute-start | bytes 245768 | tf_op jit(solution)/shard_map/ppermute | solution.py:312
  28.9 14.0 %collective-permute-start.4 = (f32[2,80,128]{2,1,0:T(8,128)S(1)}, f32[2,80,128]{2,1,0:T(8,128)S(1)}, u32[]{:S(2)}, u32[]{:S(2)}) collective-permute-start(f32[2,80,128]{2,1,0:T(8,128)S(1)} %collective-permute-done.3.refs_4_), channel_id=1, source_target_pairs={{0,1},{1,0},{2,3},{3,2},{4,5},{5,4},{6,7},{7,6},{8,9},{9,8},{10,11... | collective-permute-start | bytes 245768 | tf_op jit(solution)/shard_map/ppermute | solution.py:312
  48.7 7.0 %collective-permute-start.10 = (f32[128,256]{1,0:T(8,128)S(1)}, f32[128,256]{1,0:T(8,128)S(1)}, u32[]{:S(2)}, u32[]{:S(2)}) collective-permute-start(f32[128,256]{1,0:T(8,128)S(1)} %get-tuple-element.34), channel_id=1, source_target_pairs={{0,8},{1,9},{2,10},{3,11},{4,12},{5,13},{6,14},{7,15},{8,0},{9,1},... | collective-permute-start | bytes 393224 | tf_op jit(solution)/shard_map/ppermute | solution.py:312

commit v4 on v3

--- a/solution.py
+++ b/solution.py
@@ -13,7 +13,7 @@
 CENTER_LAT = 45.0
 SPACING = 0.25
 EPSILON = 1e-05
-PARTNERS = (0, 1, 2, 3, 7, 6, 5, 4)
+PARTNERS = (0, 1, 3, 7, 2, 6, 5, 4)
 ROWS = 80
 F32 = jnp.float32
 BF16 = jnp.bfloat16
@@ -51,7 +51,7 @@
 
 
 def stencil_kernel(
-    cos_ref, both_ref, outer_ref, partner_ref, partner_outer_ref, order_ref, chunk_ref
+    cos_ref, both_ref, outer_ref, partner_ref, partner_outer_ref, chunk_ref
 ):
     inverse = 1.0 / cos_ref[0]
     face_inner = cos_ref[1]
@@ -157,15 +157,15 @@
 
 
 def early_kernel(cos_ref, *refs):
-    pieces = refs[:5]
-    embed3_ref, qkv_high_ref, qkv_low_ref = refs[5:8]
-    hidden_ref, query3_ref, state_ref, columns_ref, edges_ref = refs[9:14]
-    key3, value3 = refs[14:]
+    pieces = refs[:4]
+    embed3_ref, qkv_high_ref, qkv_low_ref = refs[4:7]
+    hidden_ref, query3_ref, state_ref, columns_ref, edges_ref = refs[8:13]
+    key3, value3 = refs[13:]
     z = lax.axis_index("lon") % 8
     inverse = 1.0 / cos_ref[0]
     step = 0.5 * STEP_SIZE * inverse * inverse
     total = jnp.zeros((ROWS, 128), F32)
-    for k in range(5):
+    for k in range(4):
         for index in range(2):
             edges_ref[2 * k + index] = pieces[k][index, 78:80, :]
             total = place_edges(total, pieces[k][index], 2 * k + index)
@@ -179,7 +179,7 @@
         here = pieces[0][index, 78:80, :]
         beside = pieces[1][index, 78:80, :]
         wrapped = jnp.where(wraps == 1, 1 - index, index)
-        across = jnp.where(outer, pieces[4][wrapped, 78:80, :], pieces[3][index, 78:80, :])
+        across = jnp.where(outer, pieces[3][wrapped, 78:80, :], pieces[2][index, 78:80, :])
         west = jnp.where(flag, across, beside)
         east = jnp.where(flag, beside, across)
         fixes.append(face_fix(step, here[0:1], west[1:2]))
@@ -191,7 +191,7 @@
         part = part + jnp.where(lane == 0, fixes[:, 2 * index : 2 * index + 1], 0.0)
         part = part + jnp.where(lane == 127, fixes[:, 2 * index + 1 : 2 * index + 2], 0.0)
         parts.append(part)
-    for k in range(1, 5):
+    for k in range(1, 4):
         parts += [pieces[k][0], pieces[k][1]]
     hidden, normed = embed_tokens(jnp.concatenate(parts, axis=1), embed3_ref)
     hidden_ref[...] = jnp.transpose(hidden[:, :256])
@@ -204,7 +204,7 @@
     for h in range(HEADS):
         part = slice(32 * h, 32 * h + 32)
         query3_ref[h] = jnp.concatenate([high[:, part], high[:, part], low[:, part], mask], axis=1)
-    lane = lax.broadcasted_iota(jnp.int32, (16, 1280), 1)
+    lane = lax.broadcasted_iota(jnp.int32, (16, 1024), 1)
     edge = jnp.logical_or(lane % 128 == 0, lane % 128 == 127)
     store_keys(
         normed, jnp.logical_and(edge, lane >= 256), 0, qkv_high_ref, qkv_low_ref, key3, value3
@@ -235,11 +235,11 @@
 
 
 def late_kernel(cos_ref, *refs):
-    pieces = refs[:3]
-    embed3_ref, qkv_high_ref, qkv_low_ref, out2_ref, up2_ref, down2_ref = refs[3:9]
-    hidden_ref, query3_ref, state_ref, columns_ref, edges_ref = refs[9:14]
-    send_ref, key3, value3 = refs[14:17]
-    edges, fixes = refs[17:]
+    pieces = refs[:4]
+    embed3_ref, qkv_high_ref, qkv_low_ref, out2_ref, up2_ref, down2_ref = refs[4:10]
+    hidden_ref, query3_ref, state_ref, columns_ref, edges_ref = refs[10:15]
+    send_ref, key3, value3 = refs[15:18]
+    edges, fixes = refs[18:]
     position = lax.axis_index("lon")
     y = position // 8
     z = position % 8
@@ -249,11 +249,11 @@
     for k in range(8):
         for index in range(2):
             half = y if index == 0 else 1 - y
-            if k < 5:
+            if k < 4:
                 here = edges_ref[2 * k + index]
             else:
-                here = pieces[k - 5][index, 78:80, :]
-                total = place_edges(total, pieces[k - 5][index], 2 * k + index)
+                here = pieces[k - 4][index, 78:80, :]
+                total = place_edges(total, pieces[k - 4][index], 2 * k + index)
             edges[half * 8 + jnp.bitwise_xor(z, PARTNERS[k])] = here
     fixes[...] = jnp.zeros_like(fixes)
     for k in range(8):
@@ -267,12 +267,12 @@
             fixes[slot : slot + 1, :] = face_fix(step, here[0:1], west[1:2])
             fixes[slot + 1 : slot + 2, :] = face_fix(step, here[1:2], east[0:1])
     total = total + jnp.transpose(fixes[...])[:ROWS]
-    parts = [pieces[k][index] for k in range(3) for index in range(2)] + [total]
+    parts = [pieces[k][index] for k in range(4) for index in range(2)] + [total]
     hidden, normed = embed_tokens(jnp.concatenate(parts, axis=1), embed3_ref)
-    lane = lax.broadcasted_iota(jnp.int32, (16, 896), 1)
+    lane = lax.broadcasted_iota(jnp.int32, (16, 1152), 1)
     edge = jnp.logical_or(lane % 128 == 0, lane % 128 == 127)
-    unused = jnp.logical_or(lane < 768 + 4, lane >= 768 + 32)
-    masked = jnp.where(lane < 768, edge.astype(jnp.int32), unused.astype(jnp.int32)) == 1
+    unused = jnp.logical_or(lane < 1024 + 4, lane >= 1024 + 32)
+    masked = jnp.where(lane < 1024, edge.astype(jnp.int32), unused.astype(jnp.int32)) == 1
     store_keys(normed, masked, 0, qkv_high_ref, qkv_low_ref, key3, value3)
     send_ref[...] = finish(
         slice(128, 256), key3, value3, out2_ref, up2_ref, down2_ref, hidden_ref, query3_ref, state_ref
@@ -333,25 +333,25 @@
     partner = swap_lon(both, 8)
     outer = lax.ppermute(both[1], ("lat", "lon"), outward)
     partner_outer = lax.ppermute(both[0], ("lat", "lon"), crossing)
+    chunk = call(
+        stencil_kernel,
+        pair,
+        (cosines, both, outer, partner, partner_outer),
+        "svvvv",
+        limit=4 * 2**20,
+        moved=400000,
+    )
+    far = swap_lon(chunk, 7)
+    near = [swap_lon(chunk, k) for k in (1, 2, 3)]
+    far_near = [swap_lon(far, k) for k in (1, 2, 3)]
     first = call(
         first_weights_kernel,
         (shape(256, 3 * ROWS, dtype=BF16), shape(768, 256, dtype=BF16), shape(768, 256, dtype=BF16)),
-        (w_embed, query_weight, key_weight, value_weight, both),
+        (w_embed, query_weight, key_weight, value_weight, far),
         "vvvvh",
         limit=8 * 2**20,
         moved=2000000,
     )
-    chunk = call(
-        stencil_kernel,
-        pair,
-        (cosines, both, outer, partner, partner_outer, first[0]),
-        "svvvvh",
-        limit=4 * 2**20,
-        moved=400000,
-    )
-    far = swap_lon(chunk, 7)
-    near = [swap_lon(chunk, k) for k in (1, 2, 3)]
-    far_near = [swap_lon(far, k) for k in (1, 2, 3)]
     *last, order = call(
         last_weights_kernel,
         (
@@ -374,9 +374,9 @@
             plane,
             shape(16, 2, 128),
         ),
-        (cosines, chunk, *near, far, *first, order),
-        "s" + 8 * "v" + "h",
-        scratch=[pltpu.VMEM((HEADS, 112, 1280), BF16), pltpu.VMEM((HEADS, 80, 1280), BF16)],
+        (cosines, chunk, near[0], near[2], far, *first, order),
+        "s" + 7 * "v" + "h",
+        scratch=[pltpu.VMEM((HEADS, 112, 1024), BF16), pltpu.VMEM((HEADS, 80, 1024), BF16)],
         limit=40 * 2**20,
         flops=5 * 10**9,
         moved=3000000,
@@ -384,9 +384,9 @@
     tile = shape(128, 256)
     send, *keys = call(
         late_kernel,
-        (tile, shape(HEADS, 112, 896, dtype=BF16), shape(HEADS, 80, 896, dtype=BF16)),
-        (cosines, *far_near, *first, *last, *early),
-        "s" + 14 * "v",
+        (tile, shape(HEADS, 112, 1152, dtype=BF16), shape(HEADS, 80, 1152, dtype=BF16)),
+        (cosines, near[1], *far_near, *first, *last, *early),
+        "s" + 15 * "v",
         scratch=[pltpu.VMEM((16, 2, 128), F32), pltpu.VMEM((128, 128), F32)],
         limit=36 * 2**20,
         flops=5 * 10**9,

time: 57.1 us -> 54.5 us (0.954)
  local copies, waits for them, and re-layouts: 6.62 us -> 5.04 us
  starting transfers between devices: 26.1 us -> 25.1 us
    ppermute x9, waiting for transfers between devices: 4.33 us -> 0.02 us  [swap_lon(): return lax.ppermute(values, 'lon', [(r, r ^ mask) for r in range(count)])]
    ppermute x1, waiting for transfers between devices: 0.01 us -> 2.97 us  [on_device(): partner_outer = lax.ppermute(both[0], ('lat', 'lon'), crossing)]
    unnamed x18, local copies, waits for them, and re-layouts: 6.62 us -> 5.03 us
    ppermute x1, waiting for transfers between devices: 0.01 us -> 1.18 us  [on_device(): outer = lax.ppermute(both[1], ('lat', 'lon'), outward)]
    ppermute x9, starting transfers between devices: 21.8 us -> 20.8 us  [swap_lon(): return lax.ppermute(values, 'lon', [(r, r ^ mask) for r in range(count)])]
  transfers between devices with their start and end apart: 11 -> 11, of which waited for: 1 -> 2; matrix products, arithmetic and copies ran while one was open for 0% -> 0% of each run, Pallas kernels for 21% -> 21%
where the time goes in v4:
time: 54.5 us; the launch traced here: 54.2 us
  starting transfers between devices  25.1 us (46%)
  Pallas kernels  18.8 us (34%)
  local copies, waits for them, and re-layouts  5.04 us (9%)
  waiting for transfers between devices  4.17 us (8%)
  other arithmetic  0.86 us (2%)
    ppermute x9, starting transfers between devices, swap_lon(): return lax.ppermute(values, 'lon', [(r, r ^ mask) for r in range(count)])  20.8 us
    pallas_call x7, Pallas kernels, call(): pl.pallas_call(kernel, out_shape=outs, in_specs=[kinds[letter] for letter...  18.8 us
    unnamed x18, local copies, waits for them, and re-layouts  5.03 us
    ppermute x1, waiting for transfers between devices, on_device(): partner_outer = lax.ppermute(both[0], ('lat', 'lon'), crossing)  2.97 us
    ppermute x1, starting transfers between devices, on_device(): partner_outer = lax.ppermute(both[0], ('lat', 'lon'), crossing)  2.38 us
    ppermute x1, starting transfers between devices, on_device(): outer = lax.ppermute(both[1], ('lat', 'lon'), outward)  1.92 us
    ppermute x1, waiting for transfers between devices, on_device(): outer = lax.ppermute(both[1], ('lat', 'lon'), outward)  1.18 us
  transfers between devices with their start and end apart: 11, of which 2 were waited for; matrix products, arithmetic and copies ran while one was open for 0% of the time, Pallas kernels for 21%

profile of v4, /device:TPU:6, one launch (start us, length us, event | category | flops | bytes accessed | tf_op | source)
XLA Modules:
  0.0 54.2 jit_solution(11393906779976862459)
XLA Ops:
  0.0 0.9 %copy-done.7 = f32[78,2,128]{2,1,0:T(2,128)S(1)} copy-done((f32[78,2,128]{2,1,0:T(2,128)S(1)}, f32[78,2,128]{2,1,0:T(2,128)}, u32[]{:S(2)}) %copy-start.7) | copy-done | bytes 79896
  1.0 0.7 %copy-done.8 = f32[2,128]{1,0:T(2,128)S(1)} copy-done((f32[2,128]{1,0:T(2,128)S(1)}, f32[2,128]{1,0:T(2,128)}, u32[]{:S(2)}) %copy-start.8) | copy-done | bytes 1048
  1.7 3.3 %collective-permute-start.1 = (f32[2,80,128]{2,1,0:T(8,128)S(1)}, f32[2,80,128]{2,1,0:T(8,128)S(1)}, u32[]{:S(2)}, u32[]{:S(2)}) collective-permute-start(f32[2,80,128]{2,1,0:T(8,128)S(1)} %shard_map.91.both_ref), channel_id=1, source_target_pairs={{0,8},{1,9},{2,10},{3,11},{4,12},{5,13},{6,14},{7,15},{8,0},{9,1},... | collective-permute-start | bytes 245768 | tf_op jit(solution)/shard_map/ppermute | solution.py:312
  5.0 2.4 %collective-permute-start.2 = (f32[80,128]{1,0:T(8,128)S(1)}, f32[80,128]{1,0:T(8,128)S(1)}, u32[]{:S(2)}, u32[]{:S(2)}) collective-permute-start(f32[80,128]{1,0:T(8,128)S(1)} %get-tuple-element.37), channel_id=1, source_target_pairs={{8,16},{9,17},{10,18},{11,19},{12,20},{13,21},{14,22},{15,23},{16,... | collective-permute-start | bytes 122888 | tf_op jit(solution)/shard_map/ppermute | solution.py:335
  7.4 1.9 %collective-permute-start = (f32[80,128]{1,0:T(8,128)S(1)}, f32[80,128]{1,0:T(8,128)S(1)}, u32[]{:S(2)}, u32[]{:S(2)}) collective-permute-start(f32[80,128]{1,0:T(8,128)S(1)} %get-tuple-element.38), channel_id=1, source_target_pairs={{0,16},{1,17},{2,18},{3,19},{4,20},{5,21},{6,22},{7,23},{16,32},{1... | collective-permute-start | bytes 122888 | tf_op jit(solution)/shard_map/ppermute | solution.py:334
  9.4 3.0 %collective-permute-done.2.partner_outer_ref = f32[80,128]{1,0:T(8,128)S(1)} collective-permute-done((f32[80,128]{1,0:T(8,128)S(1)}, f32[80,128]{1,0:T(8,128)S(1)}, u32[]{:S(2)}, u32[]{:S(2)}) %collective-permute-start.2) | collective-permute-done | bytes 40992 | tf_op jit(solution)/shard_map/ppermute | solution.py:335
  12.4 1.2 %collective-permute-done.outer_ref = f32[80,128]{1,0:T(8,128)S(1)} collective-permute-done((f32[80,128]{1,0:T(8,128)S(1)}, f32[80,128]{1,0:T(8,128)S(1)}, u32[]{:S(2)}, u32[]{:S(2)}) %collective-permute-start) | collective-permute-done | bytes 40992 | tf_op jit(solution)/shard_map/ppermute | solution.py:334
  13.6 0.7 %shard_map.92.refs_3_.refs_0_ = f32[2,80,128]{2,1,0:T(8,128)S(1)} custom-call(f32[3]{0:T(128)S(1)} %multiply_cosine_fusion.cos_ref, f32[2,80,128]{2,1,0:T(8,128)S(1)} %shard_map.91.both_ref, f32[80,128]{1,0:T(8,128)S(1)} %collective-permute-done.outer_ref, f32[2,80,128]{2,1,0:T(8,128)S(1)} %collective-permute-done.1.partner_ref, ...), custom_call_target="tpu_custom_call" | custom-call | bytes 400000 | tf_op jit(solution)/shard_map/pallas_call | solution.py:288
  14.3 5.9 %collective-permute-start.4 = (f32[2,80,128]{2,1,0:T(8,128)S(1)}, f32[2,80,128]{2,1,0:T(8,128)S(1)}, u32[]{:S(2)}, u32[]{:S(2)}) collective-permute-start(f32[2,80,128]{2,1,0:T(8,128)S(1)} %shard_map.92.refs_3_.refs_0_), channel_id=1, source_target_pairs={{0,7},{1,6},{2,5},{3,4},{4,3},{5,2},{6,1},{7,0},{8,15},{9,14},{10,... | collective-permute-start | bytes 245768 | tf_op jit(solution)/shard_map/ppermute | solution.py:312
  20.3 1.9 %collective-permute-start.9 = (f32[2,80,128]{2,1,0:T(8,128)S(1)}, f32[2,80,128]{2,1,0:T(8,128)S(1)}, u32[]{:S(2)}, u32[]{:S(2)}) collective-permute-start(f32[2,80,128]{2,1,0:T(8,128)S(1)} %shard_map.92.refs_3_.refs_0_), channel_id=1, source_target_pairs={{0,3},{1,2},{2,1},{3,0},{4,7},{5,6},{6,5},{7,4},{8,11},{9,10},{10,... | collective-permute-start | bytes 245768 | tf_op jit(solution)/shard_map/ppermute | solution.py:312
  22.2 1.0 %collective-permute-start.8 = (f32[2,80,128]{2,1,0:T(8,128)S(1)}, f32[2,80,128]{2,1,0:T(8,128)S(1)}, u32[]{:S(2)}, u32[]{:S(2)}) collective-permute-start(f32[2,80,128]{2,1,0:T(8,128)S(1)} %shard_map.92.refs_3_.refs_0_), channel_id=1, source_target_pairs={{0,1},{1,0},{2,3},{3,2},{4,5},{5,4},{6,7},{7,6},{8,9},{9,8},{10,11... | collective-permute-start | bytes 245768 | tf_op jit(solution)/shard_map/ppermute | solution.py:312
  23.2 1.5 %collective-permute-start.3 = (f32[2,80,128]{2,1,0:T(8,128)S(1)}, f32[2,80,128]{2,1,0:T(8,128)S(1)}, u32[]{:S(2)}, u32[]{:S(2)}) collective-permute-start(f32[2,80,128]{2,1,0:T(8,128)S(1)} %shard_map.92.refs_3_.refs_0_), channel_id=1, source_target_pairs={{0,2},{1,3},{2,0},{3,1},{4,6},{5,7},{6,4},{7,5},{8,10},{9,11},{10,... | collective-permute-start | bytes 245768 | tf_op jit(solution)/shard_map/ppermute | solution.py:312
  24.7 1.2 %copy-done = f32[256,1024]{1,0:T(8,128)S(1)} copy-done((f32[256,1024]{1,0:T(8,128)S(1)}, f32[256,1024]{1,0:T(8,128)}, u32[]{:S(2)}) %copy-start) | copy-done | bytes 1048600
  25.9 1.2 %copy-done.1 = f32[1024,256]{1,0:T(8,128)S(1)} copy-done((f32[1024,256]{1,0:T(8,128)S(1)}, f32[1024,256]{1,0:T(8,128)}, u32[]{:S(2)}) %copy-start.1) | copy-done | bytes 1048600
  27.1 0.9 %copy-done.2 = f32[256,256]{1,0:T(8,128)S(1)} copy-done((f32[256,256]{1,0:T(8,128)S(1)}, f32[256,256]{1,0:T(8,128)}, u32[]{:S(2)}) %copy-start.2) | copy-done | bytes 262168
  28.4 2.0 %collective-permute-start.7 = (f32[2,80,128]{2,1,0:T(8,128)S(1)}, f32[2,80,128]{2,1,0:T(8,128)S(1)}, u32[]{:S(2)}, u32[]{:S(2)}) collective-permute-start(f32[2,80,128]{2,1,0:T(8,128)S(1)} %collective-permute-done.4.refs_4_.refs_3_), channel_id=1, source_target_pairs={{0,3},{1,2},{2,1},{3,0},{4,7},{5,6},{6,5},{7,4},{8,11},{9,10},{10,... | collective-permute-start | bytes 245768 | tf_op jit(solution)/shard_map/ppermute | solution.py:312
  30.4 0.6 %collective-permute-start.6 = (f32[2,80,128]{2,1,0:T(8,128)S(1)}, f32[2,80,128]{2,1,0:T(8,128)S(1)}, u32[]{:S(2)}, u32[]{:S(2)}) collective-permute-start(f32[2,80,128]{2,1,0:T(8,128)S(1)} %collective-permute-done.4.refs_4_.refs_3_), channel_id=1, source_target_pairs={{0,2},{1,3},{2,0},{3,1},{4,6},{5,7},{6,4},{7,5},{8,10},{9,11},{10,... | collective-permute-start | bytes 245768 | tf_op jit(solution)/shard_map/ppermute | solution.py:312
  31.0 0.4 shard_map.93
  31.4 2.2 %collective-permute-start.5 = (f32[2,80,128]{2,1,0:T(8,128)S(1)}, f32[2,80,128]{2,1,0:T(8,128)S(1)}, u32[]{:S(2)}, u32[]{:S(2)}) collective-permute-start(f32[2,80,128]{2,1,0:T(8,128)S(1)} %collective-permute-done.4.refs_4_.refs_3_), channel_id=1, source_target_pairs={{0,1},{1,0},{2,3},{3,2},{4,5},{5,4},{6,7},{7,6},{8,9},{9,8},{10,11... | collective-permute-start | bytes 245768 | tf_op jit(solution)/shard_map/ppermute | solution.py:312
  33.6 6.4 %shard_map.95 = (f32[256,256]{1,0:T(8,128)S(1)}, bf16[8,256,112]{2,1,0:T(8,128)(2,1)S(1)}, f32[8,256,128]{2,1,0:T(8,128)S(1)}, f32[80,128]{1,0:T(8,128)S(1)}, f32[16,2,128]{2,1,0:T(2,128)S(1)}) custom-call(f32[3]{0:T(128)S(1)} %multiply_cosine_fusion.cos_ref, f32[2,80,128]{2,1,0:T(8,128)S(1)} %shard_map.92.refs_3_.refs_0_, ...), custom_call_target="tpu_custom_call" | custom-call | flops 5000000000 | bytes 3000000 | tf_op jit(solution)/shard_map/pallas_call | solution.py:288
  40.1 6.5 %shard_map.96 = (f32[128,256]{1,0:T(8,128)S(1)}, bf16[8,112,1152]{2,1,0:T(8,128)(2,1)S(1)}, bf16[8,80,1152]{2,1,0:T(8,128)(2,1)S(1)}) custom-call(f32[3]{0:T(128)S(1)} %multiply_cosine_fusion.cos_ref, f32[2,80,128]{2,1,0:T(8,128)S(1)} %collective-permute-done.3.refs_0_, f32[2,80,128]{2,1,0:T(8,128)S(1)} %collective-permute-done.5.refs_1_, ...), custom_call_target="tpu_custom_call" | custom-call | flops 5000000000 | bytes 6000000 | tf_op jit(solution)/shard_map/pallas_call | solution.py:288
  46.6 2.5 %collective-permute-start.10 = (f32[128,256]{1,0:T(8,128)S(1)}, f32[128,256]{1,0:T(8,128)S(1)}, u32[]{:S(2)}, u32[]{:S(2)}) collective-permute-start(f32[128,256]{1,0:T(8,128)S(1)} %get-tuple-element.34), channel_id=1, source_target_pairs={{0,8},{1,9},{2,10},{3,11},{4,12},{5,13},{6,14},{7,15},{8,0},{9,1},... | collective-permute-start | bytes 393224 | tf_op jit(solution)/shard_map/ppermute | solution.py:312
  49.1 4.3 %shard_map.97 = f32[128,256]{1,0:T(8,128)S(1)} custom-call(bf16[8,112,1152]{2,1,0:T(8,128)(2,1)S(1)} %get-tuple-element.32.refs_0_, bf16[8,80,1152]{2,1,0:T(8,128)(2,1)S(1)} %get-tuple-element.33.refs_1_, bf16[2,256,256]{2,1,0:T(8,128)(2,1)S(1)} %get-tuple-element.23.refs_7_.refs_2_, bf16[2,256,1024]{2,1,0:T(8,128)(2,1)S(1)} %get-tuple-element.24.refs_8_.refs_3_, ...), custom_call_target="tpu_custom_call" | custom-call | flops 3000000000 | bytes 6000000 | tf_op jit(solution)/shard_map/pallas_call | solution.py:288
  53.5 0.7 %pad_maximum_fusion = f32[2,128,256]{2,1,0:T(8,128)} fusion(f32[1,128,256]{2,1,0:T(8,128)S(1)} %get-tuple-element.36, f32[1,128,256]{2,1,0:T(8,128)S(1)} %get-tuple-element.35), kind=kLoop, calls=%fused_computation | loop fusion | flops 65536 | bytes 524288 | tf_op jit(solution)/shard_map/stack | solution.py:407
  (27 shorter events, 0.6 us)
Async XLA Ops:
  0.0 31.0 %copy-start.4 = (f32[256,256]{1,0:T(8,128)S(1)}, f32[256,256]{1,0:T(8,128)}, u32[]{:S(2)}) copy-start(f32[256,256]{1,0:T(8,128)} %refs_2_.2) | copy-start | bytes 786436
  0.0 31.0 %copy-start.3 = (f32[256,256]{1,0:T(8,128)S(1)}, f32[256,256]{1,0:T(8,128)}, u32[]{:S(2)}) copy-start(f32[256,256]{1,0:T(8,128)} %refs_1_.2) | copy-start | bytes 786436
  0.0 0.9 %copy-start.7 = (f32[78,2,128]{2,1,0:T(2,128)S(1)}, f32[78,2,128]{2,1,0:T(2,128)}, u32[]{:S(2)}) copy-start(f32[78,2,128]{2,1,0:T(2,128)} %fields_ref.1) | copy-start | bytes 239620
  0.9 0.7 %copy-start.8 = (f32[2,128]{1,0:T(2,128)S(1)}, f32[2,128]{1,0:T(2,128)}, u32[]{:S(2)}) copy-start(f32[2,128]{1,0:T(2,128)} %kappa_ref.1) | copy-start | bytes 3076
  1.6 29.3 %copy-start.6 = (f32[78,256]{1,0:T(8,128)S(1)}, f32[78,256]{1,0:T(8,128)}, u32[]{:S(2)}) copy-start(f32[78,256]{1,0:T(8,128)} %refs_0_.2) | copy-start | bytes 239620
  1.7 11.9 %collective-permute-start.1 = (f32[2,80,128]{2,1,0:T(8,128)S(1)}, f32[2,80,128]{2,1,0:T(8,128)S(1)}, u32[]{:S(2)}, u32[]{:S(2)}) collective-permute-start(f32[2,80,128]{2,1,0:T(8,128)S(1)} %shard_map.91.both_ref), channel_id=1, source_target_pairs={{0,8},{1,9},{2,10},{3,11},{4,12},{5,13},{6,14},{7,15},{8,0},{9,1},... | collective-permute-start | bytes 245768 | tf_op jit(solution)/shard_map/ppermute | solution.py:312
  5.0 7.4 %collective-permute-start.2 = (f32[80,128]{1,0:T(8,128)S(1)}, f32[80,128]{1,0:T(8,128)S(1)}, u32[]{:S(2)}, u32[]{:S(2)}) collective-permute-start(f32[80,128]{1,0:T(8,128)S(1)} %get-tuple-element.37), channel_id=1, source_target_pairs={{8,16},{9,17},{10,18},{11,19},{12,20},{13,21},{14,22},{15,23},{16,... | collective-permute-start | bytes 122888 | tf_op jit(solution)/shard_map/ppermute | solution.py:335
  7.4 6.2 %collective-permute-start = (f32[80,128]{1,0:T(8,128)S(1)}, f32[80,128]{1,0:T(8,128)S(1)}, u32[]{:S(2)}, u32[]{:S(2)}) collective-permute-start(f32[80,128]{1,0:T(8,128)S(1)} %get-tuple-element.38), channel_id=1, source_target_pairs={{0,16},{1,17},{2,18},{3,19},{4,20},{5,21},{6,22},{7,23},{16,32},{1... | collective-permute-start | bytes 122888 | tf_op jit(solution)/shard_map/ppermute | solution.py:334
  14.3 14.1 %collective-permute-start.4 = (f32[2,80,128]{2,1,0:T(8,128)S(1)}, f32[2,80,128]{2,1,0:T(8,128)S(1)}, u32[]{:S(2)}, u32[]{:S(2)}) collective-permute-start(f32[2,80,128]{2,1,0:T(8,128)S(1)} %shard_map.92.refs_3_.refs_0_), channel_id=1, source_target_pairs={{0,7},{1,6},{2,5},{3,4},{4,3},{5,2},{6,1},{7,0},{8,15},{9,14},{10,... | collective-permute-start | bytes 245768 | tf_op jit(solution)/shard_map/ppermute | solution.py:312
  20.3 11.1 %collective-permute-start.9 = (f32[2,80,128]{2,1,0:T(8,128)S(1)}, f32[2,80,128]{2,1,0:T(8,128)S(1)}, u32[]{:S(2)}, u32[]{:S(2)}) collective-permute-start(f32[2,80,128]{2,1,0:T(8,128)S(1)} %shard_map.92.refs_3_.refs_0_), channel_id=1, source_target_pairs={{0,3},{1,2},{2,1},{3,0},{4,7},{5,6},{6,5},{7,4},{8,11},{9,10},{10,... | collective-permute-start | bytes 245768 | tf_op jit(solution)/shard_map/ppermute | solution.py:312
  22.2 11.4 %collective-permute-start.8 = (f32[2,80,128]{2,1,0:T(8,128)S(1)}, f32[2,80,128]{2,1,0:T(8,128)S(1)}, u32[]{:S(2)}, u32[]{:S(2)}) collective-permute-start(f32[2,80,128]{2,1,0:T(8,128)S(1)} %shard_map.92.refs_3_.refs_0_), channel_id=1, source_target_pairs={{0,1},{1,0},{2,3},{3,2},{4,5},{5,4},{6,7},{7,6},{8,9},{9,8},{10,11... | collective-permute-start | bytes 245768 | tf_op jit(solution)/shard_map/ppermute | solution.py:312
  23.2 16.8 %collective-permute-start.3 = (f32[2,80,128]{2,1,0:T(8,128)S(1)}, f32[2,80,128]{2,1,0:T(8,128)S(1)}, u32[]{:S(2)}, u32[]{:S(2)}) collective-permute-start(f32[2,80,128]{2,1,0:T(8,128)S(1)} %shard_map.92.refs_3_.refs_0_), channel_id=1, source_target_pairs={{0,2},{1,3},{2,0},{3,1},{4,6},{5,7},{6,4},{7,5},{8,10},{9,11},{10,... | collective-permute-start | bytes 245768 | tf_op jit(solution)/shard_map/ppermute | solution.py:312
  24.7 1.2 %copy-start = (f32[256,1024]{1,0:T(8,128)S(1)}, f32[256,1024]{1,0:T(8,128)}, u32[]{:S(2)}) copy-start(f32[256,1024]{1,0:T(8,128)} %refs_1_.3) | copy-start | bytes 3145732
  25.9 1.2 %copy-start.1 = (f32[1024,256]{1,0:T(8,128)S(1)}, f32[1024,256]{1,0:T(8,128)}, u32[]{:S(2)}) copy-start(f32[1024,256]{1,0:T(8,128)} %refs_2_.3) | copy-start | bytes 3145732
  27.1 0.9 %copy-start.2 = (f32[256,256]{1,0:T(8,128)S(1)}, f32[256,256]{1,0:T(8,128)}, u32[]{:S(2)}) copy-start(f32[256,256]{1,0:T(8,128)} %refs_0_.3) | copy-start | bytes 786436
  28.1 2.9 %copy-start.5 = (f32[256,256]{1,0:T(8,128)S(1)}, f32[256,256]{1,0:T(8,128)}, u32[]{:S(2)}) copy-start(f32[256,256]{1,0:T(8,128)} %refs_3_.1) | copy-start | bytes 786436
  28.4 11.6 %collective-permute-start.7 = (f32[2,80,128]{2,1,0:T(8,128)S(1)}, f32[2,80,128]{2,1,0:T(8,128)S(1)}, u32[]{:S(2)}, u32[]{:S(2)}) collective-permute-start(f32[2,80,128]{2,1,0:T(8,128)S(1)} %collective-permute-done.4.refs_4_.refs_3_), channel_id=1, source_target_pairs={{0,3},{1,2},{2,1},{3,0},{4,7},{5,6},{6,5},{7,4},{8,11},{9,10},{10,... | collective-permute-start | bytes 245768 | tf_op jit(solution)/shard_map/ppermute | solution.py:312
  30.4 9.6 %collective-permute-start.6 = (f32[2,80,128]{2,1,0:T(8,128)S(1)}, f32[2,80,128]{2,1,0:T(8,128)S(1)}, u32[]{:S(2)}, u32[]{:S(2)}) collective-permute-start(f32[2,80,128]{2,1,0:T(8,128)S(1)} %collective-permute-done.4.refs_4_.refs_3_), channel_id=1, source_target_pairs={{0,2},{1,3},{2,0},{3,1},{4,6},{5,7},{6,4},{7,5},{8,10},{9,11},{10,... | collective-permute-start | bytes 245768 | tf_op jit(solution)/shard_map/ppermute | solution.py:312
  31.4 8.6 %collective-permute-start.5 = (f32[2,80,128]{2,1,0:T(8,128)S(1)}, f32[2,80,128]{2,1,0:T(8,128)S(1)}, u32[]{:S(2)}, u32[]{:S(2)}) collective-permute-start(f32[2,80,128]{2,1,0:T(8,128)S(1)} %collective-permute-done.4.refs_4_.refs_3_), channel_id=1, source_target_pairs={{0,1},{1,0},{2,3},{3,2},{4,5},{5,4},{6,7},{7,6},{8,9},{9,8},{10,11... | collective-permute-start | bytes 245768 | tf_op jit(solution)/shard_map/ppermute | solution.py:312
  46.6 6.8 %collective-permute-start.10 = (f32[128,256]{1,0:T(8,128)S(1)}, f32[128,256]{1,0:T(8,128)S(1)}, u32[]{:S(2)}, u32[]{:S(2)}) collective-permute-start(f32[128,256]{1,0:T(8,128)S(1)} %get-tuple-element.34), channel_id=1, source_target_pairs={{0,8},{1,9},{2,10},{3,11},{4,12},{5,13},{6,14},{7,15},{8,0},{9,1},... | collective-permute-start | bytes 393224 | tf_op jit(solution)/shard_map/ppermute | solution.py:312

commit v5 on v4

--- a/solution.py
+++ b/solution.py
@@ -31,7 +31,9 @@
 
 
 def dot3(left, right):
-    return dot(left[0], right[0]) + dot(left[1], right[0]) + dot(left[0], right[1])
+    count = left[0].shape[0]
+    sums = dot(jnp.concatenate(left, axis=0), right[0])
+    return sums[:count] + sums[count:] + dot(left[0], right[1])
 
 
 def pack_kernel(fields_ref, kappa_ref, both_ref):
@@ -113,7 +115,7 @@
 def store_keys(normed, masked, start, qkv_high_ref, qkv_low_ref, key3, value3):
     count = masked.shape[1]
     tokens = slice(start, start + count)
-    high, low = split(dot3((qkv_high_ref[256:768], qkv_low_ref[256:768]), normed))
+    high, low = split(dot3((qkv_high_ref[256:768, :], qkv_low_ref[256:768, :]), normed))
     row = lax.broadcasted_iota(jnp.int32, (16, count), 0)
     mask = jnp.where(jnp.logical_and(masked, row == 0), -1e30, 0.0).astype(BF16)
     ones = jnp.ones((16, count), BF16)
@@ -143,8 +145,11 @@
         if starts is not None:
             largest = jnp.maximum(largest, starts(h))
         high, low = split(jnp.exp2(scores - largest))
-        sums = lax.dot_general(high, value3[h], nt, preferred_element_type=F32)
-        sums = sums + lax.dot_general(low, value3[h], nt, preferred_element_type=F32)
+        count = high.shape[0]
+        sums = lax.dot_general(
+            jnp.concatenate([high, low], axis=0), value3[h], nt, preferred_element_type=F32
+        )
+        sums = sums[:count] + sums[count:]
         found.append((largest, sums))
         scores = later
     return found

time: 54.5 us -> 54 us (level)
  transfers between devices with their start and end apart: 11 -> 11, of which waited for: 2 -> 2; matrix products, arithmetic and copies ran while one was open for 0% -> 0% of each run, Pallas kernels for 21% -> 20%
where the time goes in v5:
time: 54 us; the launch traced here: 53.7 us
  starting transfers between devices  25.1 us (46%)
  Pallas kernels  18.3 us (34%)
  local copies, waits for them, and re-layouts  5.04 us (9%)
  waiting for transfers between devices  4.18 us (8%)
  other arithmetic  0.86 us (2%)
    ppermute x9, starting transfers between devices, swap_lon(): return lax.ppermute(values, 'lon', [(r, r ^ mask) for r in range(count)])  20.9 us
    pallas_call x7, Pallas kernels, call(): pl.pallas_call(kernel, out_shape=outs, in_specs=[kinds[letter] for letter...  18.3 us
    unnamed x18, local copies, waits for them, and re-layouts  5.03 us
    ppermute x1, waiting for transfers between devices, on_device(): partner_outer = lax.ppermute(both[0], ('lat', 'lon'), crossing)  2.97 us
    ppermute x1, starting transfers between devices, on_device(): partner_outer = lax.ppermute(both[0], ('lat', 'lon'), crossing)  2.38 us
    ppermute x1, starting transfers between devices, on_device(): outer = lax.ppermute(both[1], ('lat', 'lon'), outward)  1.92 us
    ppermute x1, waiting for transfers between devices, on_device(): outer = lax.ppermute(both[1], ('lat', 'lon'), outward)  1.18 us
  transfers between devices with their start and end apart: 11, of which 2 were waited for; matrix products, arithmetic and copies ran while one was open for 0% of the time, Pallas kernels for 20%

profile of v5, /device:TPU:6, one launch (start us, length us, event | category | flops | bytes accessed | tf_op | source)
XLA Modules:
  0.0 53.7 jit_solution(5549412336535876145)
XLA Ops:
  0.0 0.9 %copy-done.7 = f32[78,2,128]{2,1,0:T(2,128)S(1)} copy-done((f32[78,2,128]{2,1,0:T(2,128)S(1)}, f32[78,2,128]{2,1,0:T(2,128)}, u32[]{:S(2)}) %copy-start.7) | copy-done | bytes 79896
  1.0 0.7 %copy-done.8 = f32[2,128]{1,0:T(2,128)S(1)} copy-done((f32[2,128]{1,0:T(2,128)S(1)}, f32[2,128]{1,0:T(2,128)}, u32[]{:S(2)}) %copy-start.8) | copy-done | bytes 1048
  1.7 3.3 %collective-permute-start.1 = (f32[2,80,128]{2,1,0:T(8,128)S(1)}, f32[2,80,128]{2,1,0:T(8,128)S(1)}, u32[]{:S(2)}, u32[]{:S(2)}) collective-permute-start(f32[2,80,128]{2,1,0:T(8,128)S(1)} %shard_map.91.both_ref), channel_id=1, source_target_pairs={{0,8},{1,9},{2,10},{3,11},{4,12},{5,13},{6,14},{7,15},{8,0},{9,1},... | collective-permute-start | bytes 245768 | tf_op jit(solution)/shard_map/ppermute | solution.py:317
  5.0 2.4 %collective-permute-start.2 = (f32[80,128]{1,0:T(8,128)S(1)}, f32[80,128]{1,0:T(8,128)S(1)}, u32[]{:S(2)}, u32[]{:S(2)}) collective-permute-start(f32[80,128]{1,0:T(8,128)S(1)} %get-tuple-element.37), channel_id=1, source_target_pairs={{8,16},{9,17},{10,18},{11,19},{12,20},{13,21},{14,22},{15,23},{16,... | collective-permute-start | bytes 122888 | tf_op jit(solution)/shard_map/ppermute | solution.py:340
  7.4 1.9 %collective-permute-start = (f32[80,128]{1,0:T(8,128)S(1)}, f32[80,128]{1,0:T(8,128)S(1)}, u32[]{:S(2)}, u32[]{:S(2)}) collective-permute-start(f32[80,128]{1,0:T(8,128)S(1)} %get-tuple-element.38), channel_id=1, source_target_pairs={{0,16},{1,17},{2,18},{3,19},{4,20},{5,21},{6,22},{7,23},{16,32},{1... | collective-permute-start | bytes 122888 | tf_op jit(solution)/shard_map/ppermute | solution.py:339
  9.4 3.0 %collective-permute-done.2.partner_outer_ref = f32[80,128]{1,0:T(8,128)S(1)} collective-permute-done((f32[80,128]{1,0:T(8,128)S(1)}, f32[80,128]{1,0:T(8,128)S(1)}, u32[]{:S(2)}, u32[]{:S(2)}) %collective-permute-start.2) | collective-permute-done | bytes 40992 | tf_op jit(solution)/shard_map/ppermute | solution.py:340
  12.4 1.2 %collective-permute-done.outer_ref = f32[80,128]{1,0:T(8,128)S(1)} collective-permute-done((f32[80,128]{1,0:T(8,128)S(1)}, f32[80,128]{1,0:T(8,128)S(1)}, u32[]{:S(2)}, u32[]{:S(2)}) %collective-permute-start) | collective-permute-done | bytes 40992 | tf_op jit(solution)/shard_map/ppermute | solution.py:339
  13.6 0.7 %shard_map.92.refs_3_.refs_0_ = f32[2,80,128]{2,1,0:T(8,128)S(1)} custom-call(f32[3]{0:T(128)S(1)} %multiply_cosine_fusion.cos_ref, f32[2,80,128]{2,1,0:T(8,128)S(1)} %shard_map.91.both_ref, f32[80,128]{1,0:T(8,128)S(1)} %collective-permute-done.outer_ref, f32[2,80,128]{2,1,0:T(8,128)S(1)} %collective-permute-done.1.partner_ref, ...), custom_call_target="tpu_custom_call" | custom-call | bytes 400000 | tf_op jit(solution)/shard_map/pallas_call | solution.py:293
  14.3 5.9 %collective-permute-start.4 = (f32[2,80,128]{2,1,0:T(8,128)S(1)}, f32[2,80,128]{2,1,0:T(8,128)S(1)}, u32[]{:S(2)}, u32[]{:S(2)}) collective-permute-start(f32[2,80,128]{2,1,0:T(8,128)S(1)} %shard_map.92.refs_3_.refs_0_), channel_id=1, source_target_pairs={{0,7},{1,6},{2,5},{3,4},{4,3},{5,2},{6,1},{7,0},{8,15},{9,14},{10,... | collective-permute-start | bytes 245768 | tf_op jit(solution)/shard_map/ppermute | solution.py:317
  20.3 1.9 %collective-permute-start.9 = (f32[2,80,128]{2,1,0:T(8,128)S(1)}, f32[2,80,128]{2,1,0:T(8,128)S(1)}, u32[]{:S(2)}, u32[]{:S(2)}) collective-permute-start(f32[2,80,128]{2,1,0:T(8,128)S(1)} %shard_map.92.refs_3_.refs_0_), channel_id=1, source_target_pairs={{0,3},{1,2},{2,1},{3,0},{4,7},{5,6},{6,5},{7,4},{8,11},{9,10},{10,... | collective-permute-start | bytes 245768 | tf_op jit(solution)/shard_map/ppermute | solution.py:317
  22.2 1.0 %collective-permute-start.8 = (f32[2,80,128]{2,1,0:T(8,128)S(1)}, f32[2,80,128]{2,1,0:T(8,128)S(1)}, u32[]{:S(2)}, u32[]{:S(2)}) collective-permute-start(f32[2,80,128]{2,1,0:T(8,128)S(1)} %shard_map.92.refs_3_.refs_0_), channel_id=1, source_target_pairs={{0,1},{1,0},{2,3},{3,2},{4,5},{5,4},{6,7},{7,6},{8,9},{9,8},{10,11... | collective-permute-start | bytes 245768 | tf_op jit(solution)/shard_map/ppermute | solution.py:317
  23.2 1.5 %collective-permute-start.3 = (f32[2,80,128]{2,1,0:T(8,128)S(1)}, f32[2,80,128]{2,1,0:T(8,128)S(1)}, u32[]{:S(2)}, u32[]{:S(2)}) collective-permute-start(f32[2,80,128]{2,1,0:T(8,128)S(1)} %shard_map.92.refs_3_.refs_0_), channel_id=1, source_target_pairs={{0,2},{1,3},{2,0},{3,1},{4,6},{5,7},{6,4},{7,5},{8,10},{9,11},{10,... | collective-permute-start | bytes 245768 | tf_op jit(solution)/shard_map/ppermute | solution.py:317
  24.7 1.2 %copy-done = f32[256,1024]{1,0:T(8,128)S(1)} copy-done((f32[256,1024]{1,0:T(8,128)S(1)}, f32[256,1024]{1,0:T(8,128)}, u32[]{:S(2)}) %copy-start) | copy-done | bytes 1048600
  25.9 1.2 %copy-done.1 = f32[1024,256]{1,0:T(8,128)S(1)} copy-done((f32[1024,256]{1,0:T(8,128)S(1)}, f32[1024,256]{1,0:T(8,128)}, u32[]{:S(2)}) %copy-start.1) | copy-done | bytes 1048600
  27.1 0.9 %copy-done.2 = f32[256,256]{1,0:T(8,128)S(1)} copy-done((f32[256,256]{1,0:T(8,128)S(1)}, f32[256,256]{1,0:T(8,128)}, u32[]{:S(2)}) %copy-start.2) | copy-done | bytes 262168
  28.4 2.0 %collective-permute-start.7 = (f32[2,80,128]{2,1,0:T(8,128)S(1)}, f32[2,80,128]{2,1,0:T(8,128)S(1)}, u32[]{:S(2)}, u32[]{:S(2)}) collective-permute-start(f32[2,80,128]{2,1,0:T(8,128)S(1)} %collective-permute-done.4.refs_4_.refs_3_), channel_id=1, source_target_pairs={{0,3},{1,2},{2,1},{3,0},{4,7},{5,6},{6,5},{7,4},{8,11},{9,10},{10,... | collective-permute-start | bytes 245768 | tf_op jit(solution)/shard_map/ppermute | solution.py:317
  30.4 0.6 %collective-permute-start.6 = (f32[2,80,128]{2,1,0:T(8,128)S(1)}, f32[2,80,128]{2,1,0:T(8,128)S(1)}, u32[]{:S(2)}, u32[]{:S(2)}) collective-permute-start(f32[2,80,128]{2,1,0:T(8,128)S(1)} %collective-permute-done.4.refs_4_.refs_3_), channel_id=1, source_target_pairs={{0,2},{1,3},{2,0},{3,1},{4,6},{5,7},{6,4},{7,5},{8,10},{9,11},{10,... | collective-permute-start | bytes 245768 | tf_op jit(solution)/shard_map/ppermute | solution.py:317
  31.0 0.4 shard_map.93
  31.4 2.2 %collective-permute-start.5 = (f32[2,80,128]{2,1,0:T(8,128)S(1)}, f32[2,80,128]{2,1,0:T(8,128)S(1)}, u32[]{:S(2)}, u32[]{:S(2)}) collective-permute-start(f32[2,80,128]{2,1,0:T(8,128)S(1)} %collective-permute-done.4.refs_4_.refs_3_), channel_id=1, source_target_pairs={{0,1},{1,0},{2,3},{3,2},{4,5},{5,4},{6,7},{7,6},{8,9},{9,8},{10,11... | collective-permute-start | bytes 245768 | tf_op jit(solution)/shard_map/ppermute | solution.py:317
  33.6 6.0 %shard_map.95 = (f32[256,256]{1,0:T(8,128)S(1)}, bf16[8,256,112]{2,1,0:T(8,128)(2,1)S(1)}, f32[8,256,128]{2,1,0:T(8,128)S(1)}, f32[80,128]{1,0:T(8,128)S(1)}, f32[16,2,128]{2,1,0:T(2,128)S(1)}) custom-call(f32[3]{0:T(128)S(1)} %multiply_cosine_fusion.cos_ref, f32[2,80,128]{2,1,0:T(8,128)S(1)} %shard_map.92.refs_3_.refs_0_, ...), custom_call_target="tpu_custom_call" | custom-call | flops 5000000000 | bytes 3000000 | tf_op jit(solution)/shard_map/pallas_call | solution.py:293
  39.7 6.5 %shard_map.96 = (f32[128,256]{1,0:T(8,128)S(1)}, bf16[8,112,1152]{2,1,0:T(8,128)(2,1)S(1)}, bf16[8,80,1152]{2,1,0:T(8,128)(2,1)S(1)}) custom-call(f32[3]{0:T(128)S(1)} %multiply_cosine_fusion.cos_ref, f32[2,80,128]{2,1,0:T(8,128)S(1)} %collective-permute-done.3.refs_0_, f32[2,80,128]{2,1,0:T(8,128)S(1)} %collective-permute-done.5.refs_1_, ...), custom_call_target="tpu_custom_call" | custom-call | flops 5000000000 | bytes 6000000 | tf_op jit(solution)/shard_map/pallas_call | solution.py:293
  46.1 2.5 %collective-permute-start.10 = (f32[128,256]{1,0:T(8,128)S(1)}, f32[128,256]{1,0:T(8,128)S(1)}, u32[]{:S(2)}, u32[]{:S(2)}) collective-permute-start(f32[128,256]{1,0:T(8,128)S(1)} %get-tuple-element.34), channel_id=1, source_target_pairs={{0,8},{1,9},{2,10},{3,11},{4,12},{5,13},{6,14},{7,15},{8,0},{9,1},... | collective-permute-start | bytes 393224 | tf_op jit(solution)/shard_map/ppermute | solution.py:317
  48.6 4.3 %shard_map.97 = f32[128,256]{1,0:T(8,128)S(1)} custom-call(bf16[8,112,1152]{2,1,0:T(8,128)(2,1)S(1)} %get-tuple-element.32.refs_0_, bf16[8,80,1152]{2,1,0:T(8,128)(2,1)S(1)} %get-tuple-element.33.refs_1_, bf16[2,256,256]{2,1,0:T(8,128)(2,1)S(1)} %get-tuple-element.23.refs_7_.refs_2_, bf16[2,256,1024]{2,1,0:T(8,128)(2,1)S(1)} %get-tuple-element.24.refs_8_.refs_3_, ...), custom_call_target="tpu_custom_call" | custom-call | flops 3000000000 | bytes 6000000 | tf_op jit(solution)/shard_map/pallas_call | solution.py:293
  53.0 0.7 %pad_maximum_fusion = f32[2,128,256]{2,1,0:T(8,128)} fusion(f32[1,128,256]{2,1,0:T(8,128)S(1)} %get-tuple-element.36, f32[1,128,256]{2,1,0:T(8,128)S(1)} %get-tuple-element.35), kind=kLoop, calls=%fused_computation | loop fusion | flops 65536 | bytes 524288 | tf_op jit(solution)/shard_map/stack | solution.py:412
  (27 shorter events, 0.6 us)
Async XLA Ops:
  0.0 31.0 %copy-start.4 = (f32[256,256]{1,0:T(8,128)S(1)}, f32[256,256]{1,0:T(8,128)}, u32[]{:S(2)}) copy-start(f32[256,256]{1,0:T(8,128)} %refs_2_.2) | copy-start | bytes 786436
  0.0 31.0 %copy-start.3 = (f32[256,256]{1,0:T(8,128)S(1)}, f32[256,256]{1,0:T(8,128)}, u32[]{:S(2)}) copy-start(f32[256,256]{1,0:T(8,128)} %refs_1_.2) | copy-start | bytes 786436
  0.0 0.9 %copy-start.7 = (f32[78,2,128]{2,1,0:T(2,128)S(1)}, f32[78,2,128]{2,1,0:T(2,128)}, u32[]{:S(2)}) copy-start(f32[78,2,128]{2,1,0:T(2,128)} %fields_ref.1) | copy-start | bytes 239620
  0.9 0.7 %copy-start.8 = (f32[2,128]{1,0:T(2,128)S(1)}, f32[2,128]{1,0:T(2,128)}, u32[]{:S(2)}) copy-start(f32[2,128]{1,0:T(2,128)} %kappa_ref.1) | copy-start | bytes 3076
  1.6 29.3 %copy-start.6 = (f32[78,256]{1,0:T(8,128)S(1)}, f32[78,256]{1,0:T(8,128)}, u32[]{:S(2)}) copy-start(f32[78,256]{1,0:T(8,128)} %refs_0_.2) | copy-start | bytes 239620
  1.7 11.9 %collective-permute-start.1 = (f32[2,80,128]{2,1,0:T(8,128)S(1)}, f32[2,80,128]{2,1,0:T(8,128)S(1)}, u32[]{:S(2)}, u32[]{:S(2)}) collective-permute-start(f32[2,80,128]{2,1,0:T(8,128)S(1)} %shard_map.91.both_ref), channel_id=1, source_target_pairs={{0,8},{1,9},{2,10},{3,11},{4,12},{5,13},{6,14},{7,15},{8,0},{9,1},... | collective-permute-start | bytes 245768 | tf_op jit(solution)/shard_map/ppermute | solution.py:317
  5.0 7.4 %collective-permute-start.2 = (f32[80,128]{1,0:T(8,128)S(1)}, f32[80,128]{1,0:T(8,128)S(1)}, u32[]{:S(2)}, u32[]{:S(2)}) collective-permute-start(f32[80,128]{1,0:T(8,128)S(1)} %get-tuple-element.37), channel_id=1, source_target_pairs={{8,16},{9,17},{10,18},{11,19},{12,20},{13,21},{14,22},{15,23},{16,... | collective-permute-start | bytes 122888 | tf_op jit(solution)/shard_map/ppermute | solution.py:340
  7.4 6.2 %collective-permute-start = (f32[80,128]{1,0:T(8,128)S(1)}, f32[80,128]{1,0:T(8,128)S(1)}, u32[]{:S(2)}, u32[]{:S(2)}) collective-permute-start(f32[80,128]{1,0:T(8,128)S(1)} %get-tuple-element.38), channel_id=1, source_target_pairs={{0,16},{1,17},{2,18},{3,19},{4,20},{5,21},{6,22},{7,23},{16,32},{1... | collective-permute-start | bytes 122888 | tf_op jit(solution)/shard_map/ppermute | solution.py:339
  14.3 14.1 %collective-permute-start.4 = (f32[2,80,128]{2,1,0:T(8,128)S(1)}, f32[2,80,128]{2,1,0:T(8,128)S(1)}, u32[]{:S(2)}, u32[]{:S(2)}) collective-permute-start(f32[2,80,128]{2,1,0:T(8,128)S(1)} %shard_map.92.refs_3_.refs_0_), channel_id=1, source_target_pairs={{0,7},{1,6},{2,5},{3,4},{4,3},{5,2},{6,1},{7,0},{8,15},{9,14},{10,... | collective-permute-start | bytes 245768 | tf_op jit(solution)/shard_map/ppermute | solution.py:317
  20.3 11.1 %collective-permute-start.9 = (f32[2,80,128]{2,1,0:T(8,128)S(1)}, f32[2,80,128]{2,1,0:T(8,128)S(1)}, u32[]{:S(2)}, u32[]{:S(2)}) collective-permute-start(f32[2,80,128]{2,1,0:T(8,128)S(1)} %shard_map.92.refs_3_.refs_0_), channel_id=1, source_target_pairs={{0,3},{1,2},{2,1},{3,0},{4,7},{5,6},{6,5},{7,4},{8,11},{9,10},{10,... | collective-permute-start | bytes 245768 | tf_op jit(solution)/shard_map/ppermute | solution.py:317
  22.2 11.4 %collective-permute-start.8 = (f32[2,80,128]{2,1,0:T(8,128)S(1)}, f32[2,80,128]{2,1,0:T(8,128)S(1)}, u32[]{:S(2)}, u32[]{:S(2)}) collective-permute-start(f32[2,80,128]{2,1,0:T(8,128)S(1)} %shard_map.92.refs_3_.refs_0_), channel_id=1, source_target_pairs={{0,1},{1,0},{2,3},{3,2},{4,5},{5,4},{6,7},{7,6},{8,9},{9,8},{10,11... | collective-permute-start | bytes 245768 | tf_op jit(solution)/shard_map/ppermute | solution.py:317
  23.2 16.4 %collective-permute-start.3 = (f32[2,80,128]{2,1,0:T(8,128)S(1)}, f32[2,80,128]{2,1,0:T(8,128)S(1)}, u32[]{:S(2)}, u32[]{:S(2)}) collective-permute-start(f32[2,80,128]{2,1,0:T(8,128)S(1)} %shard_map.92.refs_3_.refs_0_), channel_id=1, source_target_pairs={{0,2},{1,3},{2,0},{3,1},{4,6},{5,7},{6,4},{7,5},{8,10},{9,11},{10,... | collective-permute-start | bytes 245768 | tf_op jit(solution)/shard_map/ppermute | solution.py:317
  24.7 1.2 %copy-start = (f32[256,1024]{1,0:T(8,128)S(1)}, f32[256,1024]{1,0:T(8,128)}, u32[]{:S(2)}) copy-start(f32[256,1024]{1,0:T(8,128)} %refs_1_.3) | copy-start | bytes 3145732
  25.9 1.2 %copy-start.1 = (f32[1024,256]{1,0:T(8,128)S(1)}, f32[1024,256]{1,0:T(8,128)}, u32[]{:S(2)}) copy-start(f32[1024,256]{1,0:T(8,128)} %refs_2_.3) | copy-start | bytes 3145732
  27.1 0.9 %copy-start.2 = (f32[256,256]{1,0:T(8,128)S(1)}, f32[256,256]{1,0:T(8,128)}, u32[]{:S(2)}) copy-start(f32[256,256]{1,0:T(8,128)} %refs_0_.3) | copy-start | bytes 786436
  28.1 2.9 %copy-start.5 = (f32[256,256]{1,0:T(8,128)S(1)}, f32[256,256]{1,0:T(8,128)}, u32[]{:S(2)}) copy-start(f32[256,256]{1,0:T(8,128)} %refs_3_.1) | copy-start | bytes 786436
  28.4 11.2 %collective-permute-start.7 = (f32[2,80,128]{2,1,0:T(8,128)S(1)}, f32[2,80,128]{2,1,0:T(8,128)S(1)}, u32[]{:S(2)}, u32[]{:S(2)}) collective-permute-start(f32[2,80,128]{2,1,0:T(8,128)S(1)} %collective-permute-done.4.refs_4_.refs_3_), channel_id=1, source_target_pairs={{0,3},{1,2},{2,1},{3,0},{4,7},{5,6},{6,5},{7,4},{8,11},{9,10},{10,... | collective-permute-start | bytes 245768 | tf_op jit(solution)/shard_map/ppermute | solution.py:317
  30.4 9.2 %collective-permute-start.6 = (f32[2,80,128]{2,1,0:T(8,128)S(1)}, f32[2,80,128]{2,1,0:T(8,128)S(1)}, u32[]{:S(2)}, u32[]{:S(2)}) collective-permute-start(f32[2,80,128]{2,1,0:T(8,128)S(1)} %collective-permute-done.4.refs_4_.refs_3_), channel_id=1, source_target_pairs={{0,2},{1,3},{2,0},{3,1},{4,6},{5,7},{6,4},{7,5},{8,10},{9,11},{10,... | collective-permute-start | bytes 245768 | tf_op jit(solution)/shard_map/ppermute | solution.py:317
  31.4 8.2 %collective-permute-start.5 = (f32[2,80,128]{2,1,0:T(8,128)S(1)}, f32[2,80,128]{2,1,0:T(8,128)S(1)}, u32[]{:S(2)}, u32[]{:S(2)}) collective-permute-start(f32[2,80,128]{2,1,0:T(8,128)S(1)} %collective-permute-done.4.refs_4_.refs_3_), channel_id=1, source_target_pairs={{0,1},{1,0},{2,3},{3,2},{4,5},{5,4},{6,7},{7,6},{8,9},{9,8},{10,11... | collective-permute-start | bytes 245768 | tf_op jit(solution)/shard_map/ppermute | solution.py:317
  46.1 6.8 %collective-permute-start.10 = (f32[128,256]{1,0:T(8,128)S(1)}, f32[128,256]{1,0:T(8,128)S(1)}, u32[]{:S(2)}, u32[]{:S(2)}) collective-permute-start(f32[128,256]{1,0:T(8,128)S(1)} %get-tuple-element.34), channel_id=1, source_target_pairs={{0,8},{1,9},{2,10},{3,11},{4,12},{5,13},{6,14},{7,15},{8,0},{9,1},... | collective-permute-start | bytes 393224 | tf_op jit(solution)/shard_map/ppermute | solution.py:317

commit v6 on v5

--- a/solution.py
+++ b/solution.py
@@ -96,7 +96,6 @@
         high, low = split(source[...])
         target[0] = high
         target[1] = low
-    refs[7][...] = jnp.zeros_like(refs[7])
 
 
 def layer_norm(values, axis):
@@ -164,8 +163,8 @@
 def early_kernel(cos_ref, *refs):
     pieces = refs[:4]
     embed3_ref, qkv_high_ref, qkv_low_ref = refs[4:7]
-    hidden_ref, query3_ref, state_ref, columns_ref, edges_ref = refs[8:13]
-    key3, value3 = refs[13:]
+    hidden_ref, query3_ref, state_ref, columns_ref, edges_ref = refs[7:12]
+    key3, value3 = refs[12:]
     z = lax.axis_index("lon") % 8
     inverse = 1.0 / cos_ref[0]
     step = 0.5 * STEP_SIZE * inverse * inverse
@@ -352,23 +351,10 @@
     first = call(
         first_weights_kernel,
         (shape(256, 3 * ROWS, dtype=BF16), shape(768, 256, dtype=BF16), shape(768, 256, dtype=BF16)),
-        (w_embed, query_weight, key_weight, value_weight, far),
+        (w_embed, query_weight, key_weight, value_weight, both),
         "vvvvh",
         limit=8 * 2**20,
         moved=2000000,
-    )
-    *last, order = call(
-        last_weights_kernel,
-        (
-            shape(2, 256, 256, dtype=BF16),
-            shape(2, 256, 1024, dtype=BF16),
-            shape(2, 1024, 256, dtype=BF16),
-            shape(8, 128),
-        ),
-        (out_weight, up_weight, down_weight, chunk),
-        "vvvh",
-        limit=12 * 2**20,
-        moved=5000000,
     )
     early = call(
         early_kernel,
@@ -379,12 +365,24 @@
             plane,
             shape(16, 2, 128),
         ),
-        (cosines, chunk, near[0], near[2], far, *first, order),
-        "s" + 7 * "v" + "h",
+        (cosines, chunk, near[0], near[2], far, *first),
+        "s" + 7 * "v",
         scratch=[pltpu.VMEM((HEADS, 112, 1024), BF16), pltpu.VMEM((HEADS, 80, 1024), BF16)],
         limit=40 * 2**20,
         flops=5 * 10**9,
         moved=3000000,
+    )
+    last = call(
+        last_weights_kernel,
+        (
+            shape(2, 256, 256, dtype=BF16),
+            shape(2, 256, 1024, dtype=BF16),
+            shape(2, 1024, 256, dtype=BF16),
+        ),
+        (out_weight, up_weight, down_weight, early[3]),
+        "vvvh",
+        limit=12 * 2**20,
+        moved=5000000,
     )
     tile = shape(128, 256)
     send, *keys = call(

time: 54 us -> 54.3 us (level)
  transfers between devices with their start and end apart: 11 -> 11, of which waited for: 2 -> 2; matrix products, arithmetic and copies ran while one was open for 0% -> 0% of each run, Pallas kernels for 20% -> 21%
where the time goes in v6:
time: 54.3 us; the launch traced here: 54 us
  starting transfers between devices  25 us (46%)
  Pallas kernels  18.5 us (34%)
  local copies, waits for them, and re-layouts  5.32 us (10%)
  waiting for transfers between devices  4.17 us (8%)
  other arithmetic  0.86 us (2%)
    ppermute x9, starting transfers between devices, swap_lon(): return lax.ppermute(values, 'lon', [(r, r ^ mask) for r in range(count)])  20.7 us
    pallas_call x7, Pallas kernels, call(): pl.pallas_call(kernel, out_shape=outs, in_specs=[kinds[letter] for letter...  18.5 us
    unnamed x18, local copies, waits for them, and re-layouts  5.31 us
    ppermute x1, waiting for transfers between devices, on_device(): partner_outer = lax.ppermute(both[0], ('lat', 'lon'), crossing)  2.97 us
    ppermute x1, starting transfers between devices, on_device(): partner_outer = lax.ppermute(both[0], ('lat', 'lon'), crossing)  2.38 us
    ppermute x1, starting transfers between devices, on_device(): outer = lax.ppermute(both[1], ('lat', 'lon'), outward)  1.92 us
    ppermute x1, waiting for transfers between devices, on_device(): outer = lax.ppermute(both[1], ('lat', 'lon'), outward)  1.18 us
  transfers between devices with their start and end apart: 11, of which 2 were waited for; matrix products, arithmetic and copies ran while one was open for 0% of the time, Pallas kernels for 21%

profile of v6, /device:TPU:6, one launch (start us, length us, event | category | flops | bytes accessed | tf_op | source)
XLA Modules:
  0.0 54.0 jit_solution(12136325242694011276)
XLA Ops:
  0.0 0.9 %copy-done.7 = f32[78,2,128]{2,1,0:T(2,128)S(1)} copy-done((f32[78,2,128]{2,1,0:T(2,128)S(1)}, f32[78,2,128]{2,1,0:T(2,128)}, u32[]{:S(2)}) %copy-start.7) | copy-done | bytes 79896
  0.9 0.7 %copy-done.8 = f32[2,128]{1,0:T(2,128)S(1)} copy-done((f32[2,128]{1,0:T(2,128)S(1)}, f32[2,128]{1,0:T(2,128)}, u32[]{:S(2)}) %copy-start.8) | copy-done | bytes 1048
  1.6 3.3 %collective-permute-start.1 = (f32[2,80,128]{2,1,0:T(8,128)S(1)}, f32[2,80,128]{2,1,0:T(8,128)S(1)}, u32[]{:S(2)}, u32[]{:S(2)}) collective-permute-start(f32[2,80,128]{2,1,0:T(8,128)S(1)} %shard_map.91.both_ref.refs_4_), channel_id=1, source_target_pairs={{0,8},{1,9},{2,10},{3,11},{4,12},{5,13},{6,14},{7,15},{8,0},{9,1},... | collective-permute-start | bytes 245768 | tf_op jit(solution)/shard_map/ppermute | solution.py:316
  4.9 2.4 %collective-permute-start.2 = (f32[80,128]{1,0:T(8,128)S(1)}, f32[80,128]{1,0:T(8,128)S(1)}, u32[]{:S(2)}, u32[]{:S(2)}) collective-permute-start(f32[80,128]{1,0:T(8,128)S(1)} %get-tuple-element.35), channel_id=1, source_target_pairs={{8,16},{9,17},{10,18},{11,19},{12,20},{13,21},{14,22},{15,23},{16,... | collective-permute-start | bytes 122888 | tf_op jit(solution)/shard_map/ppermute | solution.py:339
  7.3 1.9 %collective-permute-start = (f32[80,128]{1,0:T(8,128)S(1)}, f32[80,128]{1,0:T(8,128)S(1)}, u32[]{:S(2)}, u32[]{:S(2)}) collective-permute-start(f32[80,128]{1,0:T(8,128)S(1)} %get-tuple-element.36), channel_id=1, source_target_pairs={{0,16},{1,17},{2,18},{3,19},{4,20},{5,21},{6,22},{7,23},{16,32},{1... | collective-permute-start | bytes 122888 | tf_op jit(solution)/shard_map/ppermute | solution.py:338
  9.4 3.0 %collective-permute-done.2.partner_outer_ref = f32[80,128]{1,0:T(8,128)S(1)} collective-permute-done((f32[80,128]{1,0:T(8,128)S(1)}, f32[80,128]{1,0:T(8,128)S(1)}, u32[]{:S(2)}, u32[]{:S(2)}) %collective-permute-start.2) | collective-permute-done | bytes 40992 | tf_op jit(solution)/shard_map/ppermute | solution.py:339
  12.3 1.2 %collective-permute-done.outer_ref = f32[80,128]{1,0:T(8,128)S(1)} collective-permute-done((f32[80,128]{1,0:T(8,128)S(1)}, f32[80,128]{1,0:T(8,128)S(1)}, u32[]{:S(2)}, u32[]{:S(2)}) %collective-permute-start) | collective-permute-done | bytes 40992 | tf_op jit(solution)/shard_map/ppermute | solution.py:338
  13.5 0.7 %shard_map.92.refs_0_ = f32[2,80,128]{2,1,0:T(8,128)S(1)} custom-call(f32[3]{0:T(128)S(1)} %multiply_cosine_fusion.cos_ref, f32[2,80,128]{2,1,0:T(8,128)S(1)} %shard_map.91.both_ref.refs_4_, f32[80,128]{1,0:T(8,128)S(1)} %collective-permute-done.outer_ref, f32[2,80,128]{2,1,0:T(8,128)S(1)} %collective-permute-done.1.partner_ref, ...), custom_call_target="tpu_custom_call" | custom-call | bytes 400000 | tf_op jit(solution)/shard_map/pallas_call | solution.py:292
  14.3 5.9 %collective-permute-start.4 = (f32[2,80,128]{2,1,0:T(8,128)S(1)}, f32[2,80,128]{2,1,0:T(8,128)S(1)}, u32[]{:S(2)}, u32[]{:S(2)}) collective-permute-start(f32[2,80,128]{2,1,0:T(8,128)S(1)} %shard_map.92.refs_0_), channel_id=1, source_target_pairs={{0,7},{1,6},{2,5},{3,4},{4,3},{5,2},{6,1},{7,0},{8,15},{9,14},{10,... | collective-permute-start | bytes 245768 | tf_op jit(solution)/shard_map/ppermute | solution.py:316
  20.2 1.9 %collective-permute-start.9 = (f32[2,80,128]{2,1,0:T(8,128)S(1)}, f32[2,80,128]{2,1,0:T(8,128)S(1)}, u32[]{:S(2)}, u32[]{:S(2)}) collective-permute-start(f32[2,80,128]{2,1,0:T(8,128)S(1)} %shard_map.92.refs_0_), channel_id=1, source_target_pairs={{0,3},{1,2},{2,1},{3,0},{4,7},{5,6},{6,5},{7,4},{8,11},{9,10},{10,... | collective-permute-start | bytes 245768 | tf_op jit(solution)/shard_map/ppermute | solution.py:316
  22.1 1.0 %collective-permute-start.8 = (f32[2,80,128]{2,1,0:T(8,128)S(1)}, f32[2,80,128]{2,1,0:T(8,128)S(1)}, u32[]{:S(2)}, u32[]{:S(2)}) collective-permute-start(f32[2,80,128]{2,1,0:T(8,128)S(1)} %shard_map.92.refs_0_), channel_id=1, source_target_pairs={{0,1},{1,0},{2,3},{3,2},{4,5},{5,4},{6,7},{7,6},{8,9},{9,8},{10,11... | collective-permute-start | bytes 245768 | tf_op jit(solution)/shard_map/ppermute | solution.py:316
  23.1 0.9 %copy-done.3 = f32[256,256]{1,0:T(8,128)S(1)} copy-done((f32[256,256]{1,0:T(8,128)S(1)}, f32[256,256]{1,0:T(8,128)}, u32[]{:S(2)}) %copy-start.3) | copy-done | bytes 262168
  24.1 0.9 %copy-done.4 = f32[256,256]{1,0:T(8,128)S(1)} copy-done((f32[256,256]{1,0:T(8,128)S(1)}, f32[256,256]{1,0:T(8,128)}, u32[]{:S(2)}) %copy-start.4) | copy-done | bytes 262168
  25.0 0.9 %copy-done.5 = f32[256,256]{1,0:T(8,128)S(1)} copy-done((f32[256,256]{1,0:T(8,128)S(1)}, f32[256,256]{1,0:T(8,128)}, u32[]{:S(2)}) %copy-start.5) | copy-done | bytes 262168
  26.0 0.9 %copy-done.6 = f32[78,256]{1,0:T(8,128)S(1)} copy-done((f32[78,256]{1,0:T(8,128)S(1)}, f32[78,256]{1,0:T(8,128)}, u32[]{:S(2)}) %copy-start.6) | copy-done | bytes 79896
  27.3 1.6 %collective-permute-start.3 = (f32[2,80,128]{2,1,0:T(8,128)S(1)}, f32[2,80,128]{2,1,0:T(8,128)S(1)}, u32[]{:S(2)}, u32[]{:S(2)}) collective-permute-start(f32[2,80,128]{2,1,0:T(8,128)S(1)} %shard_map.92.refs_0_), channel_id=1, source_target_pairs={{0,2},{1,3},{2,0},{3,1},{4,6},{5,7},{6,4},{7,5},{8,10},{9,11},{10,... | collective-permute-start | bytes 245768 | tf_op jit(solution)/shard_map/ppermute | solution.py:316
  28.8 1.9 %collective-permute-start.7 = (f32[2,80,128]{2,1,0:T(8,128)S(1)}, f32[2,80,128]{2,1,0:T(8,128)S(1)}, u32[]{:S(2)}, u32[]{:S(2)}) collective-permute-start(f32[2,80,128]{2,1,0:T(8,128)S(1)} %collective-permute-done.4.refs_3_), channel_id=1, source_target_pairs={{0,3},{1,2},{2,1},{3,0},{4,7},{5,6},{6,5},{7,4},{8,11},{9,10},{10,... | collective-permute-start | bytes 245768 | tf_op jit(solution)/shard_map/ppermute | solution.py:316
  30.7 0.6 %collective-permute-start.6 = (f32[2,80,128]{2,1,0:T(8,128)S(1)}, f32[2,80,128]{2,1,0:T(8,128)S(1)}, u32[]{:S(2)}, u32[]{:S(2)}) collective-permute-start(f32[2,80,128]{2,1,0:T(8,128)S(1)} %collective-permute-done.4.refs_3_), channel_id=1, source_target_pairs={{0,2},{1,3},{2,0},{3,1},{4,6},{5,7},{6,4},{7,5},{8,10},{9,11},{10,... | collective-permute-start | bytes 245768 | tf_op jit(solution)/shard_map/ppermute | solution.py:316
  31.3 1.9 %collective-permute-start.5 = (f32[2,80,128]{2,1,0:T(8,128)S(1)}, f32[2,80,128]{2,1,0:T(8,128)S(1)}, u32[]{:S(2)}, u32[]{:S(2)}) collective-permute-start(f32[2,80,128]{2,1,0:T(8,128)S(1)} %collective-permute-done.4.refs_3_), channel_id=1, source_target_pairs={{0,1},{1,0},{2,3},{3,2},{4,5},{5,4},{6,7},{7,6},{8,9},{9,8},{10,11... | collective-permute-start | bytes 245768 | tf_op jit(solution)/shard_map/ppermute | solution.py:316
  33.2 6.1 %shard_map.94 = (f32[256,256]{1,0:T(8,128)S(1)}, bf16[8,256,112]{2,1,0:T(8,128)(2,1)S(1)}, f32[8,256,128]{2,1,0:T(8,128)S(1)}, f32[80,128]{1,0:T(8,128)S(1)}, f32[16,2,128]{2,1,0:T(2,128)S(1)}) custom-call(f32[3]{0:T(128)S(1)} %multiply_cosine_fusion.cos_ref, f32[2,80,128]{2,1,0:T(8,128)S(1)} %shard_map.92.refs_0_, ...), custom_call_target="tpu_custom_call" | custom-call | flops 5000000000 | bytes 3000000 | tf_op jit(solution)/shard_map/pallas_call | solution.py:292
  39.7 6.6 %shard_map.96 = (f32[128,256]{1,0:T(8,128)S(1)}, bf16[8,112,1152]{2,1,0:T(8,128)(2,1)S(1)}, bf16[8,80,1152]{2,1,0:T(8,128)(2,1)S(1)}) custom-call(f32[3]{0:T(128)S(1)} %multiply_cosine_fusion.cos_ref, f32[2,80,128]{2,1,0:T(8,128)S(1)} %collective-permute-done.3.refs_0_, f32[2,80,128]{2,1,0:T(8,128)S(1)} %collective-permute-done.5.refs_1_, ...), custom_call_target="tpu_custom_call" | custom-call | flops 5000000000 | bytes 6000000 | tf_op jit(solution)/shard_map/pallas_call | solution.py:292
  46.3 2.6 %collective-permute-start.10 = (f32[128,256]{1,0:T(8,128)S(1)}, f32[128,256]{1,0:T(8,128)S(1)}, u32[]{:S(2)}, u32[]{:S(2)}) collective-permute-start(f32[128,256]{1,0:T(8,128)S(1)} %get-tuple-element.32), channel_id=1, source_target_pairs={{0,8},{1,9},{2,10},{3,11},{4,12},{5,13},{6,14},{7,15},{8,0},{9,1},... | collective-permute-start | bytes 393224 | tf_op jit(solution)/shard_map/ppermute | solution.py:316
  48.9 4.3 %shard_map.97 = f32[128,256]{1,0:T(8,128)S(1)} custom-call(bf16[8,112,1152]{2,1,0:T(8,128)(2,1)S(1)} %get-tuple-element.30.refs_0_, bf16[8,80,1152]{2,1,0:T(8,128)(2,1)S(1)} %get-tuple-element.31.refs_1_, bf16[2,256,256]{2,1,0:T(8,128)(2,1)S(1)} %get-tuple-element.23.refs_7_.refs_2_, bf16[2,256,1024]{2,1,0:T(8,128)(2,1)S(1)} %get-tuple-element.24.refs_8_.refs_3_, ...), custom_call_target="tpu_custom_call" | custom-call | flops 3000000000 | bytes 6000000 | tf_op jit(solution)/shard_map/pallas_call | solution.py:292
  53.3 0.7 %pad_maximum_fusion = f32[2,128,256]{2,1,0:T(8,128)} fusion(f32[1,128,256]{2,1,0:T(8,128)S(1)} %get-tuple-element.34, f32[1,128,256]{2,1,0:T(8,128)S(1)} %get-tuple-element.33), kind=kLoop, calls=%fused_computation | loop fusion | flops 65536 | bytes 524288 | tf_op jit(solution)/shard_map/stack | solution.py:410
  (27 shorter events, 1.0 us)
Async XLA Ops:
  0.0 0.9 %copy-start.7 = (f32[78,2,128]{2,1,0:T(2,128)S(1)}, f32[78,2,128]{2,1,0:T(2,128)}, u32[]{:S(2)}) copy-start(f32[78,2,128]{2,1,0:T(2,128)} %fields_ref.1) | copy-start | bytes 239620
  0.9 0.7 %copy-start.8 = (f32[2,128]{1,0:T(2,128)S(1)}, f32[2,128]{1,0:T(2,128)}, u32[]{:S(2)}) copy-start(f32[2,128]{1,0:T(2,128)} %kappa_ref.1) | copy-start | bytes 3076
  1.6 11.9 %collective-permute-start.1 = (f32[2,80,128]{2,1,0:T(8,128)S(1)}, f32[2,80,128]{2,1,0:T(8,128)S(1)}, u32[]{:S(2)}, u32[]{:S(2)}) collective-permute-start(f32[2,80,128]{2,1,0:T(8,128)S(1)} %shard_map.91.both_ref.refs_4_), channel_id=1, source_target_pairs={{0,8},{1,9},{2,10},{3,11},{4,12},{5,13},{6,14},{7,15},{8,0},{9,1},... | collective-permute-start | bytes 245768 | tf_op jit(solution)/shard_map/ppermute | solution.py:316
  4.9 7.4 %collective-permute-start.2 = (f32[80,128]{1,0:T(8,128)S(1)}, f32[80,128]{1,0:T(8,128)S(1)}, u32[]{:S(2)}, u32[]{:S(2)}) collective-permute-start(f32[80,128]{1,0:T(8,128)S(1)} %get-tuple-element.35), channel_id=1, source_target_pairs={{8,16},{9,17},{10,18},{11,19},{12,20},{13,21},{14,22},{15,23},{16,... | collective-permute-start | bytes 122888 | tf_op jit(solution)/shard_map/ppermute | solution.py:339
  7.3 6.2 %collective-permute-start = (f32[80,128]{1,0:T(8,128)S(1)}, f32[80,128]{1,0:T(8,128)S(1)}, u32[]{:S(2)}, u32[]{:S(2)}) collective-permute-start(f32[80,128]{1,0:T(8,128)S(1)} %get-tuple-element.36), channel_id=1, source_target_pairs={{0,16},{1,17},{2,18},{3,19},{4,20},{5,21},{6,22},{7,23},{16,32},{1... | collective-permute-start | bytes 122888 | tf_op jit(solution)/shard_map/ppermute | solution.py:338
  14.3 14.6 %collective-permute-start.4 = (f32[2,80,128]{2,1,0:T(8,128)S(1)}, f32[2,80,128]{2,1,0:T(8,128)S(1)}, u32[]{:S(2)}, u32[]{:S(2)}) collective-permute-start(f32[2,80,128]{2,1,0:T(8,128)S(1)} %shard_map.92.refs_0_), channel_id=1, source_target_pairs={{0,7},{1,6},{2,5},{3,4},{4,3},{5,2},{6,1},{7,0},{8,15},{9,14},{10,... | collective-permute-start | bytes 245768 | tf_op jit(solution)/shard_map/ppermute | solution.py:316
  20.2 11.1 %collective-permute-start.9 = (f32[2,80,128]{2,1,0:T(8,128)S(1)}, f32[2,80,128]{2,1,0:T(8,128)S(1)}, u32[]{:S(2)}, u32[]{:S(2)}) collective-permute-start(f32[2,80,128]{2,1,0:T(8,128)S(1)} %shard_map.92.refs_0_), channel_id=1, source_target_pairs={{0,3},{1,2},{2,1},{3,0},{4,7},{5,6},{6,5},{7,4},{8,11},{9,10},{10,... | collective-permute-start | bytes 245768 | tf_op jit(solution)/shard_map/ppermute | solution.py:316
  22.1 11.1 %collective-permute-start.8 = (f32[2,80,128]{2,1,0:T(8,128)S(1)}, f32[2,80,128]{2,1,0:T(8,128)S(1)}, u32[]{:S(2)}, u32[]{:S(2)}) collective-permute-start(f32[2,80,128]{2,1,0:T(8,128)S(1)} %shard_map.92.refs_0_), channel_id=1, source_target_pairs={{0,1},{1,0},{2,3},{3,2},{4,5},{5,4},{6,7},{7,6},{8,9},{9,8},{10,11... | collective-permute-start | bytes 245768 | tf_op jit(solution)/shard_map/ppermute | solution.py:316
  23.1 0.9 %copy-start.3 = (f32[256,256]{1,0:T(8,128)S(1)}, f32[256,256]{1,0:T(8,128)}, u32[]{:S(2)}) copy-start(f32[256,256]{1,0:T(8,128)} %refs_1_.2) | copy-start | bytes 786436
  24.1 0.9 %copy-start.4 = (f32[256,256]{1,0:T(8,128)S(1)}, f32[256,256]{1,0:T(8,128)}, u32[]{:S(2)}) copy-start(f32[256,256]{1,0:T(8,128)} %refs_2_.2) | copy-start | bytes 786436
  25.0 0.9 %copy-start.5 = (f32[256,256]{1,0:T(8,128)S(1)}, f32[256,256]{1,0:T(8,128)}, u32[]{:S(2)}) copy-start(f32[256,256]{1,0:T(8,128)} %refs_3_.1) | copy-start | bytes 786436
  26.0 0.9 %copy-start.6 = (f32[78,256]{1,0:T(8,128)S(1)}, f32[78,256]{1,0:T(8,128)}, u32[]{:S(2)}) copy-start(f32[78,256]{1,0:T(8,128)} %refs_0_.2) | copy-start | bytes 239620
  27.3 12.4 %collective-permute-start.3 = (f32[2,80,128]{2,1,0:T(8,128)S(1)}, f32[2,80,128]{2,1,0:T(8,128)S(1)}, u32[]{:S(2)}, u32[]{:S(2)}) collective-permute-start(f32[2,80,128]{2,1,0:T(8,128)S(1)} %shard_map.92.refs_0_), channel_id=1, source_target_pairs={{0,2},{1,3},{2,0},{3,1},{4,6},{5,7},{6,4},{7,5},{8,10},{9,11},{10,... | collective-permute-start | bytes 245768 | tf_op jit(solution)/shard_map/ppermute | solution.py:316
  28.8 10.9 %collective-permute-start.7 = (f32[2,80,128]{2,1,0:T(8,128)S(1)}, f32[2,80,128]{2,1,0:T(8,128)S(1)}, u32[]{:S(2)}, u32[]{:S(2)}) collective-permute-start(f32[2,80,128]{2,1,0:T(8,128)S(1)} %collective-permute-done.4.refs_3_), channel_id=1, source_target_pairs={{0,3},{1,2},{2,1},{3,0},{4,7},{5,6},{6,5},{7,4},{8,11},{9,10},{10,... | collective-permute-start | bytes 245768 | tf_op jit(solution)/shard_map/ppermute | solution.py:316
  30.7 9.0 %collective-permute-start.6 = (f32[2,80,128]{2,1,0:T(8,128)S(1)}, f32[2,80,128]{2,1,0:T(8,128)S(1)}, u32[]{:S(2)}, u32[]{:S(2)}) collective-permute-start(f32[2,80,128]{2,1,0:T(8,128)S(1)} %collective-permute-done.4.refs_3_), channel_id=1, source_target_pairs={{0,2},{1,3},{2,0},{3,1},{4,6},{5,7},{6,4},{7,5},{8,10},{9,11},{10,... | collective-permute-start | bytes 245768 | tf_op jit(solution)/shard_map/ppermute | solution.py:316
  31.3 8.4 %collective-permute-start.5 = (f32[2,80,128]{2,1,0:T(8,128)S(1)}, f32[2,80,128]{2,1,0:T(8,128)S(1)}, u32[]{:S(2)}, u32[]{:S(2)}) collective-permute-start(f32[2,80,128]{2,1,0:T(8,128)S(1)} %collective-permute-done.4.refs_3_), channel_id=1, source_target_pairs={{0,1},{1,0},{2,3},{3,2},{4,5},{5,4},{6,7},{7,6},{8,9},{9,8},{10,11... | collective-permute-start | bytes 245768 | tf_op jit(solution)/shard_map/ppermute | solution.py:316
  33.2 6.1 %copy-start = (f32[256,1024]{1,0:T(8,128)S(1)}, f32[256,1024]{1,0:T(8,128)}, u32[]{:S(2)}) copy-start(f32[256,1024]{1,0:T(8,128)} %refs_1_.3) | copy-start | bytes 3145732
  33.2 6.1 %copy-start.1 = (f32[1024,256]{1,0:T(8,128)S(1)}, f32[1024,256]{1,0:T(8,128)}, u32[]{:S(2)}) copy-start(f32[1024,256]{1,0:T(8,128)} %refs_2_.3) | copy-start | bytes 3145732
  33.2 6.1 %copy-start.2 = (f32[256,256]{1,0:T(8,128)S(1)}, f32[256,256]{1,0:T(8,128)}, u32[]{:S(2)}) copy-start(f32[256,256]{1,0:T(8,128)} %refs_0_.3) | copy-start | bytes 786436
  46.3 6.9 %collective-permute-start.10 = (f32[128,256]{1,0:T(8,128)S(1)}, f32[128,256]{1,0:T(8,128)S(1)}, u32[]{:S(2)}, u32[]{:S(2)}) collective-permute-start(f32[128,256]{1,0:T(8,128)S(1)} %get-tuple-element.32), channel_id=1, source_target_pairs={{0,8},{1,9},{2,10},{3,11},{4,12},{5,13},{6,14},{7,15},{8,0},{9,1},... | collective-permute-start | bytes 393224 | tf_op jit(solution)/shard_map/ppermute | solution.py:316
